TPU v7x, 32 devices: a whole 2x2x4 slice. The times are simulated.
32 devices in a mesh: fsdp: 8 (over y, x, core), tp: 4 (over z).
Axes of the slice: x: 2, y: 2, z: 4, core: 2. Of those that a mesh axis runs over, the one named last changes fastest.
Arguments:
- tokens: bfloat16 [16, 1024, 1024], P('fsdp', 'tp'), may hold values from -6 to 6
- lengths: int32 [16], replicated, may hold values from 1 to 1024, 10240 in all
- perm: int32 [16], replicated, may hold values from 0 to 15, as said below
- cotangent: bfloat16 [16, 1024, 1024], P('fsdp', 'tp'), may hold values from -6 to 6
- norm1_gain: float32 [1024], replicated, may hold values from 0.5 to 1.5
- input_weight: bfloat16 [1024, 8, 771], P('fsdp', 'tp'), may hold values from -0.1875 to 0.1875
- conv_w: float32 [8, 640, 4], replicated, may hold values from -3 to 3
- decay_log: float32 [8], replicated, may hold values from -7 to -2
- decay_bias: float32 [8], replicated, may hold values from -1 to 1
- out_gain: float32 [128], replicated, may hold values from 0.5 to 1.5
- w_out: bfloat16 [1024, 1024], P('tp', 'fsdp'), may hold values from -0.1875 to 0.1875
- norm2_gain: float32 [1024], replicated, may hold values from 0.5 to 1.5
- gate_up_weight: bfloat16 [1024, 2, 2816], P('fsdp', None, 'tp'), may hold values from -0.1875 to 0.1875
- down_weight: bfloat16 [2816, 1024], P('tp', 'fsdp'), may hold values from -0.109375 to 0.109375
Outputs:
- output: bfloat16 [16, 1024, 1024], P('fsdp', 'tp')
- input_grad: bfloat16 [16, 1024, 1024], P('fsdp', 'tp')
- grad_norm1_gain: float32 [1024], replicated
- grad_w_in: float32 [1024, 8, 771], P('fsdp', 'tp')
- grad_conv_w: float32 [8, 640, 4], replicated
- grad_decay_log: float32 [8], replicated
- grad_decay_bias: float32 [8], replicated
- grad_out_gain: float32 [128], replicated
- grad_w_out: float32 [1024, 1024], P('tp', 'fsdp')
- grad_norm2_gain: float32 [1024], replicated
- grad_w_gate_up: float32 [1024, 2, 2816], P('fsdp', None, 'tp')
- grad_w_down: float32 [2816, 1024], P('tp', 'fsdp')
Inputs may be any that keep to these rules, and one draw needn't show every extreme that they name: lengths[i] is the number of live tokens of sequence i; one sequence has exactly 1024. perm is a permutation; slot d belongs to index d // 2 of fsdp. The sequences of one index of fsdp (given order) go to 2 different indices, and each index receives at most one sequence from each index.
All inputs are finite; a program needn't handle non-finite values.
Results may differ from a plain program's by a relative error of at most 0.03.
Values may be sent and summed in bfloat16 or wider, within the bound.
No kernel may reach another device: no remote copies, remote signals or barrier semaphores. Data moves between devices by JAX's collectives and lax.ppermute only.
A program may use at most 320 MiB of HBM per device.

v0:
```python
import jax
import jax.numpy as jnp
from jax import lax
from jax.sharding import PartitionSpec as P

HEAD_DIM = 128
NH = 2
SPAN = 64


EPS_NORM = 1e-05
EPS_UNIT = 1e-06
PRECISION_MAX = lax.Precision.HIGHEST


def rms_scale(value, gain):
    return value * lax.rsqrt(jnp.mean(value * value, axis=-1, keepdims=True) + EPS_NORM) * gain


def unit_norm(value):
    return value * lax.rsqrt(jnp.sum(value * value, axis=-1, keepdims=True) + EPS_UNIT)


def causal_conv(raw_values, kernel):
    kernel_len = kernel.shape[-1]
    seq_len = raw_values.shape[1]
    padded = jnp.pad(raw_values, ((0, 0), (kernel_len - 1, 0), (0, 0), (0, 0)))
    summed = jnp.zeros_like(raw_values)
    for offset in range(kernel_len):
        summed = summed + padded[:, offset : offset + seq_len] * kernel[:, :, offset]
    return summed


def carry_step(state, pieces):
    weighted_block, value_block, key_block, decay_block = pieces
    updates = value_block - jnp.einsum("shid,shdv->shiv", key_block, state, precision=PRECISION_MAX)
    carried = decay_block * state + jnp.einsum(
        "shjd,shjv->shdv", weighted_block, updates, precision=PRECISION_MAX
    )
    return (carried, (state, updates))


def delta_product(queries, key_rows, values, beta_rows, log_decay):
    batch_seqs, seq_len, head_count, head_dim = queries.shape
    value_dim = values.shape[-1]
    blocks = seq_len // SPAN
    sub_decay = jnp.concatenate([log_decay[..., None], jnp.zeros_like(beta_rows[..., 1:])], axis=-1)

    def split_steps(value):
        tail_dims = value.shape[4:]
        shaped = value.reshape((batch_seqs, blocks, SPAN, head_count, NH) + tail_dims)
        axes_order = (1, 0, 3, 2, 4) + tuple(range(5, 5 + len(tail_dims)))
        return shaped.transpose(axes_order).reshape(
            (blocks, batch_seqs, head_count, SPAN * NH) + tail_dims
        )

    block_queries = queries.reshape(batch_seqs, blocks, SPAN, head_count, head_dim).transpose(
        1, 0, 3, 2, 4
    )
    block_keys = split_steps(key_rows)
    block_values = split_steps(values)
    block_betas = split_steps(beta_rows)
    cumulative = jnp.cumsum(split_steps(sub_decay), axis=-1)
    steps_in = SPAN * NH
    row_ids = lax.broadcasted_iota(jnp.int32, (steps_in, steps_in), 0)
    col_ids = lax.broadcasted_iota(jnp.int32, (steps_in, steps_in), 1)
    strictly = col_ids < row_ids
    key_inner = jnp.einsum("nshid,nshjd->nshij", block_keys, block_keys, precision=PRECISION_MAX)
    spread_log = cumulative[..., :, None] - cumulative[..., None, :]
    fading = jnp.where(strictly, jnp.exp(jnp.where(strictly, spread_log, 0.0)), 0.0)
    lower_mat = key_inner * fading * block_betas[..., :, None]
    right_sides = jnp.concatenate(
        [
            block_betas[..., None] * block_values,
            (block_betas * jnp.exp(cumulative))[..., None] * block_keys,
        ],
        axis=-1,
    )
    solved = jax.scipy.linalg.solve_triangular(
        lower_mat, right_sides, lower=True, unit_diagonal=True
    )
    value_part = solved[..., :value_dim]
    key_part = solved[..., value_dim:]
    last_log = cumulative[..., -1:]
    weighted = block_keys * jnp.exp(last_log - cumulative)[..., None]
    block_decay = jnp.exp(last_log)[..., None]
    first_state = jnp.zeros((batch_seqs, head_count, head_dim, value_dim), jnp.float32)
    last_state, (entering, updates) = lax.scan(
        carry_step, first_state, (weighted, value_part, key_part, block_decay)
    )
    read_log = cumulative[..., NH - 1 :: NH]
    out_rows = lax.broadcasted_iota(jnp.int32, (SPAN, steps_in), 0)
    out_cols = lax.broadcasted_iota(jnp.int32, (SPAN, steps_in), 1)
    visible = out_cols <= out_rows * NH + NH - 1
    query_key = jnp.einsum("nshid,nshjd->nshij", block_queries, block_keys, precision=PRECISION_MAX)
    read_spread = read_log[..., :, None] - cumulative[..., None, :]
    read_fade = jnp.where(visible, jnp.exp(jnp.where(visible, read_spread, 0.0)), 0.0)
    from_state = jnp.einsum("nshid,nshdv->nshiv", block_queries, entering, precision=PRECISION_MAX)
    outputs = jnp.exp(read_log)[..., None] * from_state + jnp.einsum(
        "nshij,nshjv->nshiv", query_key * read_fade, updates, precision=PRECISION_MAX
    )
    return outputs.transpose(1, 0, 3, 2, 4).reshape(batch_seqs, seq_len, head_count, value_dim)


def mixer_inner(projected_rows, conv_part, log_part, bias_part, out_gain):
    batch_seqs, seq_len, head_count, _ = projected_rows.shape
    conv_ch = conv_part.shape[1]
    conv_out = jax.nn.silu(causal_conv(projected_rows[..., :conv_ch], conv_part))
    queries = unit_norm(conv_out[..., :HEAD_DIM])
    key_rows = unit_norm(
        conv_out[..., HEAD_DIM : HEAD_DIM * (1 + NH)].reshape(
            batch_seqs, seq_len, head_count, NH, HEAD_DIM
        )
    )
    values = conv_out[..., HEAD_DIM * (1 + NH) :].reshape(
        batch_seqs, seq_len, head_count, NH, HEAD_DIM
    )
    out_gate = projected_rows[..., conv_ch : conv_ch + HEAD_DIM]
    beta_rows = jax.nn.sigmoid(projected_rows[..., conv_ch + HEAD_DIM : conv_ch + HEAD_DIM + NH])
    log_decay = -jnp.exp(log_part) * jax.nn.softplus(
        projected_rows[..., conv_ch + HEAD_DIM + NH] + bias_part
    )
    result = delta_product(queries, key_rows, values, beta_rows, log_decay)
    return rms_scale(result, out_gain) * jax.nn.silu(out_gate)


def swiglu(gate_up_result):
    return jax.nn.silu(gate_up_result[..., 0, :]) * gate_up_result[..., 1, :]


def spread(value):
    return lax.all_gather(value, "tp", axis=1, tiled=True)


def collect(value):
    return lax.psum_scatter(
        value.astype(jnp.bfloat16), "tp", scatter_dimension=1, tiled=True
    ).astype(jnp.float32)


def spread_back(value):
    return lax.all_gather(value, "tp", axis=1, tiled=True)


def collect_back(value):
    return lax.psum_scatter(
        value.astype(jnp.bfloat16), "tp", scatter_dimension=1, tiled=True
    ).astype(jnp.float32)


def local(
    tokens,
    lengths,
    perm,
    cotangent,
    norm1_gain,
    input_weight,
    conv_w,
    decay_log,
    decay_bias,
    out_gain,
    w_out,
    norm2_gain,
    gate_up_weight,
    down_weight,
):
    group_count = lax.axis_size("fsdp")
    own_group = lax.axis_index("fsdp")
    tensor_pos = lax.axis_index("tp")
    slot_count = tokens.shape[0]
    piece_len = tokens.shape[1]
    sources = perm.reshape(group_count, slot_count)
    local_ids = jnp.arange(slot_count, dtype=jnp.int32)
    group_ids = jnp.arange(group_count, dtype=jnp.int32)
    from_here = sources // slot_count == own_group
    matches = jnp.logical_and(
        from_here[:, :, None], (sources % slot_count)[:, :, None] == local_ids[None, None, :]
    )
    send_pick = jnp.sum(matches.astype(jnp.int32), axis=1).astype(jnp.bfloat16)
    sending = jnp.einsum(
        "gj,jtd->gtd", send_pick, tokens, preferred_element_type=jnp.float32
    ).astype(jnp.bfloat16)
    arrived = lax.all_to_all(sending, "fsdp", split_axis=0, concat_axis=0, tiled=True)
    my_sources = lax.dynamic_index_in_dim(sources, own_group, 0, keepdims=False)
    take_pick = ((my_sources // slot_count)[:, None] == group_ids[None, :]).astype(jnp.bfloat16)
    slot_tokens = jnp.einsum("sg,gtd->std", take_pick, arrived, preferred_element_type=jnp.float32)
    slot_len = jnp.take(lengths, my_sources)
    positions = tensor_pos * piece_len + jnp.arange(piece_len, dtype=jnp.int32)
    live_mask = (positions[None, :] < slot_len[:, None]).astype(jnp.float32)[..., None]
    head_count = input_weight.shape[1]
    head_start = tensor_pos * head_count
    conv_part = lax.dynamic_slice_in_dim(conv_w, head_start, head_count, 0)
    log_part = lax.dynamic_slice_in_dim(decay_log, head_start, head_count, 0)
    bias_part = lax.dynamic_slice_in_dim(decay_bias, head_start, head_count, 0)
    input_weight_whole, out_full = (
        lax.all_gather(input_weight, "fsdp", axis=0, tiled=True),
        lax.all_gather(w_out, "fsdp", axis=1, tiled=True),
    )
    model_dim = input_weight_whole.shape[0]
    output_matrix = out_full.reshape(head_count, HEAD_DIM, model_dim)
    normed_one = rms_scale(slot_tokens, norm1_gain).astype(jnp.bfloat16)
    gathered_first = spread(normed_one)
    projected_rows = jnp.einsum(
        "mzk,kin->mzin", gathered_first, input_weight_whole, preferred_element_type=jnp.float32
    )
    gated, inner_pull = jax.vjp(
        mixer_inner, projected_rows, conv_part, log_part, bias_part, out_gain
    )
    gated_reduced = gated.astype(jnp.bfloat16)
    mixer_result = jnp.einsum(
        "gtpo,poz->gtz", gated_reduced, output_matrix, preferred_element_type=jnp.float32
    )
    middle = slot_tokens + collect(mixer_result)
    gate_up_weight_whole, down_weight_whole = (
        lax.all_gather(gate_up_weight, "fsdp", axis=0, tiled=True),
        lax.all_gather(down_weight, "fsdp", axis=1, tiled=True),
    )
    normed_two = rms_scale(middle, norm2_gain).astype(jnp.bfloat16)
    gathered_second = spread(normed_two)
    gate_up_result = jnp.einsum(
        "tux,xeg->tueg", gathered_second, gate_up_weight_whole, preferred_element_type=jnp.float32
    )
    hidden_val, hidden_pull = jax.vjp(swiglu, gate_up_result)
    hidden_reduced = hidden_val.astype(jnp.bfloat16)
    forward_net_output = jnp.einsum(
        "wqh,hv->wqv", hidden_reduced, down_weight_whole, preferred_element_type=jnp.float32
    )
    block_out = live_mask * (middle + collect(forward_net_output))
    slot_cot = live_mask * cotangent.astype(jnp.float32)
    gradient_rows_second = spread_back(slot_cot.astype(jnp.bfloat16))
    grad_down = jnp.einsum(
        "kob,koi->bi", hidden_reduced, gradient_rows_second, preferred_element_type=jnp.float32
    )
    grad_hidden = jnp.einsum(
        "igx,bx->igb", gradient_rows_second, down_weight_whole, preferred_element_type=jnp.float32
    )
    gradient_couple = hidden_pull(grad_hidden)[0]
    grad_gate_up = jnp.einsum(
        "rzt,rzih->tih",
        gathered_second.astype(jnp.float32),
        gradient_couple,
        precision=PRECISION_MAX,
    )
    grad_normed_two = jnp.einsum(
        "uxmw,zmw->uxz",
        gradient_couple,
        gate_up_weight_whole.astype(jnp.float32),
        precision=PRECISION_MAX,
    )
    norm_pull_two = jax.vjp(rms_scale, middle, norm2_gain)[1]
    grad_mid_norm, grad_gain_two = norm_pull_two(collect_back(grad_normed_two))
    grad_middle = slot_cot + grad_mid_norm
    gradient_rows_first = spread_back(grad_middle.astype(jnp.bfloat16))
    grad_out = jnp.einsum(
        "irpy,irk->pyk", gated_reduced, gradient_rows_first, preferred_element_type=jnp.float32
    ).reshape(head_count * HEAD_DIM, model_dim)
    grad_gated = jnp.einsum(
        "ein,wcn->eiwc", gradient_rows_first, output_matrix, preferred_element_type=jnp.float32
    )
    gradient_projected, grad_conv, grad_log, grad_bias, grad_gain_out = inner_pull(grad_gated)
    grad_in = jnp.einsum(
        "bwg,bwfi->gfi",
        gathered_first.astype(jnp.float32),
        gradient_projected,
        precision=PRECISION_MAX,
    )
    grad_normed_one = jnp.einsum(
        "zqtv,btv->zqb",
        gradient_projected,
        input_weight_whole.astype(jnp.float32),
        precision=PRECISION_MAX,
    )
    norm_pull_one = jax.vjp(rms_scale, slot_tokens, norm1_gain)[1]
    grad_tok_norm, grad_gain_one = norm_pull_one(collect_back(grad_normed_one))
    input_slot = (grad_middle + grad_tok_norm).astype(jnp.bfloat16)
    grad_in, grad_out, grad_gate_up, grad_down = (
        lax.psum_scatter(
            grad_in.astype(jnp.bfloat16), "fsdp", scatter_dimension=0, tiled=True
        ).astype(jnp.float32),
        lax.psum_scatter(
            grad_out.astype(jnp.bfloat16), "fsdp", scatter_dimension=1, tiled=True
        ).astype(jnp.float32),
        lax.psum_scatter(
            grad_gate_up.astype(jnp.bfloat16), "fsdp", scatter_dimension=0, tiled=True
        ).astype(jnp.float32),
        lax.psum_scatter(
            grad_down.astype(jnp.bfloat16), "fsdp", scatter_dimension=1, tiled=True
        ).astype(jnp.float32),
    )
    conv_full = lax.dynamic_update_slice_in_dim(jnp.zeros_like(conv_w), grad_conv, head_start, 0)
    log_full = lax.dynamic_update_slice_in_dim(jnp.zeros_like(decay_log), grad_log, head_start, 0)
    bias_full = lax.dynamic_update_slice_in_dim(
        jnp.zeros_like(decay_bias), grad_bias, head_start, 0
    )
    small_sums = lax.psum(
        (grad_gain_one, grad_gain_two, conv_full, log_full, bias_full, grad_gain_out),
        ("fsdp", "tp"),
    )
    out_home = jnp.einsum(
        "sg,std->gtd", take_pick, block_out.astype(jnp.bfloat16), preferred_element_type=jnp.float32
    ).astype(jnp.bfloat16)
    grad_home = jnp.einsum(
        "sg,std->gtd", take_pick, input_slot, preferred_element_type=jnp.float32
    ).astype(jnp.bfloat16)
    back_out, back_grad = (
        lax.all_to_all(out_home, "fsdp", split_axis=0, concat_axis=0, tiled=True),
        lax.all_to_all(grad_home, "fsdp", split_axis=0, concat_axis=0, tiled=True),
    )
    output = jnp.einsum(
        "gj,gtd->jtd", send_pick, back_out, preferred_element_type=jnp.float32
    ).astype(jnp.bfloat16)
    input_grad = jnp.einsum(
        "gj,gtd->jtd", send_pick, back_grad, preferred_element_type=jnp.float32
    ).astype(jnp.bfloat16)
    return (
        output,
        input_grad,
        small_sums[0],
        grad_in,
        small_sums[2],
        small_sums[3],
        small_sums[4],
        small_sums[5],
        grad_out,
        small_sums[1],
        grad_gate_up,
        grad_down,
    )


def solution(mesh):
    return jax.shard_map(
        local,
        mesh=mesh,
        in_specs=(
            P("fsdp", "tp", None),
            P(),
            P(),
            P("fsdp", "tp", None),
            P(),
            P("fsdp", "tp", None),
            P(),
            P(),
            P(),
            P(),
            P("tp", "fsdp"),
            P(),
            P("fsdp", None, "tp"),
            P("tp", "fsdp"),
        ),
        out_specs=(
            P("fsdp", "tp", None),
            P("fsdp", "tp", None),
            P(),
            P("fsdp", "tp", None),
            P(),
            P(),
            P(),
            P(),
            P("tp", "fsdp"),
            P(),
            P("fsdp", None, "tp"),
            P("tp", "fsdp"),
        ),
        check_vma=False,
    )
```

profile of v0, /device:TPU:0, one launch (start us, length us, event | category | flops | bytes accessed | tf_op | source)
XLA Modules:
  0.0 2861.9 jit_solution(13583249474675545995)
XLA Ops:
  23.3 58.9 %all-to-all-done = bf16[8,256,1024]{2,1,0:T(8,128)(2,1)} async-done(((bf16[8,256,1024]{2,1,0:T(8,128)(2,1)}), bf16[8,256,1024]{2,1,0:T(8,128)(2,1)}, u32[]{:S(2)}, u32[]{:S(2)}) %all-to-all-start) | async-done | bytes 4194336 | tf_op jit(solution)/shard_map/all_to_all | solution.py:183
  101.2 68.5 %all-gather.8.cloned.1.call-done = bf16[2,1024,1024]{2,0,1:T(2,128)(2,1)} async-done(((bf16[2,256,1024]{2,0,1:T(2,128)(2,1)}), bf16[2,1024,1024]{2,0,1:T(2,128)(2,1)}) %all-gather.8.cloned.1.call-update) | async-done | bytes 4194320 | tf_op jit(solution)/shard_map/all_gather | solution.py:132
  169.8 12.8 fusion.63
  267.3 630.3 %custom-call.10 = f32[16,2,2,1,128,128]{4,5,3,2,1,0:T(8,128)} custom-call(f32[16,2,2,1,128,128]{5,4,3,2,1,0:T(8,128)} %get-tuple-element.727), custom_call_target="InvertDiagBlocksLowerTriangular" | custom-call | tf_op jit(solution)/shard_map/jvp(jit(_solve_triangular))/vmap(vmap(vmap()))/triangular_solve | solution.py:79
  929.2 81.9 %while.38 = (s32[]{:T(128)}, f32[2,2,128,128]{3,2,1,0:T(8,128)S(1)}, f32[16,2,2,128,128]{4,3,2,1,0:T(8,128)}, f32[16,2,2,128,128]{4,3,2,1,0:T(8,128)}, f32[16,2,...) while((s32[]{:T(128)}, ...), condition=%wide.region_6.7_spmd.clone, body=%wide.region_5.6_spmd.clone.sunk | while | flops 201719808 | bytes 2885797 | solution.py:88
  1063.5 151.8 %all-reduce.36.cloned.1.call-done = bf16[2,1024,1024]{2,0,1:T(2,128)(2,1)} async-done(((bf16[2,1024,1024]{2,0,1:T(2,128)(2,1)}), bf16[2,1024,1024]{2,0,1:T(2,128)(2,1)}) %all-reduce.36.cloned.1.call-update) | async-done | bytes 4194320
  1226.4 21.5 all-gather.14.cloned.1.call-done
  1247.9 82.9 %all-gather.12.cloned.1.call-done = bf16[2,1024,1024]{2,0,1:T(2,128)(2,1)} async-done(((bf16[2,256,1024]{2,0,1:T(2,128)(2,1)}), bf16[2,1024,1024]{2,0,1:T(2,128)(2,1)}) %all-gather.12.cloned.1.call-update) | async-done | bytes 4194320 | tf_op jit(solution)/shard_map/all_gather | solution.py:132
  1330.8 12.1 fusion.57
  1342.9 13.6 all-gather.16.cloned.1.call-done
  1356.5 83.0 %all-gather.18.cloned.1.call-done = bf16[2,1024,1024]{2,0,1:T(2,128)(2,1)} async-done(((bf16[2,256,1024]{2,0,1:T(2,128)(2,1)}), bf16[2,1024,1024]{2,0,1:T(2,128)(2,1)}) %all-gather.18.cloned.1.call-update) | async-done | bytes 4194320 | tf_op jit(solution)/shard_map/all_gather | solution.py:142
  1455.2 22.6 bitcast_convert_fusion.1
  1486.4 153.6 %all-reduce.38.cloned.1.call-done = bf16[2,1024,1024]{2,0,1:T(2,128)(2,1)} async-done(((bf16[2,1024,1024]{2,0,1:T(2,128)(2,1)}), bf16[2,1024,1024]{2,0,1:T(2,128)(2,1)}) %all-reduce.38.cloned.1.call-update) | async-done | bytes 4194320
  1677.8 58.0 %all-gather.20.cloned.1.call-done = bf16[2,1024,1024]{2,0,1:T(2,128)(2,1)} async-done(((bf16[2,256,1024]{2,0,1:T(2,128)(2,1)}), bf16[2,1024,1024]{2,0,1:T(2,128)(2,1)}) %all-gather.20.cloned.1.call-update) | async-done | bytes 4194320 | tf_op jit(solution)/shard_map/all_gather | solution.py:142
  1790.3 164.5 %while.39 = (s32[]{:T(128)}, f32[2,2,128,128]{3,2,1,0:T(8,128)S(1)}, f32[16,2,2,128,128]{4,3,2,1,0:T(8,128)}, f32[16,2,2,128,128]{4,3,2,1,0:T(8,128)}, f32[16,2,...) while((s32[]{:T(128)}, ...), condition=%wide.region_19.20_spmd.clone, body=%wide.region_17.19_spmd.clone.sunk | while | flops 403439616 | bytes 4726519 | solution.py:88
  1954.9 16.3 fusion.48
  1971.2 12.5 fusion.49
  1983.7 19.7 multiply_reduce_fusion.6
  2003.3 13.9 fusion.94
  2026.1 11.9 add_add_fusion.1
  2124.2 23.4 multiply_reduce_fusion.2
  2147.6 14.4 broadcast_multiply_fusion
  2162.1 16.2 pad_add_fusion.2
  2182.1 26.0 bitcast_convert_fusion
  2222.3 25.0 bitcast_convert_fusion.4
  2252.2 252.4 %all-reduce.40.cloned.1.call-done = (bf16[2,1024,1024]{2,0,1:T(2,128)(2,1)}, bf16[2,1024,1024]{2,0,1:T(2,128)(2,1)}) async-done(((bf16[2,1024,1024]{2,0,1:T(2,128)(2,1)}, bf16[2,1024,1024]{2,0,1:T(2,128)(2,1)}), (bf16[2,1024,1024]{2,0,1:T(2,128)(2,1)}, bf16[2,1024,1024]{2,0,1:T(2,128)(2,1)})) %all-reduce.40.cloned.1.call-update) | async-done | bytes 8388624
  2527.9 30.3 %bitcast_convert_fusion.3 = bf16[1024,2,771]{0,2,1:T(8,128)(2,1)} fusion(f32[2,1024,2,640]{1,3,2,0:T(8,128)} %copy-done.27, f32[2,1024,2,128]{1,3,2,0:T(8,128)} %get-tuple-element.701, f32[2,1024,2,2]{1,3,2,0:T(2,128)S(1)} %fusion.193, f32[2,1024,2,1]{1,3,2,0:T(1,128)S(1)} %get-tuple-element.703, bf16[2,1024,1024]{2,0,1:T(2,128)(2,1)} %all-gather.8.cloned.1.call-done), kind=kOutput, calls=%fused_computation.85 | convolution fusion | flops 38816751616 | bytes 19984384 | tf_op jit(solution)/shard_map/bwg,bwfi->gfi/dot_general | solution.py:261
  2584.9 54.2 %reduce-scatter.17.cloned.1.call-done = bf16[128,1408]{1,0:T(8,128)(2,1)} async-done(((bf16[1024,1408]{1,0:T(8,128)(2,1)}), bf16[128,1408]{1,0:T(8,128)(2,1)}) %reduce-scatter.17.cloned.1.call-update) | async-done | bytes 360464
  2642.8 33.5 %reduce-scatter.15.cloned.1.call-done = bf16[128,256]{1,0:T(8,128)(2,1)} async-done(((bf16[1024,256]{1,0:T(8,128)(2,1)}), bf16[128,256]{1,0:T(8,128)(2,1)}) %reduce-scatter.15.cloned.1.call-update) | async-done | bytes 65552
  2677.9 49.2 %reduce-scatter.13.cloned.1.call-done = bf16[128,1542]{1,0:T(8,128)(2,1)} async-done(((bf16[1024,1542]{1,0:T(8,128)(2,1)}), bf16[128,1542]{1,0:T(8,128)(2,1)}) %reduce-scatter.13.cloned.1.call-update) | async-done | bytes 394768
  2730.4 39.5 %all-reduce.27 = (f32[1024]{0:T(1024)}, f32[8]{0:T(128)}, f32[8]{0:T(128)}, f32[128]{0:T(128)}, f32[1024]{0:T(1024)}) all-reduce(f32[1024]{0:T(1024)S(1)} %get-tuple-element.632, f32[8]{0:T(128)S(1)} %multiply_dynamic-update-slice_fusion, f32[8]{0:T(128)S(1)} %dynamic_update_slice.55, ...), channel_id=1, replica_groups=mesh['fsdp'=8,'tp'=4] {'fsdp','tp'}, use_global_device_ids=true, to_apply=%region_33.34 | all-reduce | flops 2192 | bytes 17536 | tf_op jit(solution)/shard_map/psum | solution.py:295
  2782.5 71.1 %all-reduce.34.cloned.1.call-done = f32[8,640,4]{1,2,0:T(4,128)} async-done(((f32[8,640,4]{1,2,0:T(4,128)}), f32[8,640,4]{1,2,0:T(4,128)}) %all-reduce.34.cloned.1.call-update) | async-done | bytes 81936 | tf_op jit(solution)/shard_map/psum | solution.py:295
  (633 shorter events, 765.4 us)
Async XLA Ops:
  7.2 94.0 %all-gather.10.cloned.1.call-start = ((), (), s32[]{:S(2)}) async-start(), calls=%async_computation.8 | async-start | bytes 3575808 | tf_op jit(solution)/shard_map/all_gather | solution.py:196
  16.7 65.4 %all-to-all-start = ((bf16[8,256,1024]{2,1,0:T(8,128)(2,1)}), bf16[8,256,1024]{2,1,0:T(8,128)(2,1)}, u32[]{:S(2)}, u32[]{:S(2)}) async-start(bf16[8,256,1024]{2,1,0:T(8,128)(2,1)} %copy.605), calls=%async_computation | async-start | bytes 8388608 | tf_op jit(solution)/shard_map/all_to_all | solution.py:183
  22.0 147.7 %all-gather.8.cloned.1.call-start = ((), (), s32[]{:S(2)}) async-start(), calls=%async_computation.7 | async-start | bytes 5242880 | tf_op jit(solution)/shard_map/all_gather | solution.py:132
  89.6 1125.7 %all-reduce.36.cloned.1.call-start = ((), (), s32[]{:S(2)}) async-start(), calls=%async_computation.19 | async-start | bytes 8388608
  101.2 158.1 %copy-start.58 = (pred[128,128]{1,0:T(8,128)(4,1)}, pred[128,128]{1,0:T(8,128)(4,1)S(1)}, u32[]{:S(2)}) copy-start(pred[128,128]{1,0:T(8,128)(4,1)S(1)} %get-tuple-element.744) | copy-start | bytes 49156
  210.0 713.6 %copy-start.81 = (f32[16,2,2,1]{0,2,3,1:T(2,128)}, f32[16,2,2,1]{0,2,3,1:T(2,128)S(1)}, u32[]{:S(2)}) copy-start(f32[16,2,2,1]{0,2,3,1:T(2,128)S(1)} %copy.768) | copy-start | bytes 772
  211.8 799.3 %copy-start.54 = (f32[2,1024,2]{1,2,0:T(2,128)}, f32[2,1024,2]{1,2,0:T(2,128)S(1)}, u32[]{:S(2)}) copy-start(f32[2,1024,2]{1,2,0:T(2,128)S(1)} %multiply_reduce_fusion.14) | copy-start | bytes 49156
  212.7 820.7 %copy-start.39 = (f32[16,2,2,64]{0,2,3,1:T(2,128)}, f32[16,2,2,64]{0,2,3,1:T(2,128)S(1)}, u32[]{:S(2)}) copy-start(f32[16,2,2,64]{0,2,3,1:T(2,128)S(1)} %copy.614) | copy-start | bytes 49156
  259.2 638.7 %copy-start.28 = (f32[2,16,64,2,2]{1,4,2,3,0:T(2,128)}, f32[2,16,64,2,2]{1,4,2,3,0:T(2,128)S(1)}, u32[]{:S(2)}) copy-start(f32[2,16,64,2,2]{1,4,2,3,0:T(2,128)S(1)} %copy.626) | copy-start | bytes 98308
  1061.6 186.3 %all-gather.14.cloned.1.call-start = ((), (), s32[]{:S(2)}) async-start(), calls=%async_computation.10 | async-start | bytes 3244032 | tf_op jit(solution)/shard_map/all_gather | solution.py:215
  1062.2 268.5 %all-gather.12.cloned.1.call-start = ((), (), s32[]{:S(2)}) async-start(), calls=%async_computation.9 | async-start | bytes 5242880 | tf_op jit(solution)/shard_map/all_gather | solution.py:132
  1063.5 160.1 %copy-start.30 = (bf16[2,256,1024]{2,1,0:T(8,128)(2,1)S(1)}, bf16[2,256,1024]{2,1,0:T(8,128)(2,1)}, u32[]{:S(2)}) copy-start(bf16[2,256,1024]{2,1,0:T(8,128)(2,1)} %param.21) | copy-start | bytes 3145732
  1218.6 430.2 %copy-start.9 = (f32[2,256,1024]{2,0,1:T(2,128)}, f32[2,256,1024]{2,0,1:T(2,128)S(1)}, u32[]{:S(2)}) copy-start(f32[2,256,1024]{2,0,1:T(2,128)S(1)} %get-tuple-element.692) | copy-start | bytes 6291460
  1220.8 135.7 %all-gather.16.cloned.1.call-start = ((), (), s32[]{:S(2)}) async-start(), calls=%async_computation.11 | async-start | bytes 1622016 | tf_op jit(solution)/shard_map/all_gather | solution.py:216
  1221.4 218.1 %all-gather.18.cloned.1.call-start = ((), (), s32[]{:S(2)}) async-start(), calls=%async_computation.12 | async-start | bytes 5242880 | tf_op jit(solution)/shard_map/all_gather | solution.py:142
  1223.6 425.3 %copy-start.35 = (f32[2,256]{0,1:T(8,128)}, f32[2,256]{0,1:T(8,128)S(1)}, u32[]{:S(2)}) copy-start(f32[2,256]{0,1:T(8,128)S(1)} %copy.603) | copy-start | bytes 6148
  1226.3 413.6 %all-reduce.38.cloned.1.call-start = ((), (), s32[]{:S(2)}) async-start(), calls=%async_computation.20 | async-start | bytes 8388608
  1486.3 249.5 %all-gather.20.cloned.1.call-start = ((), (), s32[]{:S(2)}) async-start(), calls=%async_computation.13 | async-start | bytes 5242880 | tf_op jit(solution)/shard_map/all_gather | solution.py:142
  1655.9 848.7 %all-reduce.40.cloned.1.call-start = ((), (), s32[]{:S(2)}) async-start(), calls=%async_computation.21 | async-start | bytes 16777216
  2214.4 368.6 %reduce-scatter.19.cloned.1.call-start = ((), (), s32[]{:S(2)}) async-start(), calls=%async_computation.18 | async-start | bytes 1769472
  2222.3 416.8 %reduce-scatter.17.cloned.1.call-start = ((), (), s32[]{:S(2)}) async-start(), calls=%async_computation.17 | async-start | bytes 3244032
  2247.4 257.2 %copy-start.21 = (f32[2,256,1024]{2,0,1:T(2,128)S(1)}, f32[2,256,1024]{2,0,1:T(2,128)}, u32[]{:S(2)}) copy-start(f32[2,256,1024]{2,0,1:T(2,128)} %copy-done.20) | copy-start | bytes 6291460
  2247.4 257.2 %copy-start.38 = (f32[2,256]{0,1:T(8,128)S(1)}, f32[2,256]{0,1:T(8,128)}, u32[]{:S(2)}) copy-start(f32[2,256]{0,1:T(8,128)} %copy-done.37) | copy-start | bytes 6148
  2247.4 257.2 %copy-start.84 = (f32[1024]{0:T(1024)S(1)}, f32[1024]{0:T(1024)}, u32[]{:S(2)}) copy-start(f32[1024]{0:T(1024)} %param.22) | copy-start | bytes 12292
  2252.2 256.5 %copy-start.80 = (f32[2,256]{1,0:T(2,128)S(1)}, f32[2,256]{1,0:T(2,128)}, u32[]{:S(2)}) copy-start(f32[2,256]{1,0:T(2,128)} %copy-done.79) | copy-start | bytes 6148
  2252.2 256.7 %copy-start.93 = (s32[2]{0:T(128)S(1)}, s32[2]{0:T(128)}, u32[]{:S(2)}) copy-start(s32[2]{0:T(128)} %copy-done.92) | copy-start | bytes 28
  2518.1 60.2 %all-to-all-start.2 = ((bf16[8,256,1024]{2,1,0:T(8,128)(2,1)}), bf16[8,256,1024]{2,1,0:T(8,128)(2,1)}, u32[]{:S(2)}, u32[]{:S(2)}) async-start(bf16[8,256,1024]{2,1,0:T(8,128)(2,1)} %copy.709), calls=%async_computation.2 | async-start | bytes 8388608 | tf_op jit(solution)/shard_map/all_to_all | solution.py:307
  2522.8 153.4 %reduce-scatter.15.cloned.1.call-start = ((), (), s32[]{:S(2)}) async-start(), calls=%async_computation.16 | async-start | bytes 589824
  2527.7 199.4 %reduce-scatter.13.cloned.1.call-start = ((), (), s32[]{:S(2)}) async-start(), calls=%async_computation.15 | async-start | bytes 3833856
  2578.3 196.7 %all-to-all-start.1 = ((bf16[8,256,1024]{2,1,0:T(8,128)(2,1)}), bf16[8,256,1024]{2,1,0:T(8,128)(2,1)}, u32[]{:S(2)}, u32[]{:S(2)}) async-start(bf16[8,256,1024]{2,1,0:T(8,128)(2,1)} %copy.650), calls=%async_computation.1 | async-start | bytes 8388608 | tf_op jit(solution)/shard_map/all_to_all | solution.py:306
  2582.9 187.0 %copy-start.87 = (s32[8,2]{0,1:T(2,128)S(1)}, s32[8,2]{0,1:T(2,128)}, u32[]{:S(2)}) copy-start(s32[8,2]{0,1:T(2,128)} %copy-done.86) | copy-start | bytes 196
  2582.9 270.7 %all-reduce.34.cloned.1.call-start = ((), (), s32[]{:S(2)}) async-start(), calls=%async_computation.14 | async-start | bytes 163840 | tf_op jit(solution)/shard_map/psum | solution.py:295
  (92 other events, 2373.5 us)
Sparse Core Ops, SparseCore 0:
  10.5 59.9 all-gather.9
  89.7 80.0 all-gather.7
  1061.8 153.4 all-reduce.35
  1217.2 30.6 all-gather.13
  1250.0 80.7 all-gather.11
  1332.7 23.8 all-gather.15
  1358.7 80.7 all-gather.17
  1486.4 153.4 all-reduce.37
  1656.0 79.7 all-gather.19
  2214.5 290.0 all-reduce.39
  2507.9 51.0 reduce-scatter.18
  2562.2 76.7 reduce-scatter.16
  2643.0 33.2 reduce-scatter.14
  2679.6 47.4 reduce-scatter.12
  2734.1 119.4 all-reduce.33
where the time goes:
time: 2880 us; the launch traced here: 2860 us
  waiting for transfers between devices  1160 us (40%)
  other arithmetic  816 us (28%)
  matrix products  569 us (20%)
  local copies, waits for them, and re-layouts  238 us (8%)
  blocking collectives  49.7 us (2%)
    unnamed x22, waiting for transfers between devices  696 us
    another operation x4, other arithmetic, delta_product(): jax.scipy.linalg.solve_triangular(lower_mat, right_sides, lower=True, uni...  638 us
    all_gather x2, waiting for transfers between devices, spread(): return lax.all_gather(value, 'tp', axis=1, tiled=True)  151 us
    all_gather x2, waiting for transfers between devices, spread_back(): return lax.all_gather(value, 'tp', axis=1, tiled=True)  141 us
    dot_general x48, matrix products, carry_step(): jnp.einsum('shid,shdv->shiv', key_block, state, precision=PRECISION_MAX)  98.7 us
    dot_general x48, matrix products, carry_step(): jnp.einsum('shjd,shjv->shdv', weighted_block, updates, precision=PRECISIO...  96.4 us
    psum x1, waiting for transfers between devices, local(): lax.psum((grad_gain_one, grad_gain_two, conv_full, log_full, bias_full, g...  71.1 us
    all_to_all x1, waiting for transfers between devices, local(): lax.all_to_all(sending, 'fsdp', split_axis=0, concat_axis=0, tiled=True)  58.9 us
  transfers between devices with their start and end apart: 18, of which 15 were waited for; matrix products, arithmetic and copies ran while one was open for 7% of the time, Pallas kernels for 0%

commit v1 on v0

v1 whole, which is shorter than its diff:
```python
import functools

import jax
import jax.numpy as jnp
from jax import lax
from jax.experimental import pallas as pl
from jax.experimental.pallas import tpu as pltpu
from jax.sharding import PartitionSpec as P

HD = 128
NH = 2
SPAN = 64
SUB = SPAN * NH
TAPS = 4
SMALL = 16
UNITS = 6 * HD + SMALL
EPS_NORM = 1e-05
EPS_UNIT = 1e-06
F32 = jnp.float32
BF16 = jnp.bfloat16
FAR = -1e30
VMEM_BYTES = 56 * 1024 * 1024
EXACT = lax.Precision.HIGHEST


def params(**kw):
    return pltpu.CompilerParams(vmem_limit_bytes=VMEM_BYTES, **kw)


def cost(flops, nbytes, trans=0):
    return pl.CostEstimate(flops=int(flops), bytes_accessed=int(nbytes), transcendentals=int(trans))


def nn(a, b):
    return lax.dot_general(a, b, (((1,), (0,)), ((), ())), preferred_element_type=F32)


def nt(a, b):
    return lax.dot_general(a, b, (((1,), (1,)), ((), ())), preferred_element_type=F32)


def tn(a, b):
    return lax.dot_general(a, b, (((0,), (0,)), ((), ())), preferred_element_type=F32)


def exact_nn(a, b):
    return lax.dot_general(a, b, (((1,), (0,)), ((), ())), precision=EXACT, preferred_element_type=F32)


def sigmoid(v):
    return 1.0 / (1.0 + jnp.exp(-v))


def sides(pieces, bit):
    return [p for p in range(pieces) if not p & bit], [p for p in range(pieces) if p & bit]


def stacks(pieces, shape):
    return [jax.ShapeDtypeStruct((pieces // 2,) + shape, BF16)] * 2


def add_kernel(count, *refs):
    ins, outs = refs[: 2 * count], refs[2 * count :]
    for i in range(count):
        for j in range(2):
            outs[2 * i + j][...] = (ins[2 * i][j].astype(F32) + ins[2 * i + 1][j].astype(F32)).astype(BF16)


def add_stacks(pairs):
    flat = [v for pair in pairs for v in pair]
    steps = 3
    blocks = [pl.BlockSpec((2, v.shape[1] // steps, v.shape[2]), lambda i: (0, i, 0)) for v in flat]
    single = [pl.BlockSpec((v.shape[1] // steps, v.shape[2]), lambda i: (i, 0)) for v in flat]
    res = pl.pallas_call(
        functools.partial(add_kernel, len(pairs)),
        out_shape=[jax.ShapeDtypeStruct(v.shape[1:], BF16) for v in flat],
        grid=(steps,),
        in_specs=blocks,
        out_specs=single,
        compiler_params=params(),
        cost_estimate=cost(1e6, 1e6),
        name="add_stacks",
    )(*flat)
    return [res[2 * i : 2 * i + 2] for i in range(len(pairs))]


def lane_sum(value):
    return jnp.sum(value, axis=-1, keepdims=True)


def conv_shifts(ref, start, rows, lanes):
    window = ref[start : start + rows + 8, lanes]
    views = [pltpu.roll(window, TAPS - 1 - j, 0)[8 : 8 + rows] for j in range(TAPS - 1)]
    return views + [window[8 : 8 + rows]]


def conv_shifts_back(ref, start, rows, lanes):
    window = ref[start : start + rows + 8, lanes]
    views = [pltpu.roll(window, rows + 8 - (TAPS - 1 - j), 0)[:rows] for j in range(TAPS - 1)]
    return views + [window[:rows]]


def iota(shape, dim):
    return lax.broadcasted_iota(jnp.int32, shape, dim)


def project_kernel(pieces, h, scal_ref, a_ref, cw_ref, *refs):
    parts = refs[:pieces]
    raw_ref, gate_ref, q_ref, k_ref, v_ref, rows_ref, raw_s, mix_s, aux_s = refs[pieces:]
    tile = a_ref.shape[0]
    depth = parts[0].shape[1]
    head = 8

    @pl.when(pl.program_id(0) == 0)
    def _():
        raw_s[0:head, :] = jnp.zeros_like(raw_s[0:head, :])

    @pl.when(pl.program_id(0) > 0)
    def _():
        raw_s[0:head, :] = raw_s[tile : tile + head, :]

    acc = jnp.zeros((tile, UNITS), F32)
    for p in range(pieces):
        acc += nt(a_ref[:, p * depth : (p + 1) * depth], parts[p][HD:])
    raw_s[head : tile + head, :] = acc[:, : 5 * HD]
    raw_ref[...] = acc[:, : 5 * HD].astype(BF16)
    gate_ref[...] = acc[:, 5 * HD : 6 * HD].astype(BF16)

    small = acc[:, 6 * HD :]
    rate, bias = scal_ref[h, 0], scal_ref[h, 1]
    arg = small[:, 2:3] + bias
    soft = jnp.maximum(arg, 0.0) + jnp.log(1.0 + jnp.exp(-jnp.abs(arg)))
    beta = sigmoid(small[:, 0:2])
    lane = iota((tile, HD), 1)
    aux_s[pl.ds(0, tile, 2), :] = jnp.where(
        lane == 0, beta[:, 0:1], jnp.where(lane == 1, -rate * soft, jnp.where(lane == 2, arg, 0.0))
    )
    aux_s[pl.ds(1, tile, 2), :] = jnp.where(lane == 0, beta[:, 1:2], 0.0)
    upper = jnp.where(iota((SUB, SUB), 0) <= iota((SUB, SUB), 1), 1.0, 0.0)
    for b in range(tile // SPAN):
        rows = jnp.transpose(aux_s[b * SUB : (b + 1) * SUB, :])[:8]
        cum = exact_nn(rows, upper)
        rows_ref[b] = jnp.where(iota((8, SUB), 0) == 3, cum[1:2], rows)

    chunk = 64
    for g in range(5):
        taps = cw_ref[0, :, g * HD : (g + 1) * HD]
        for i in range(tile // chunk):
            start = i * chunk
            views = conv_shifts(raw_s, start, chunk, slice(g * HD, (g + 1) * HD))
            pre = views[0] * taps[0:1]
            for j in range(1, TAPS):
                pre += views[j] * taps[j : j + 1]
            act = pre * sigmoid(pre)
            if g < 3:
                act = act * lax.rsqrt(lane_sum(act * act) + EPS_UNIT)
            if g == 0:
                q_ref[start : start + chunk, :] = act.astype(BF16)
            else:
                mix_s[pl.ds(2 * start + (g + 1) % 2, chunk, 2), :] = act
        if g in (2, 4):
            (k_ref if g == 2 else v_ref)[...] = mix_s[...].astype(BF16)


def project(h, normed, parts, conv_t, scal):
    seq, dim = normed.shape
    pieces = len(parts)
    tile = min(256, seq)
    fix = lambda i: (0, 0)
    along = lambda i: (i, 0)
    outs = [((seq, 5 * HD), BF16, 1), ((seq, HD), BF16, 1), ((seq, HD), BF16, 1), ((NH * seq, HD), BF16, NH), ((NH * seq, HD), BF16, NH)]
    return pl.pallas_call(
        functools.partial(project_kernel, pieces, h),
        out_shape=[jax.ShapeDtypeStruct(s, d) for s, d, _ in outs] + [jax.ShapeDtypeStruct((seq // SPAN, 8, SUB), F32)],
        grid=(seq // tile,),
        in_specs=[
            pl.BlockSpec(memory_space=pltpu.SMEM),
            pl.BlockSpec((tile, dim), along),
            pl.BlockSpec((1,) + conv_t.shape[1:], lambda i: (h, 0, 0)),
        ]
        + [pl.BlockSpec(w.shape, fix) for w in parts],
        out_specs=[pl.BlockSpec((tile * n, s[1]), along) for s, _, n in outs]
        + [pl.BlockSpec((tile // SPAN, 8, SUB), lambda i: (i, 0, 0))],
        scratch_shapes=[
            pltpu.VMEM((tile + 8, 5 * HD), F32),
            pltpu.VMEM((NH * tile, HD), F32),
            pltpu.VMEM((NH * tile, HD), F32),
        ],
        compiler_params=params(),
        cost_estimate=cost(2 * seq * dim * UNITS, 8e6),
        name="project",
    )(scal, normed, conv_t, *parts)


BASE = 16


def unit_lower_inverses(lowers):
    n, groups = SUB, SUB // BASE
    lane = iota((BASE, n), 1)
    group = lane // BASE
    packed = []
    for low in lowers:
        p = jnp.where(group == 0, low[:BASE], 0.0)
        for b in range(1, groups):
            p = jnp.where(group == b, low[b * BASE : (b + 1) * BASE], p)
        packed.append(p)
    eye = jnp.where(lane % BASE == iota((BASE, n), 0), 1.0, 0.0)
    invs = [eye] * len(lowers)
    first = group * BASE
    for j in range(BASE - 1):
        coefs = [jnp.take_along_axis(p, first + j, axis=1) for p in packed]
        invs = [x - c * x[j : j + 1] for x, c in zip(invs, coefs)]
    fulls = [
        jnp.concatenate([jnp.where(group == b, x, 0.0).astype(BF16) for b in range(groups)], axis=0) for x in invs
    ]
    row, col = iota((n, n), 0), iota((n, n), 1)
    size = BASE
    while size < n:
        odd = range(1, n // size, 2)
        mask = jnp.logical_and(row // size == col // size + 1, row // (2 * size) == col // (2 * size))
        crosses = [jnp.where(mask, low, 0.0).astype(BF16) for low in lowers]
        picks = [jnp.concatenate([f[b * size : (b + 1) * size] for b in odd], axis=0) for f in fulls]
        halves = [nn(p, c).astype(BF16) for p, c in zip(picks, crosses)]
        belows = [(p.astype(F32) - nn(h, f)).astype(BF16) for p, h, f in zip(picks, halves, fulls)]
        fulls = [
            jnp.concatenate(
                [
                    below[(b // 2) * size : (b // 2 + 1) * size] if b % 2 else f[b * size : (b + 1) * size]
                    for b in range(n // size)
                ],
                axis=0,
            )
            for f, below in zip(fulls, belows)
        ]
        size *= 2
    return fulls


def turned(value, eye):
    return nt(eye, value)


def decay_terms(rows_ref, cums, items):
    out = []
    pick_row = iota((8, SUB), 0)
    for i, (b, h) in enumerate(items):
        rows = rows_ref[h][b]
        g = rows[3:4, :]
        g_last = g[:, SUB - 1 :]
        e = jnp.exp(g)
        wide = jnp.where(pick_row == 1, e, jnp.where(pick_row == 2, jnp.exp(g_last - g), rows))
        wide = jnp.where(pick_row == 4, rows[0:1, :] * e, wide)
        cols = jnp.transpose(jnp.concatenate([wide] * (SUB // 8), axis=0))
        cums[i] = cols
        c_col = cums[i, pl.ds(1, SPAN, 2), :][:, 3:4]
        out.append((cols[:, 0:1], cols[:, 1:2], cols[:, 2:3], cols[:, 3:4], cols[:, 4:5], g, c_col, g_last))
    return out


PER_STEP = 2


def recur_kernel(heads, more, gain_ref, start_ref, *refs):
    q_r, k_r, v_r, g_r, rows_r = (refs[i * heads : (i + 1) * heads] for i in range(5))
    refs = refs[: 5 * heads] + refs[5 * heads + more :]
    z_ref, end_ref = refs[5 * heads : 5 * heads + 2]
    o_r = refs[5 * heads + 2 : 6 * heads + 2]
    u_r = refs[6 * heads + 2 : 7 * heads + 2]
    s_ref, t_ref, cums = refs[7 * heads + 2 :]

    @pl.when(pl.program_id(0) == 0)
    def _():
        end_ref[...] = start_ref[...]

    row, col = iota((SUB, SUB), 0), iota((SUB, SUB), 1)
    strict = col < row
    vis = iota((SPAN, SUB), 1) // NH <= iota((SPAN, SUB), 0)
    items = [(b, h) for b in range(PER_STEP) for h in range(heads)]
    tok = [pl.ds(b * SPAN, SPAN) for b, _ in items]
    sub = [pl.ds(b * SUB, SUB) for b, _ in items]
    eye = jnp.where(row == col, 1.0, 0.0).astype(BF16)
    terms = decay_terms(rows_r, cums, items)
    ks = [k_r[h][sub[i]] for i, (b, h) in enumerate(items)]
    qs = [q_r[h][tok[i]] for i, (b, h) in enumerate(items)]
    prods = [nt(jnp.concatenate([k, q], axis=0), k) for k, q in zip(ks, qs)]
    lowers = [
        t[0] * jnp.exp(jnp.where(strict, t[3] - t[5], FAR)) * p[:SUB] for p, t in zip(prods, terms)
    ]
    inner = [(jnp.exp(jnp.where(vis, t[6] - t[5], FAR)) * p[SUB:]).astype(BF16) for p, t in zip(prods, terms)]
    inverses = unit_lower_inverses(lowers)
    for (b, h), inv in zip(items, inverses):
        t_ref[b, h] = inv
    solved, backs = [], []
    for i, (b, h) in enumerate(items):
        t = terms[i]
        k = ks[i].astype(F32)
        right = jnp.concatenate([t[0] * v_r[h][sub[i]].astype(F32), t[4] * k], axis=1)
        solved.append(nn(inverses[i], right.astype(BF16)))
        weighted = turned((t[2] * k).astype(BF16), eye).astype(BF16)
        backs.append(jnp.concatenate([weighted, inner[i]], axis=0))
    gain = gain_ref[...]
    for b in range(PER_STEP):
        mine = [i for i, it in enumerate(items) if it[0] == b]
        olds = [end_ref[items[i][1]] for i in mine]
        old_bs = [o.astype(BF16) for o in olds]
        reads = [
            nn(jnp.concatenate([solved[i][:, HD:].astype(BF16), qs[i]], axis=0), ob) for i, ob in zip(mine, old_bs)
        ]
        ubs = [(solved[i][:, :HD] - r[:SUB]).astype(BF16) for i, r in zip(mine, reads)]
        adds = [nn(backs[i], ub) for i, ub in zip(mine, ubs)]
        for i, old, ob, r, ub, add in zip(mine, olds, old_bs, reads, ubs, adds):
            h = items[i][1]
            c_col, g_last = terms[i][6:]
            end_ref[h] = jnp.exp(g_last) * old + add[:HD]
            s_ref[b, h] = ob
            u_r[h][sub[i], :] = ub
            o = jnp.exp(c_col) * r[SUB:] + add[HD:]
            o_r[h][tok[i], :] = o.astype(BF16)
            scaled = o * lax.rsqrt(jnp.mean(o * o, axis=-1, keepdims=True) + EPS_NORM) * gain
            gate = g_r[h][tok[i]].astype(F32)
            z_ref[tok[i], h * HD : (h + 1) * HD] = (scaled * gate * sigmoid(gate)).astype(BF16)


def recur_specs(heads, at):
    tok = pl.BlockSpec((PER_STEP * SPAN, HD), lambda i: (at(i), 0))
    sub = pl.BlockSpec((PER_STEP * SUB, HD), lambda i: (at(i), 0))
    rows = pl.BlockSpec((PER_STEP, 8, SUB), lambda i: (at(i), 0, 0))
    wide = pl.BlockSpec((PER_STEP * SPAN, heads * HD), lambda i: (at(i), 0))
    mat = pl.BlockSpec((PER_STEP, heads, HD, HD), lambda i: (at(i), 0, 0, 0))
    one = pl.BlockSpec((1, HD), lambda i: (0, 0))
    state = pl.BlockSpec((heads, HD, HD), lambda i: (0, 0, 0))
    return tok, sub, rows, wide, mat, one, state


def recur(gain, start, q, k, v, gate, rows, first, steps, z=None):
    heads = len(q)
    tok, sub, row, wide, mat, one, state = recur_specs(heads, lambda i: i + first)
    o_tok, o_sub, _, _, o_mat, _, _ = recur_specs(heads, lambda i: i)
    n = steps * PER_STEP
    more = [] if z is None else [z]

    def shape(s, d):
        return jax.ShapeDtypeStruct(s, d)

    res = pl.pallas_call(
        functools.partial(recur_kernel, heads, len(more)),
        out_shape=[shape((q[0].shape[0], heads * HD), BF16), shape((heads, HD, HD), F32)]
        + [shape((n * SPAN, HD), BF16)] * heads
        + [shape((n * SUB, HD), BF16)] * heads
        + [shape((n, heads, HD, HD), BF16)] * 2,
        grid=(steps,),
        in_specs=[one, state]
        + [tok] * heads
        + [sub] * (2 * heads)
        + [tok] * heads
        + [row] * heads
        + [pl.BlockSpec(memory_space=pl.ANY)] * len(more),
        out_specs=[wide, state] + [o_tok] * heads + [o_sub] * heads + [o_mat] * 2,
        scratch_shapes=[pltpu.VMEM((PER_STEP * heads, SUB, SUB), F32)],
        compiler_params=params(),
        input_output_aliases={2 + 5 * heads: 0} if more else {},
        cost_estimate=cost(heads * n * 20 * 4.2e6, 1e6),
        name="recur",
    )(gain, start, *q, *k, *v, *gate, *rows, *more)
    return res[0], res[1], res[2 : 2 + heads], res[2 + heads : 2 + 2 * heads], res[2 + 2 * heads], res[3 + 2 * heads]


def recur_back_kernel(heads, more, gain_ref, start_ref, dz_ref, *refs):
    q_r, k_r, v_r, g_r, rows_r, o_r, u_r = (refs[i * heads : (i + 1) * heads] for i in range(7))
    s_ref, t_ref = refs[7 * heads : 7 * heads + 2]
    refs = refs[: 7 * heads + 2] + refs[7 * heads + 2 + more :]
    d_r = refs[7 * heads + 2 : 8 * heads + 2]
    drows_r = refs[8 * heads + 2 : 9 * heads + 2]
    dgain_ref, end_ref, cums, mixed = refs[9 * heads + 2 :]

    @pl.when(pl.program_id(0) == 0)
    def _():
        end_ref[...] = start_ref[...]
        dgain_ref[...] = jnp.zeros_like(dgain_ref)

    row, col = iota((SUB, SUB), 0), iota((SUB, SUB), 1)
    strict = col < row
    later = jnp.where(row >= col, 1.0, 0.0)
    vis = iota((SPAN, SUB), 1) // NH <= iota((SPAN, SUB), 0)
    gain = gain_ref[...]
    items = [(b, h) for b in reversed(range(PER_STEP)) for h in range(heads)]
    every = range(len(items))
    tok = [pl.ds(b * SPAN, SPAN) for b, _ in items]
    sub = [pl.ds(b * SUB, SUB) for b, _ in items]
    terms = decay_terms(rows_r, cums, items)
    ks = [k_r[h][sub[i]] for i, (b, h) in enumerate(items)]
    qs = [q_r[h][tok[i]] for i, (b, h) in enumerate(items)]
    us = [u_r[h][sub[i]] for i, (b, h) in enumerate(items)]
    ss = [s_ref[b, h] for b, h in items]
    prods = [nt(jnp.concatenate([k, q], axis=0), k) for k, q in zip(ks, qs)]

    dos = []
    dgain = jnp.zeros((1, HD), F32)
    for i, (b, h) in enumerate(items):
        dz = dz_ref[tok[i], h * HD : (h + 1) * HD].astype(F32)
        o = o_r[h][tok[i]].astype(F32)
        gate = g_r[h][tok[i]].astype(F32)
        inv_rms = lax.rsqrt(jnp.mean(o * o, axis=-1, keepdims=True) + EPS_NORM)
        n = o * inv_rms
        sg = sigmoid(gate)
        dy = dz * gate * sg
        d_r[h][tok[i], 5 * HD :] = (dz * n * gain * sg * (1.0 + gate * (1.0 - sg))).astype(BF16)
        dgain += jnp.sum(dy * n, axis=0, keepdims=True)
        dn = dy * gain
        dos.append((inv_rms * (dn - n * jnp.mean(dn * n, axis=-1, keepdims=True))).astype(BF16))
    dgain_ref[...] += dgain

    eye = jnp.where(row == col, 1.0, 0.0).astype(BF16)
    reads = [jnp.exp(jnp.where(vis, t[6] - t[5], FAR)) for t in terms]
    ecs = [jnp.exp(t[6]) for t in terms]
    kfs = [k.astype(F32) for k in ks]
    qfs = [q.astype(F32) for q in qs]
    lefts = [
        jnp.concatenate([turned((p[SUB:] * r).astype(BF16), eye).astype(BF16), (t[2] * k).astype(BF16)], axis=1)
        for p, r, t, k in zip(prods, reads, terms, kfs)
    ]
    downs = [
        turned(jnp.concatenate([(ec * q).astype(BF16), (-t[4] * k).astype(BF16)], axis=0), eye).astype(BF16)
        for ec, q, t, k in zip(ecs, qfs, terms, kfs)
    ]
    solves = [turned(t_ref[b, h], eye).astype(BF16) for b, h in items]

    drs, dsbs, dots = [None] * len(items), [None] * len(items), [None] * len(items)
    for b in reversed(range(PER_STEP)):
        mine = [i for i, it in enumerate(items) if it[0] == b]
        dss = {i: end_ref[items[i][1]] for i in mine}
        for i in mine:
            dsbs[i] = dss[i].astype(BF16)
            dots[i] = jnp.sum(dss[i] * ss[i].astype(F32), axis=0, keepdims=True)
        dus = {i: nn(lefts[i], jnp.concatenate([dos[i], dsbs[i]], axis=0)).astype(BF16) for i in mine}
        for i in mine:
            drs[i] = nn(solves[i], dus[i])
        for i in mine:
            add = nn(downs[i], jnp.concatenate([dos[i], drs[i].astype(BF16)], axis=0))
            end_ref[items[i][1]] = jnp.exp(terms[i][7]) * dss[i] + add

    drbs = [d.astype(BF16) for d in drs]
    from_s = [nt(jnp.concatenate([a, c], axis=0), s) for a, c, s in zip(drbs, dos, ss)]
    from_u = [nt(jnp.concatenate([a, c], axis=0), u) for a, c, u in zip(drbs, dos, us)]
    ks0 = [nn(k, s) for k, s in zip(ks, ss)]
    dws = [nt(u, d) for u, d in zip(us, dsbs)]
    dgs, dbs, dks, minus, dcs, syms = [], [], [], [], [], []
    nms = []
    for i, (b, h) in enumerate(items):
        beta, e_col, e_rest, g_col, beta_e, g_row, c_col, g_last = terms[i]
        k, q = kfs[i], qfs[i]
        mixed[i] = beta * drs[i]
        d_r[h][tok[i], 3 * HD : 4 * HD] = mixed[i, pl.ds(0, SPAN, 2), :].astype(BF16)
        d_r[h][tok[i], 4 * HD : 5 * HD] = mixed[i, pl.ds(1, SPAN, 2), :].astype(BF16)
        t1 = beta_e * from_s[i][:SUB]
        t3 = e_rest * dws[i]
        fade = jnp.exp(jnp.where(strict, g_col - g_row, FAR))
        y = -from_u[i][:SUB] * fade
        le = y * prods[i][:SUB]
        hh = beta * le
        kt3 = k * t3
        dbs.append(lane_sum(drs[i] * (v_r[h][sub[i]].astype(F32) - e_col * ks0[i]) + le))
        dg = lane_sum(hh - k * t1 - kt3)
        d_last = lane_sum(jnp.sum(kt3, axis=0, keepdims=True) + jnp.exp(g_last) * dots[i])
        dgs.append(dg + jnp.where(row[:, :1] == SUB - 1, d_last, 0.0))
        dks.append(t3 - t1)
        dkk = beta * y
        syms.append(dkk + turned(dkk.astype(BF16), eye))
        nm = from_u[i][SUB:] * reads[i]
        hm = nm * prods[i][SUB:]
        t2 = ecs[i] * from_s[i][SUB:]
        nms.append((nm.astype(BF16), t2))
        dcs.append(lane_sum(hm + q * t2))
        minus.append(jnp.sum(hh, axis=0, keepdims=True) + jnp.sum(hm, axis=0, keepdims=True))
    tops = [
        nn(jnp.concatenate([s.astype(BF16), nm], axis=0), k) for s, (nm, _), k in zip(syms, nms, ks)
    ]
    turns = [nn(turned(nm, eye).astype(BF16), q) for (nm, _), q in zip(nms, qs)]
    for i, (b, h) in enumerate(items):
        d_r[h][tok[i], :HD] = (tops[i][SUB:] + nms[i][1]).astype(BF16)
        mixed[i] = dks[i] + tops[i][:SUB] + turns[i]
        d_r[h][tok[i], HD : 2 * HD] = mixed[i, pl.ds(0, SPAN, 2), :].astype(BF16)
        d_r[h][tok[i], 2 * HD : 3 * HD] = mixed[i, pl.ds(1, SPAN, 2), :].astype(BF16)
        cums[i] = jnp.where(col == 0, dbs[i], jnp.where(col == 1, dgs[i], 0.0))
        odd = pl.ds(1, SPAN, 2)
        cums[i, odd, :] = cums[i, odd, :] + jnp.where(col[:SPAN] == 1, dcs[i], 0.0)
        rows = jnp.transpose(cums[i])[:8]
        first = iota((8, SUB), 0)
        summed = exact_nn(rows - jnp.where(first == 1, minus[i], 0.0), later)
        drows_r[h][b] = jnp.where(first == 0, rows, summed)


def recur_back(gain, start, dz, q, k, v, gate, rows, o, u, s, t, first, steps, done=()):
    heads = len(q)
    tok, sub, row, wide, mat, one, state = recur_specs(heads, lambda i: first + steps - 1 - i)
    o_tok, o_sub, _, _, o_mat, _, _ = recur_specs(heads, lambda i: steps - 1 - i)
    n = steps * PER_STEP
    seq = q[0].shape[0]
    d_spec = pl.BlockSpec((PER_STEP * SPAN, 6 * HD), lambda i: (first + steps - 1 - i, 0))

    def shape(s, d):
        return jax.ShapeDtypeStruct(s, d)

    res = pl.pallas_call(
        functools.partial(recur_back_kernel, heads, len(done)),
        out_shape=[shape((seq, 6 * HD), BF16)] * heads
        + [shape((seq // SPAN, 8, SUB), F32)] * heads
        + [shape((1, HD), F32), shape((heads, HD, HD), F32)],
        grid=(steps,),
        in_specs=[one, state, wide]
        + [tok] * heads
        + [sub] * (2 * heads)
        + [tok] * heads
        + [row] * heads
        + [o_tok] * heads
        + [o_sub] * heads
        + [o_mat] * 2
        + [pl.BlockSpec(memory_space=pl.ANY)] * len(done),
        out_specs=[d_spec] * heads + [row] * heads + [one, state],
        scratch_shapes=[pltpu.VMEM((PER_STEP * heads, SUB, SUB), F32)] * 2,
        compiler_params=params(),
        input_output_aliases={5 + 7 * heads + i: i for i in range(len(done))},
        cost_estimate=cost(heads * n * 30 * 4.2e6, 1e6),
        name="recur_back",
    )(gain, start, dz, *q, *k, *v, *gate, *rows, *o, *u, s, t, *done)
    return res[:heads], res[heads : 2 * heads], res[2 * heads], res[2 * heads + 1]


def project_back_kernel(pieces, bit, h, scal_ref, a_ref, cw_ref, raw_ref, rows_ref, d_ref, drow_ref, *refs):
    outer, refs = refs[:pieces], refs[pieces:]
    dp_ref, dcw_ref, dsm_ref = refs[:3]
    stacked = refs[3:5]
    raw_s, ds_s, acc, aux_s = refs[5:]
    tile = a_ref.shape[0]
    depth = outer[0].shape[1]
    chunk = 64
    step, steps = pl.program_id(0), pl.num_programs(0)
    base = pl.multiple_of((steps - 1 - step) * tile, tile)

    @pl.when(step == 0)
    def _():
        ds_s[tile : tile + 8, :] = jnp.zeros_like(ds_s[tile : tile + 8, :])
        dcw_ref[...] = jnp.zeros_like(dcw_ref)
        dsm_ref[...] = jnp.zeros_like(dsm_ref)

    @pl.when(step > 0)
    def _():
        ds_s[tile : tile + 8, :] = ds_s[0:8, :]

    @pl.when(step == steps - 1)
    def _():
        raw_s[0:8, :] = jnp.zeros_like(raw_s[0:8, :])

    @pl.when(step < steps - 1)
    def _():
        before = raw_ref[pl.ds(pl.multiple_of(base - 16, 16), 16), :].astype(F32)
        raw_s[0:8, :] = before[8:]

    raw_s[8 : tile + 8, :] = raw_ref[pl.ds(base, tile), :].astype(F32)
    for g in range(5):
        lanes = slice(g * HD, (g + 1) * HD)
        taps = cw_ref[0, :, lanes]
        sums = [jnp.zeros((8, HD), F32)] * TAPS
        for i in range(tile // chunk):
            start = i * chunk
            shifted = conv_shifts(raw_s, start, chunk, lanes)
            pre = shifted[0] * taps[0:1]
            for j in range(1, TAPS):
                pre = pre + shifted[j] * taps[j : j + 1]
            sg = sigmoid(pre)
            act = pre * sg
            d = d_ref[start : start + chunk, lanes].astype(F32)
            if g < 3:
                inv = lax.rsqrt(lane_sum(act * act) + EPS_UNIT)
                unit = act * inv
                d = inv * (d - unit * lane_sum(d * unit))
            d = d * (sg + act * (1.0 - sg))
            ds_s[start : start + chunk, lanes] = d
            sums = [s + jnp.sum((d * x).reshape(chunk // 8, 8, HD), axis=0) for s, x in zip(sums, shifted)]
        for j in range(TAPS):
            dcw_ref[j : j + 1, lanes] += jnp.sum(sums[j], axis=0, keepdims=True)
        for i in range(tile // chunk):
            start = i * chunk
            views = conv_shifts_back(ds_s, start, chunk, lanes)
            total = views[0] * taps[0:1]
            for j in range(1, TAPS):
                total = total + views[j] * taps[j : j + 1]
            dp_ref[start : start + chunk, lanes] = total.astype(BF16)

    rate = scal_ref[h, 0]
    lane = iota((SPAN, HD), 1)
    total = jnp.zeros((8, HD), F32)
    for b in range(tile // SPAN):
        both = jnp.concatenate([rows_ref[b], drow_ref[b]] + [jnp.zeros((8, SUB), F32)] * (SUB // 8 - 2), axis=0)
        aux_s[b] = jnp.transpose(both)
        even, odd = aux_s[b, pl.ds(0, SPAN, 2), :], aux_s[b, pl.ds(1, SPAN, 2), :]
        b1, b2, dg = even[:, 0:1], odd[:, 0:1], even[:, 9:10]
        darg = -rate * dg * sigmoid(even[:, 2:3])
        d1 = even[:, 8:9] * b1 * (1.0 - b1)
        d2 = odd[:, 8:9] * b2 * (1.0 - b2)
        vals = jnp.where(lane == 0, d1, jnp.where(lane == 1, d2, jnp.where(lane == 2, darg, 0.0)))
        here = pl.ds(b * SPAN, SPAN)
        dp_ref[here, 6 * HD :] = vals[:, :SMALL].astype(BF16)
        dp_ref[here, 5 * HD : 6 * HD] = d_ref[here, 5 * HD :]
        extra = jnp.where(lane == 0, dg * even[:, 1:2], jnp.where(lane == 1, darg, 0.0))
        total += jnp.sum(extra.reshape(SPAN // 8, 8, HD), axis=0)
    dsm_ref[...] += total

    term = tn(dp_ref[...], a_ref[...])

    @pl.when(step == 0)
    def _():
        acc[...] = term

    @pl.when(step > 0)
    def _():
        acc[...] += term

    @pl.when(step == steps - 1)
    def _():
        for stack, group in zip(stacked, sides(pieces, bit)):
            for i, p in enumerate(group):
                stack[i, :HD] = outer[p][...]
                stack[i, HD:] = acc[:, p * depth : (p + 1) * depth].astype(BF16)


def project_back(h, normed, conv_t, scal, raw, rows, d, drows, outer, bit):
    seq, dim = normed.shape
    pieces = len(outer)
    depth = outer[0].shape[1]
    tile = min(512, seq)
    end = seq // tile - 1
    along = lambda i: (end - i, 0)
    deep = pl.BlockSpec((tile // SPAN, 8, SUB), lambda i: (end - i, 0, 0))
    fix = lambda i: (0, 0)
    outs = [((seq, UNITS), BF16), ((8, 5 * HD), F32), ((8, HD), F32)]
    shapes = [jax.ShapeDtypeStruct(s, t) for s, t in outs] + stacks(pieces, (HD + UNITS, depth))
    res = pl.pallas_call(
        functools.partial(project_back_kernel, pieces, bit, h),
        out_shape=shapes,
        grid=(seq // tile,),
        in_specs=[
            pl.BlockSpec(memory_space=pltpu.SMEM),
            pl.BlockSpec((tile, dim), along),
            pl.BlockSpec((1,) + conv_t.shape[1:], lambda i: (h, 0, 0)),
            pl.BlockSpec(raw.shape, fix),
            deep,
            pl.BlockSpec((tile, 6 * HD), along),
            deep,
        ]
        + [pl.BlockSpec(g.shape, fix) for g in outer],
        out_specs=[pl.BlockSpec((tile, UNITS), along)]
        + [pl.BlockSpec(s, fix) for s, _ in outs[1:]]
        + [pl.BlockSpec(v.shape, lambda i: (0, 0, 0)) for v in shapes[3:]],
        scratch_shapes=[
            pltpu.VMEM((tile + 8, 5 * HD), F32),
            pltpu.VMEM((tile + 8, 5 * HD), F32),
            pltpu.VMEM((UNITS, dim), F32),
            pltpu.VMEM((tile // SPAN, SUB, SUB), F32),
        ],
        compiler_params=params(),
        cost_estimate=cost(2 * seq * dim * UNITS, 1e6),
        name="project_back",
    )(scal, normed, conv_t, raw, rows, d, drows, *outer)
    return res[0], res[1], res[2], res[3:]


def input_back_kernel(heads, pieces, *refs):
    dps, parts = refs[:heads], refs[heads : heads + heads * pieces]
    x_ref, da_ref, dgain_ref = refs[heads + heads * pieces :]
    depth = parts[0].shape[1]
    x = x_ref[...].astype(F32)
    unit = x * lax.rsqrt(jnp.mean(x * x, axis=-1, keepdims=True) + EPS_NORM)
    shares = []
    for p in range(pieces):
        total = nn(
            jnp.concatenate([d[:, 6 * HD :] for d in dps], axis=1),
            jnp.concatenate([parts[h * pieces + p][7 * HD :] for h in range(heads)], axis=0),
        )
        for h in range(heads):
            total += nn(dps[h][:, : 6 * HD], parts[h * pieces + p][HD : 7 * HD])
        low = total.astype(BF16)
        lanes = slice(p * depth, (p + 1) * depth)
        da_ref[:, lanes] = low
        shares.append(jnp.sum(low.astype(F32) * unit[:, lanes], axis=0, keepdims=True))
    share = jnp.concatenate(shares, axis=1)

    @pl.when(pl.program_id(0) == 0)
    def _():
        dgain_ref[...] = share

    @pl.when(pl.program_id(0) > 0)
    def _():
        dgain_ref[...] += share


def input_back(dps, parts, x):
    seq = dps[0].shape[0]
    heads, pieces = len(parts), len(parts[0])
    flat = [w for head in parts for w in head]
    dim = pieces * flat[0].shape[1]
    tile = min(256, seq)
    along = lambda i: (i, 0)
    return pl.pallas_call(
        functools.partial(input_back_kernel, heads, pieces),
        out_shape=[jax.ShapeDtypeStruct((seq, dim), BF16), jax.ShapeDtypeStruct((1, dim), F32)],
        grid=(seq // tile,),
        in_specs=[pl.BlockSpec((tile, UNITS), along)] * heads
        + [pl.BlockSpec(w.shape, lambda i: (0, 0)) for w in flat]
        + [pl.BlockSpec((tile, dim), along)],
        out_specs=[pl.BlockSpec((tile, dim), along), pl.BlockSpec((1, dim), lambda i: (0, 0))],
        compiler_params=params(),
        cost_estimate=cost(2 * seq * dim * UNITS * heads, 1e6),
        name="input_back",
    )(*dps, *flat, x)


def mix_kernel(heads, pieces, z_ref, *refs):
    parts, out_ref = refs[:-1], refs[-1]
    depth = parts[0].shape[1]
    for p in range(pieces):
        right = jnp.concatenate([parts[h * pieces + p][...] for h in range(heads)], axis=0)
        out_ref[:, p * depth : (p + 1) * depth] = nn(z_ref[...], right).astype(BF16)


def outer_specs(parts):
    return [pl.BlockSpec((HD, w.shape[1]), lambda i: (0, 0)) for head in parts for w in head]


def mix_out(z, parts):
    seq = z.shape[0]
    heads, pieces = len(parts), len(parts[0])
    dim = pieces * parts[0][0].shape[1]
    tile = min(256, seq)
    along = lambda i: (i, 0)
    return pl.pallas_call(
        functools.partial(mix_kernel, heads, pieces),
        out_shape=jax.ShapeDtypeStruct((seq, dim), BF16),
        grid=(seq // tile,),
        in_specs=[pl.BlockSpec((tile, z.shape[1]), along)] + outer_specs(parts),
        out_specs=pl.BlockSpec((tile, dim), along),
        compiler_params=params(),
        cost_estimate=cost(2 * seq * dim * z.shape[1], 1e6),
        name="mix_out",
    )(z, *[w for head in parts for w in head])


def mix_back_kernel(heads, pieces, gain_ref, own_ref, other_ref, mid_ref, dy_ref, z_ref, *refs):
    parts, refs = refs[: heads * pieces], refs[heads * pieces :]
    dmix_ref, dz_ref, dgain_ref = refs[:3]
    grads, acc = refs[3:-1], refs[-1]
    depth = parts[0].shape[1]
    step, steps = pl.program_id(0), pl.num_programs(0)
    mid = mid_ref[...]
    dn = own_ref[...].astype(F32) + other_ref[...].astype(F32)
    inv = lax.rsqrt(jnp.mean(mid * mid, axis=-1, keepdims=True) + EPS_NORM)
    unit = mid * inv
    prod = dn * unit
    share = jnp.sum(prod, axis=0, keepdims=True)
    scaled = dn * gain_ref[...]
    back = inv * (scaled - unit * jnp.mean(prod * gain_ref[...], axis=-1, keepdims=True))
    dmix_ref[...] = (dy_ref[...].astype(F32) + back).astype(BF16)

    @pl.when(step == 0)
    def _():
        dgain_ref[...] = share
        acc[...] = jnp.zeros_like(acc)

    @pl.when(step > 0)
    def _():
        dgain_ref[...] += share

    dz = jnp.zeros((z_ref.shape[0], heads * HD), F32)
    for p in range(pieces):
        lanes = slice(p * depth, (p + 1) * depth)
        right = jnp.concatenate([parts[h * pieces + p][...] for h in range(heads)], axis=0)
        dz += nt(dmix_ref[:, lanes], right)
    acc[...] += tn(z_ref[...], dmix_ref[...])
    dz_ref[...] = dz.astype(BF16)

    @pl.when(step == steps - 1)
    def _():
        for h in range(heads):
            for p in range(pieces):
                grads[h * pieces + p][...] = acc[h * HD : (h + 1) * HD, p * depth : (p + 1) * depth].astype(BF16)


def mix_back(gain, own, other, mid, dy, z, parts):
    seq, dim = mid.shape
    heads, pieces = len(parts), len(parts[0])
    wide = z.shape[1]
    tile = min(256, seq)
    row = pl.BlockSpec((tile, dim), lambda i: (i, 0))
    one = pl.BlockSpec((1, dim), lambda i: (0, 0))
    zs = pl.BlockSpec((tile, wide), lambda i: (i, 0))
    res = pl.pallas_call(
        functools.partial(mix_back_kernel, heads, pieces),
        out_shape=[
            jax.ShapeDtypeStruct((seq, dim), BF16),
            jax.ShapeDtypeStruct((seq, wide), BF16),
            jax.ShapeDtypeStruct((1, dim), F32),
        ]
        + [jax.ShapeDtypeStruct((HD, dim // pieces), BF16)] * (heads * pieces),
        grid=(seq // tile,),
        in_specs=[one, row, row, row, row, zs] + outer_specs(parts),
        out_specs=[row, zs, one] + outer_specs(parts),
        scratch_shapes=[pltpu.VMEM((wide, dim), F32)],
        compiler_params=params(),
        cost_estimate=cost(4 * seq * dim * wide, 1e6),
        name="mix_back",
    )(gain, own, other, mid, dy, z, *[w for head in parts for w in head])
    return res[0], res[1], res[2], [res[3 + h * pieces : 3 + (h + 1) * pieces] for h in range(heads)]


def select_kernel(counts, apart, table_ref, *refs):
    j = pl.program_id(0)
    first = 0
    for g, n in enumerate(counts):
        width = refs[first].shape[2]
        value = refs[first][...]
        for i in range(1, n):
            value = jnp.where(table_ref[2 * g, j] == i, refs[first + i][...], value)
        if apart:
            refs[sum(counts) + g][...] = value
        else:
            refs[-1][:, :, g * width : (g + 1) * width] = value
        first += n


def select_blocks(groups, table, count, apart=False):
    specs, flat = [], []
    for g, sources in enumerate(groups):
        for i, value in enumerate(sources):

            def where(j, t, g=g, i=i):
                return (jnp.where(t[2 * g, j] == i, t[2 * g + 1, j], 0), 0, 0)

            specs.append(pl.BlockSpec((1,) + value.shape[1:], where))
            flat.append(value)
    piece, width = flat[0].shape[1:]
    total = width if apart else width * len(groups)
    outs = len(groups) if apart else 1
    res = pl.pallas_call(
        functools.partial(select_kernel, [len(g) for g in groups], apart),
        out_shape=[jax.ShapeDtypeStruct((count, piece, total), flat[0].dtype)] * outs,
        grid_spec=pltpu.PrefetchScalarGridSpec(
            num_scalar_prefetch=1,
            grid=(count,),
            in_specs=specs,
            out_specs=[pl.BlockSpec((1, piece, total), lambda j, t: (j, 0, 0))] * outs,
        ),
        compiler_params=params(),
        cost_estimate=cost(1e6, 1e6),
        name="select_blocks",
    )(table, *flat)
    return res if apart else res[0]


def ffn_kernel(pieces, chunks, bits, more, b_ref, dy_ref, *refs):
    weights = refs[: pieces * chunks]
    refs = refs[pieces * chunks :]
    sums_in, refs = (refs[:2], refs[2:]) if more else (None, refs)
    out_ref, db_ref = refs[:2]
    stacked = refs[2 : 2 + 2 * chunks]
    b_s, dy_s, hid_s, dg_s, du_s = refs[2 + 2 * chunks :]
    depth = weights[0].shape[1]
    units = weights[0].shape[0] // 3
    tile = b_ref.shape[0]
    step, steps = pl.program_id(0), pl.num_programs(0)

    def weight(p, i):
        return jnp.concatenate(
            [weights[c * pieces + p][i * units : (i + 1) * units] for c in range(chunks)], axis=0
        )

    rows = pl.ds(pl.multiple_of(step * tile, tile), tile)
    b_s[rows, :] = b_ref[...]
    dy_s[rows, :] = dy_ref[...]
    gate = jnp.zeros((tile, units * chunks), F32)
    up = jnp.zeros((tile, units * chunks), F32)
    dh = jnp.zeros((tile, units * chunks), F32)
    for p in range(pieces):
        lanes = slice(p * depth, (p + 1) * depth)
        block, dblock = b_ref[:, lanes], dy_ref[:, lanes]
        gate += nt(block, weight(p, 0))
        up += nt(block, weight(p, 1))
        dh += nt(dblock, weight(p, 2))
    sg = sigmoid(gate)
    act = gate * sg
    hid = (act * up).astype(BF16)
    du = (dh * act).astype(BF16)
    dg = (dh * up * (sg + act * (1.0 - sg))).astype(BF16)
    hid_s[rows, :] = hid
    dg_s[rows, :] = dg
    du_s[rows, :] = du
    for p in range(pieces):
        lanes = slice(p * depth, (p + 1) * depth)
        o = nn(hid, weight(p, 2))
        d = nn(dg, weight(p, 0)) + nn(du, weight(p, 1))
        if more:
            o += sums_in[0][:, lanes].astype(F32)
            d += sums_in[1][:, lanes].astype(F32)
        out_ref[:, lanes] = o.astype(out_ref.dtype)
        db_ref[:, lanes] = d.astype(db_ref.dtype)

    @pl.when(step == steps - 1)
    def _():
        for i, (left, right) in enumerate([(dg_s, b_s), (du_s, b_s), (hid_s, dy_s)]):
            g = tn(left[...], right[...]).astype(BF16)
            for c in range(chunks):
                for stack, group in zip(stacked[2 * c : 2 * c + 2], sides(pieces, bits[c])):
                    for n, p in enumerate(group):
                        stack[n, i * units : (i + 1) * units] = g[
                            c * units : (c + 1) * units, p * depth : (p + 1) * depth
                        ]


def ffn(normed, dy, parts, bits, sums=None, last=True):
    seq, dim = normed.shape
    chunks, pieces = len(parts), len(parts[0])
    flat = [w for chunk in parts for w in chunk]
    units = flat[0].shape[0] // 3
    tile = min(256, seq)
    row = pl.BlockSpec((tile, dim), lambda i: (i, 0))
    more = () if sums is None else tuple(sums)
    grads = stacks(pieces, flat[0].shape) * chunks
    res = pl.pallas_call(
        functools.partial(ffn_kernel, pieces, chunks, bits, bool(more)),
        out_shape=[jax.ShapeDtypeStruct((seq, dim), BF16 if last else F32)] * 2 + grads,
        grid=(seq // tile,),
        in_specs=[row, row] + [pl.BlockSpec(w.shape, lambda i: (0, 0)) for w in flat] + [row] * len(more),
        out_specs=[row, row] + [pl.BlockSpec(g.shape, lambda i: (0, 0, 0)) for g in grads],
        scratch_shapes=[pltpu.VMEM((seq, dim), BF16)] * 2 + [pltpu.VMEM((seq, units * chunks), BF16)] * 3,
        compiler_params=params(),
        cost_estimate=cost(18 * seq * dim * units * chunks, 1e6),
        name="ffn",
    )(normed, dy, *flat, *more)
    return res[0], res[1], [res[2 + 2 * c : 4 + 2 * c] for c in range(chunks)]


def sync(*trees):
    leaves, tree = jax.tree.flatten(trees)
    return jax.tree.unflatten(tree, lax.optimization_barrier(leaves))


def bits_of(n):
    return [1 << i for i in range(n.bit_length() - 1)]


class Place:
    def __init__(self):
        self.n_f = lax.axis_size("fsdp")
        self.n_t = lax.axis_size("tp")
        self.chips = self.n_f // 2
        f = lax.axis_index("fsdp")
        self.f = f
        self.core = f % 2
        self.k = f // 2
        self.t = lax.axis_index("tp")

    def swap(self, value):
        return lax.ppermute(value, "fsdp", [(i, i ^ 1) for i in range(self.n_f)])

    def move(self, value, bit):
        return lax.ppermute(value, "fsdp", [(i, i ^ (2 * bit)) for i in range(self.n_f)])

    def turn(self, value, r):
        return lax.ppermute(value, "tp", [(i, (i + r) % self.n_t) for i in range(self.n_t)])

    def in_order(self, mine, other, axis):
        first = jnp.where(self.core == 0, mine, other)
        second = jnp.where(self.core == 0, other, mine)
        return jnp.concatenate([first, second], axis=axis)

    def halves(self, value, axis):
        size = value.shape[axis] // 2
        return (
            lax.dynamic_slice_in_dim(value, self.core * size, size, axis),
            lax.dynamic_slice_in_dim(value, (1 - self.core) * size, size, axis),
        )

    def relative(self, value):
        width = value.shape[-1] // self.chips
        blocks = [
            lax.dynamic_slice_in_dim(value, (self.k ^ p) * width, width, value.ndim - 1) for p in range(self.chips)
        ]
        return jnp.concatenate(blocks, axis=-1)

    def spread_out(self, value):
        if value.shape[0] < self.n_t:
            value = jnp.pad(value, ((0, self.n_t - value.shape[0]),) + ((0, 0),) * (value.ndim - 1))
        return lax.all_to_all(value, "tp", split_axis=0, concat_axis=0, tiled=True)

    def chip_sum(self, value):
        for bit in [1] + [2 * b for b in bits_of(self.chips)]:
            value = value + lax.ppermute(value, "fsdp", [(i, i ^ bit) for i in range(self.n_f)])
        return value

    def line_sum(self, value):
        total = value
        for r in range(1, self.n_t):
            total = total + self.turn(value, r)
        return total


def rms_terms(value):
    return lax.rsqrt(jnp.mean(value * value, axis=-1, keepdims=True) + EPS_NORM)


def rms_back(value, gain, d_normed):
    inv = rms_terms(value)
    unit = value * inv
    dn = d_normed * gain
    return inv * (dn - unit * jnp.mean(dn * unit, axis=-1, keepdims=True))


class Gather:
    def __init__(self, at, shard):
        self.at = at
        self.parts = {(0, 0): shard}

    def turn(self, r, by=None):
        by = by or r
        self.parts[r, 0] = self.at.turn(self.parts[r - by, 0], by)

    def move(self, r, to, via):
        self.parts[r, to] = self.at.move(self.parts[r, to ^ via], via)

    def full(self, r):
        return [self.parts[r, p] for p in range(self.at.chips)]

    def rest(self):
        for r in range(1, self.at.n_t):
            self.turn(r)
        for r in range(self.at.n_t):
            for p in range(1, self.at.chips):
                self.move(r, p, p & -p)
        return [self.full(r) for r in range(self.at.n_t)]


def first_bit(at, r):
    return at.chips // 2 if r % 3 == 0 else 1


class Scatter:
    def __init__(self, at):
        self.at = at
        self.near, self.far, self.two, self.one, self.end = {}, {}, {}, {}, {}

    def put(self, r, stacked):
        self.near[r], self.far[r] = stacked

    def cross(self, *turns):
        for r in turns:
            self.far[r] = self.at.move(self.far[r], first_bit(self.at, r))

    def fold(self, *turns):
        sums = add_stacks([(self.near.pop(r), self.far.pop(r)) for r in turns])
        for r, (keep, give) in zip(turns, sums):
            self.two[r] = keep, self.at.move(give, 3 - first_bit(self.at, r))

    def close(self, *turns):
        for r in turns:
            keep, came = self.two.pop(r)
            self.one[r] = (keep.astype(F32) + came.astype(F32)).astype(BF16)

    def home(self, r):
        self.end[r] = self.at.turn(self.one.pop(r), self.at.n_t - r)

    def merge(self, r):
        self.end[r] = self.at.turn(self.one.pop(r), self.at.n_t - 1)

    def join(self, r):
        self.one[r - 1] = (self.one[r - 1].astype(F32) + self.end.pop(r).astype(F32)).astype(BF16)

    def total(self):
        return sum(v.astype(F32) for v in list(self.one.values()) + list(self.end.values()))

    def state(self):
        return self.near, self.far, self.two, self.one, self.end

    def take(self, state):
        self.near, self.far, self.two, self.one, self.end = state

    def rest(self):
        for r in range(self.at.n_t):
            have = {}
            for stack, group in zip((self.near.pop(r), self.far.pop(r)), sides(self.at.chips, first_bit(self.at, r))):
                have.update({p: stack[i] for i, p in enumerate(group)})
            for bit in bits_of(self.at.chips):
                for p in [p for p in have if p & bit]:
                    came = self.at.move(have.pop(p), bit)
                    have[p ^ bit] = (have[p ^ bit].astype(F32) + came.astype(F32)).astype(BF16)
            self.one[r] = have[0]
            if r:
                self.home(r)


class Routing:
    def __init__(self, at, value, order, source):
        self.at, self.order = at, order
        self.per_chip = value.shape[0]
        self.have, self.where = [value], [0]
        reach = [0]
        for bit in order[:-1]:
            reach += [w | bit for w in reach]
        tables = []
        for chip in (at.k ^ order[-1], at.k):
            ask = lax.dynamic_slice_in_dim(source, chip * self.per_chip, self.per_chip, 0)
            distance = (ask // self.per_chip) ^ at.k
            src = sum(jnp.where(distance == w, i, 0) for i, w in enumerate(reach))
            near = (distance & order[-1]) == 0
            slot = ask % self.per_chip
            if chip is not at.k:
                tables.append((src, slot))
            else:
                tables.append(
                    (
                        jnp.where(near, src, len(reach)),
                        jnp.where(near, slot, jnp.arange(self.per_chip, dtype=jnp.int32)),
                    )
                )
        self.ask, self.keep = (jnp.stack(t) for t in tables)

    def step(self):
        bit = self.order[len(self.where).bit_length() - 1]
        self.have = self.have + [self.at.move(v, bit) for v in self.have]
        self.where = self.where + [w | bit for w in self.where]

    def last(self, give):
        self.have = self.have + [self.at.move(give, self.order[-1])]


def local(
    tokens, lengths, perm, cotangent, norm1_gain, input_weight, conv_w, decay_log, decay_bias, out_gain, w_out,
    norm2_gain, gate_up_weight, down_weight
):
    at = Place()
    slots, piece, dim = tokens.shape
    n_f, n_t, chips = at.n_f, at.n_t, at.chips
    heads_all = conv_w.shape[0]
    heads = heads_all // 2
    local_heads = input_weight.shape[1]
    cols = input_weight.shape[2]
    by_turn = local_heads == 2
    laps = list(range(n_t))
    bits = bits_of(chips)
    fast = by_turn and chips == 4 and n_t == 4
    per_chip = 2 * slots
    seq = n_t * piece
    steps = seq // SPAN // PER_STEP // 2

    pad = SMALL - (cols - 6 * HD)
    if by_turn:
        packed = jnp.transpose(input_weight, (1, 2, 0))
        zeros = jnp.zeros((local_heads, pad, packed.shape[2]), BF16)
        packed = jnp.concatenate([w_out.reshape(local_heads, HD, -1), packed, zeros], axis=1)
        mine, give = at.halves(packed, 0)
        m_own = at.in_order(mine[0], at.swap(give[0]), 1)
        head_ids = ((at.t - jnp.arange(n_t, dtype=jnp.int32)) % n_t) * 2 + at.core
    else:
        m_own = None
        head_ids = at.core * heads + jnp.arange(heads, dtype=jnp.int32)
    m_own, tokens, gate_up_weight, down_weight, cotangent = sync(
        m_own, tokens, gate_up_weight, down_weight, cotangent
    )
    mine, give = at.halves(tokens, 2)
    both = at.in_order(mine, at.swap(give), 0)
    packed = jnp.concatenate([jnp.transpose(gate_up_weight, (1, 2, 0)), down_weight[None]], axis=0)
    mine, give = at.halves(packed, 1)
    f_own = at.in_order(mine, at.swap(give), 2)
    f_own = f_own.reshape(-1, f_own.shape[2])
    mine, give = at.halves(cotangent, 2)
    cot_both = at.in_order(mine, at.swap(give), 0)

    own = head_ids[:, None] == jnp.arange(heads_all, dtype=jnp.int32)[None, :]
    taps = jnp.pad(jnp.transpose(conv_w, (0, 2, 1)), ((0, 0), (0, 8 - TAPS), (0, 0)))
    conv_t = jnp.sum(jnp.where(own[:, :, None, None], taps[None], 0.0), axis=1)
    scal = jnp.stack(
        [
            jnp.sum(jnp.where(own, jnp.exp(decay_log)[None], 0.0), axis=1),
            jnp.sum(jnp.where(own, decay_bias[None], 0.0), axis=1),
        ],
        axis=1,
    )
    gain1 = at.relative(norm1_gain)
    gain2 = at.relative(norm2_gain)
    gain_o = out_gain[None]
    start_state = jnp.zeros((heads, HD, HD), F32)

    seq_id = jnp.minimum(at.k * per_chip + at.t, lengths.shape[0] - 1)
    length = jnp.where(at.t < per_chip, lax.dynamic_index_in_dim(lengths, seq_id, 0, keepdims=False), 0)
    live = (jnp.arange(seq, dtype=jnp.int32) < length).astype(BF16)[:, None]
    slot_ids = jnp.arange(perm.shape[0], dtype=jnp.int32)
    source = jnp.sum(jnp.where(perm[None, :] == slot_ids[:, None], slot_ids[None, :], 0), axis=1)
    quarter = dim // 4
    routes = [
        Routing(at, cot_both[:, :, :quarter], bits, source),
        Routing(at, cot_both[:, :, quarter:], bits[::-1], source),
    ]

    def route_state():
        return [r.have for r in routes]

    def set_routes(state):
        for r, v in zip(routes, state):
            r.have = v

    def routed():
        groups = [r.have for r in routes]
        return select_blocks(groups, jnp.concatenate([r.keep for r in routes], axis=0), per_chip)

    def sequence(half):
        half = half.reshape(seq, -1)
        return at.relative(at.in_order(half, at.swap(half), 1))

    def norm_first(x):
        return (x * rms_terms(x) * gain1).astype(BF16)

    f = Gather(at, f_own)
    proj = {}

    def asked():
        return select_blocks([r.have for r in routes], jnp.concatenate([r.ask for r in routes], axis=0), per_chip, True)

    if fast:
        m = Gather(at, m_own)

        def run(r):
            proj[r] = project(r, normed_one, m.full(r), conv_t, scal)

        def without(parts, *keys):
            return {k: v for k, v in parts.items() if k not in keys}

        for p in range(1, chips):
            m.move(0, p, p)
        m.turn(1)
        m.turn(3)
        m.parts, f.parts, both, cot_both, conv_t, scal, gain1, gain2, live, extra = sync(
            m.parts, f.parts, both, cot_both, conv_t, scal, gain1, gain2, live, [(r.ask, r.keep) for r in routes]
        )
        for r, (ask, keep), part in zip(routes, extra, (cot_both[:, :, :quarter], cot_both[:, :, quarter:])):
            r.ask, r.keep, r.have = ask, keep, [part]
        for r in (1, 3):
            m.move(r, 1, 1)
            m.move(r, 2, 2)
        came = at.spread_out(both)
        m.turn(2, 1)
        m.parts, f.parts, came = sync(m.parts, f.parts, came)
        m.move(1, 3, 1)
        m.move(3, 3, 2)
        m.move(2, 1, 1)
        m.move(2, 2, 2)
        x = sequence(came)
        normed_one = norm_first(x.astype(F32))
        run(0)
        early = without(m.parts, (2, 1), (2, 2))
        early, f.parts, proj[0], normed_one, x = sync(early, f.parts, proj[0], normed_one, x)
        m.parts.update(early)
        m.move(2, 3, 3)
        f.turn(1)
        f.turn(3)
        run(1)
        run(3)
        state = route_state()
        m.parts, proj, normed_one, f.parts, state = sync(m.parts, proj, normed_one, f.parts, state)
        set_routes(state)
        for r in routes:
            r.step()
        f.move(0, 1, 1)
        f.move(0, 2, 2)
        run(2)
        early = without(f.parts, (0, 1), (0, 2))
        state = route_state()
        proj, early, state = sync(proj, early, state)
        f.parts.update(early)
        set_routes(state)
        give = asked()
        m_parts = [m.full(r) for r in laps]
    else:
        x = sequence(at.spread_out(both))
        normed_one = norm_first(x.astype(F32))
        if by_turn:
            m_parts = Gather(at, m_own).rest()
        else:
            full = lax.all_gather(lax.all_gather(input_weight, "tp", axis=1, tiled=True), "fsdp", axis=0, tiled=True)
            full = at.relative(jnp.transpose(full, (1, 2, 0)))
            full_out = lax.all_gather(lax.all_gather(w_out, "tp", axis=0, tiled=True), "fsdp", axis=1, tiled=True)
            full_out = at.relative(full_out).reshape(heads_all, HD, dim)
            zeros = jnp.zeros((heads_all, pad, dim), BF16)
            full = at.halves(jnp.concatenate([full_out, full, zeros], axis=1), 0)[0]
            m_parts = [jnp.split(full[h], chips, axis=1) for h in range(heads)]
        for h in range(heads):
            proj[h] = project(h, normed_one, m_parts[h], conv_t, scal)
        for r in routes:
            for _ in bits[1:]:
                r.step()
        give = asked()
        f_parts = f.rest()

    raw, gate, q, k, v, rows = (list(group) for group in zip(*[proj[h] for h in range(heads)]))
    for r, part in zip(routes, give):
        r.last(part)
    if fast:
        f.move(1, 1, 1)
        f.move(1, 2, 2)
    first = recur(gain_o, start_state, q, k, v, gate, rows, 0, steps)
    if fast:
        state = route_state()
        first, f.parts, state = sync(first, f.parts, state)
        set_routes(state)
    cot_came = at.spread_out(routed())
    if fast:
        f.move(0, 3, 2)
        f.move(1, 3, 1)
        f.move(3, 1, 1)
        f.turn(2, 1)
    second = recur(gain_o, first[1], q, k, v, gate, rows, steps, steps, first[0])
    if fast:
        second, f.parts, cot_came = sync(second, f.parts, cot_came)
        f.move(3, 2, 2)
        f.move(2, 1, 1)
    z = second[0]
    mix = mix_out(z, m_parts)
    mid = x.astype(F32) + (mix.astype(F32) + at.swap(mix).astype(F32))
    normed_two = (mid * rms_terms(mid) * gain2).astype(BF16)
    dy = live * sequence(cot_came)

    f_rs = Scatter(at)
    half = n_t // 2
    group_a, group_b = laps[:half], laps[half:][::-1]
    bits_a, bits_b = [first_bit(at, r) for r in group_a], [first_bit(at, r) for r in group_b]
    if fast:
        normed_two, dy, f.parts = sync(normed_two, dy, f.parts)
        f.move(3, 3, 2)
        f.move(2, 2, 2)
        f.move(2, 3, 2)
        f_parts = {r: f.full(r) for r in group_a}
    net, db, grads = ffn(normed_two, dy, [f_parts[r] for r in group_a], bits_a, last=False)
    if fast:
        net, db, grads, f.parts = sync(net, db, grads, f.parts)
        f_parts = {r: f.full(r) for r in group_b}
    for r, g in zip(group_a, grads):
        f_rs.put(r, g)
    if fast:
        f_rs.cross(0, 1)
    net, db, grads = ffn(normed_two, dy, [f_parts[r] for r in group_b], bits_b, (net, db))
    if fast:
        net, db, grads, state = sync(net, db, grads, f_rs.state())
        f_rs.take(state)
    for r, g in zip(group_b, grads):
        f_rs.put(r, g)

    db_other = at.swap(db)
    if fast:
        f_rs.fold(0, 1)
        f_rs.cross(3, 2)
    d_mix, dz, g_gain2, g_out = mix_back(gain2[None], db, db_other, mid, dy, z, m_parts)
    if fast:
        dz, d_mix, g_out, f_rs.two, net = sync(dz, d_mix, g_out, f_rs.two, net)
    net_other = at.swap(net)
    back = recur_back(gain_o, start_state, dz, q, k, v, gate, rows, *second[2:], steps, steps)
    if fast:
        back, state, net_other, dz = sync(back, f_rs.state(), net_other, dz)
        f_rs.take(state)
        f_rs.close(0, 1)
        f_rs.fold(3, 2)

    def give_back(value):
        mine = at.halves(at.relative(value.astype(BF16)), 1)[0]
        return mine.reshape(n_t, piece, dim // 2)

    def settle(came):
        mine, give = at.halves(came[:per_chip], 0)
        return at.in_order(mine, at.swap(give), 2)

    g_gain_o = back[2]
    out_home = give_back(live.astype(F32) * (mid + (net.astype(F32) + net_other.astype(F32))))
    out_came = lax.all_to_all(out_home, "tp", split_axis=0, concat_axis=0, tiled=True)
    back = recur_back(
        gain_o, back[3], dz, q, k, v, gate, rows, *first[2:], 0, steps, tuple(back[0]) + tuple(back[1])
    )
    g_gain_o = g_gain_o + back[2]
    ds, drows = back[:2]
    if fast:
        ds, drows, out_came, state = sync(ds, drows, out_came, f_rs.state())
        f_rs.take(state)
        f_rs.close(3, 2)
        f_rs.merge(2)
        f_rs.home(3)

    dps, g_conv, g_small = {}, {}, {}
    m_rs = Scatter(at)

    def run_back(h):
        dps[h], g_conv[h], g_small[h], grads = project_back(
            h, normed_one, conv_t, scal, raw[h], rows[h], ds[h], drows[h], g_out[h], first_bit(at, h)
        )
        m_rs.put(h, grads)

    if fast:
        run_back(2)
        dps, state, f_state, ds = sync(dps, m_rs.state(), f_rs.state(), ds)
        m_rs.take(state)
        f_rs.take(f_state)
        f_rs.join(2)
        f_rs.home(1)
        m_rs.cross(2)
        run_back(1)
        dps, state, ds = sync(dps, m_rs.state(), ds)
        m_rs.take(state)
        m_rs.fold(2)
        m_rs.cross(1)
        run_back(3)
        dps, state, ds, f_rs.end = sync(dps, m_rs.state(), ds, f_rs.end)
        m_rs.take(state)
        m_rs.close(2)
        m_rs.home(2)
        m_rs.fold(1)
        m_rs.cross(3)
        run_back(0)
        dps, m_rs.two, m_rs.near, far = sync(dps, m_rs.two, m_rs.near, {0: m_rs.far[0]})
        m_rs.far.update(far)
        m_rs.close(1)
        m_rs.home(1)
        m_rs.cross(0)
    else:
        for h in range(heads):
            run_back(h)
    output = settle(out_came)
    da, g_gain1 = input_back([dps[h] for h in range(heads)], m_parts, x)
    if fast:
        da, g_gain1, far, m_rs.near = sync(da, g_gain1, {3: m_rs.far[3]}, m_rs.near)
        m_rs.far.update(far)
        m_rs.fold(3)
    da_other = at.swap(da)
    d_x_norm = rms_back(x.astype(F32), gain1, da.astype(F32) + da_other.astype(F32))
    dx_home = give_back(d_mix.astype(F32) + d_x_norm)

    small = [jnp.sum(g_small[h], axis=0) for h in range(heads)]
    conv_all = sum(jnp.where(own[h][:, None, None], g_conv[h][None, :TAPS], 0.0) for h in range(heads)).reshape(-1, HD)
    decay_all = sum(jnp.where(own[h][:, None], small[h][None], 0.0) for h in range(heads))
    gains = jnp.concatenate([at.relative(g_gain1[0]), 0.5 * at.relative(g_gain2[0])]).reshape(-1, HD)
    sums = jnp.concatenate([conv_all, decay_all, gains, g_gain_o], axis=0)
    if fast:
        dx_home, sums, state = sync(dx_home, at.chip_sum(sums), m_rs.state())
        m_rs.take(state)
        m_rs.fold(0)
        m_rs.close(3)
        m_rs.home(3)
    else:
        sums = at.chip_sum(sums)
    sums = at.line_sum(sums)
    dx_came = lax.all_to_all(dx_home, "tp", split_axis=0, concat_axis=0, tiled=True)
    if fast:
        dx_came, sums, m_rs.two, m_rs.end = sync(dx_came, sums, m_rs.two, m_rs.end)
        m_rs.close(0)
    input_grad = settle(dx_came)
    n_conv = conv_all.shape[0]
    g_conv_all = jnp.transpose(sums[:n_conv].reshape(heads_all, TAPS, -1), (0, 2, 1))
    decay_sum = sums[n_conv : n_conv + heads_all]
    gain_sum = sums[n_conv + heads_all : -1].reshape(2, dim)

    def to_core(value, joined):
        mine, give = at.halves(value.astype(BF16), value.ndim - 1)
        return at.in_order(mine, at.swap(give), joined).astype(F32)

    if not fast:
        f_rs.rest()
    f_total = f_rs.total()
    g_ffn = to_core(f_total.reshape(3, -1, f_total.shape[1]), 1)
    grad_gate_up = jnp.transpose(g_ffn[:2], (2, 0, 1))
    grad_down = g_ffn[2]
    if by_turn:
        if not fast:
            m_rs.rest()
        joined = to_core(m_rs.total()[None], 0)
    else:
        joined = []
        for h in range(heads):
            have = {}
            for stack, group in zip((m_rs.near[h], m_rs.far[h]), sides(chips, first_bit(at, h))):
                have.update({p: stack[i] for i, p in enumerate(group)})
            joined.append(jnp.concatenate([have[p] for p in range(chips)], axis=1))
        joined = jnp.stack(joined)
        spread = jnp.zeros((heads_all,) + joined.shape[1:], BF16)
        spread = lax.dynamic_update_slice_in_dim(spread, at.relative(joined), at.core * heads, 0)
        spread = lax.psum_scatter(spread, "tp", scatter_dimension=0, tiled=True)
        joined = lax.psum_scatter(spread, "fsdp", scatter_dimension=2, tiled=True).astype(F32)
    grad_in = jnp.transpose(joined[:, HD : HD + cols], (2, 0, 1))
    grad_out = joined[:, :HD].reshape(local_heads * HD, -1)
    return (
        output, input_grad, gain_sum[0], grad_in, g_conv_all, decay_sum[:, 0], decay_sum[:, 1], sums[-1], grad_out,
        gain_sum[1], grad_gate_up, grad_down
    )


def solution(mesh):
    tokens = P("fsdp", "tp", None)
    rows = P("tp", "fsdp")
    split = P("fsdp", None, "tp")
    return jax.shard_map(
        local,
        mesh=mesh,
        in_specs=(tokens, P(), P(), tokens, P(), tokens, P(), P(), P(), P(), rows, P(), split, rows),
        out_specs=(tokens, tokens, P(), tokens, P(), P(), P(), P(), rows, P(), split, rows),
        check_vma=False,
    )
```

time: 2880 us -> 616 us (0.21)
  waiting for transfers between devices: 1160 us -> 165 us
  other arithmetic: 816 us -> 52.4 us
  matrix products: 569 us -> 0 us
  Pallas kernels: 0 us -> 262 us
  local copies, waits for them, and re-layouts: 238 us -> 30.7 us
  starting transfers between devices: 15.4 us -> 95.3 us
  blocking collectives: 49.7 us -> 0 us
    unnamed x22 -> x0, waiting for transfers between devices: 696 us -> none
    another operation x6 -> x9, other arithmetic: 644 us -> 0.78 us  [the longest x1 0.64 us: local(): jnp.stack([jnp.sum(jnp.where(own, jnp.exp(decay_log)[None], 0.0), axis=1)...]
    dot_general x127 -> x0, matrix products: 526 us -> none  [the longest x48 98.7 us: carry_step(): jnp.einsum('shid,shdv->shiv', key_block, state, precision=PRECISION_MAX)]
    all_gather x7 -> x0, waiting for transfers between devices: 328 us -> none  [the longest x2 151 us: spread(): return lax.all_gather(value, 'tp', axis=1, tiled=True)]
    pallas_call x0 -> x25, Pallas kernels: none -> 262 us  [the longest x4 54.9 us: project_back(): pl.pallas_call(functools.partial(project_back_kernel, pieces, bit, h), ou...]
    ppermute x0 -> x76, waiting for transfers between devices: none -> 158 us  [the longest x44 77.7 us: move(): lax.ppermute(value, 'fsdp', [(i, i ^ 2 * bit) for i in range(self.n_f)])]
    ppermute x0 -> x76, starting transfers between devices: none -> 81.2 us  [the longest x44 48.9 us: move(): lax.ppermute(value, 'fsdp', [(i, i ^ 2 * bit) for i in range(self.n_f)])]
    psum x1 -> x0, waiting for transfers between devices: 71.1 us -> none  [local(): lax.psum((grad_gain_one, grad_gain_two, conv_full, log_full, bias_full, g...]
  transfers between devices with their start and end apart: 18 -> 80, of which waited for: 15 -> 30; matrix products, arithmetic and copies ran while one was open for 7% -> 10% of each run, Pallas kernels for 0% -> 41%
where the time goes in v1:
time: 616 us; the launch traced here: 609 us
  Pallas kernels  262 us (43%)
  waiting for transfers between devices  165 us (27%)
  starting transfers between devices  95.3 us (15%)
  other arithmetic  52.4 us (9%)
  local copies, waits for them, and re-layouts  30.7 us (5%)
    ppermute x44, waiting for transfers between devices, move(): lax.ppermute(value, 'fsdp', [(i, i ^ 2 * bit) for i in range(self.n_f)])  77.7 us
    ppermute x15, waiting for transfers between devices, turn(): lax.ppermute(value, 'tp', [(i, (i + r) % self.n_t) for i in range(self.n_...  73.1 us
    pallas_call x4, Pallas kernels, project_back(): pl.pallas_call(functools.partial(project_back_kernel, pieces, bit, h), ou...  54.9 us
    ppermute x44, starting transfers between devices, move(): lax.ppermute(value, 'fsdp', [(i, i ^ 2 * bit) for i in range(self.n_f)])  48.9 us
    pallas_call x2, Pallas kernels, ffn(): pl.pallas_call(functools.partial(ffn_kernel, pieces, chunks, bits, bool(m...  45.2 us
    pallas_call x2, Pallas kernels, recur_back(): pl.pallas_call(functools.partial(recur_back_kernel, heads, len(done)), ou...  41.5 us
    pallas_call x4, Pallas kernels, project(): pl.pallas_call(functools.partial(project_kernel, pieces, h), out_shape=[j...  32.3 us
    pallas_call x2, Pallas kernels, recur(): pl.pallas_call(functools.partial(recur_kernel, heads, len(more)), out_sha...  28.8 us
  transfers between devices with their start and end apart: 80, of which 30 were waited for; matrix products, arithmetic and copies ran while one was open for 10% of the time, Pallas kernels for 41%

profile of v1, /device:TPU:0, one launch (start us, length us, event | category | flops | bytes accessed | tf_op | source)
XLA Modules:
  0.0 609.0 jit_solution(13611960204657675136)
XLA Ops:
  25.7 9.3 %collective-permute-done.2.refs_2_.refs_6_ = bf16[912,256]{1,0:T(8,128)(2,1)S(1)} collective-permute-done((bf16[912,256]{1,0:T(8,128)(2,1)S(1)}, bf16[912,256]{1,0:T(8,128)(2,1)S(1)}, u32[]{:S(2)}, u32[]{:S(2)}) %collective-permute-start.2) | collective-permute-done | bytes 466976 | tf_op jit(solution)/shard_map/ppermute | solution.py:966
  35.1 8.1 %collective-permute-done.5.refs_0_.refs_12_.refs_16_ = bf16[912,256]{1,0:T(8,128)(2,1)S(1)} collective-permute-done((bf16[912,256]{1,0:T(8,128)(2,1)S(1)}, bf16[912,256]{1,0:T(8,128)(2,1)S(1)}, u32[]{:S(2)}, u32[]{:S(2)}) %collective-permute-start.5) | collective-permute-done | bytes 466976 | tf_op jit(solution)/shard_map/ppermute | solution.py:969
  52.7 7.7 %collective-permute-done.10.refs_2_.refs_6_.refs_10_ = bf16[912,256]{1,0:T(8,128)(2,1)} collective-permute-done((bf16[912,256]{1,0:T(8,128)(2,1)S(1)}, bf16[912,256]{1,0:T(8,128)(2,1)}, u32[]{:S(2)}, u32[]{:S(2)}) %collective-permute-start.10) | collective-permute-done | bytes 466976 | tf_op jit(solution)/shard_map/ppermute | solution.py:966
  60.4 18.0 %collective-permute-done.11.refs_0_.refs_8_.refs_12_ = bf16[912,256]{1,0:T(8,128)(2,1)} collective-permute-done((bf16[912,256]{1,0:T(8,128)(2,1)S(1)}, bf16[912,256]{1,0:T(8,128)(2,1)}, u32[]{:S(2)}, u32[]{:S(2)}) %collective-permute-start.11) | collective-permute-done | bytes 466976 | tf_op jit(solution)/shard_map/ppermute | solution.py:969
  90.6 8.1 %project.4 = (bf16[1024,640]{1,0:T(8,128)(2,1)}, bf16[1024,128]{1,0:T(8,128)(2,1)}, bf16[1024,128]{1,0:T(8,128)(2,1)}, bf16[2048,128]{1,0:T(8,128)(2,1)}, bf16[2...) custom-call(f32[4,2]{1,0:T(4,128)} %pad_maximum_fusion.10.scal_ref, bf16[1024,1024]{1,0:T(8,128)(2,1)} %fusion.9.a_ref, ...), custom_call_target="tpu_custom_call" | custom-call | flops 1644167168 | bytes 8000000 | tf_op jit(solution)/shard_map/project/pallas_call | solution.py:172
  98.7 7.5 %collective-permute-done.14.refs_3_.refs_7_.refs_11_ = bf16[912,256]{1,0:T(8,128)(2,1)S(1)} collective-permute-done((bf16[912,256]{1,0:T(8,128)(2,1)}, bf16[912,256]{1,0:T(8,128)(2,1)S(1)}, u32[]{:S(2)}, u32[]{:S(2)}) %collective-permute-start.14) | collective-permute-done | bytes 466976 | tf_op jit(solution)/shard_map/ppermute | solution.py:966
  113.3 8.3 %project.6 = (bf16[1024,640]{1,0:T(8,128)(2,1)}, bf16[1024,128]{1,0:T(8,128)(2,1)}, bf16[1024,128]{1,0:T(8,128)(2,1)}, bf16[2048,128]{1,0:T(8,128)(2,1)}, bf16[2...) custom-call(f32[4,2]{1,0:T(4,128)} %pad_maximum_fusion.10.scal_ref, bf16[1024,1024]{1,0:T(8,128)(2,1)} %fusion.9.a_ref, ...), custom_call_target="tpu_custom_call" | custom-call | flops 1644167168 | bytes 8000000 | tf_op jit(solution)/shard_map/project/pallas_call | solution.py:172
  121.6 8.0 %project.5 = (bf16[1024,640]{1,0:T(8,128)(2,1)}, bf16[1024,128]{1,0:T(8,128)(2,1)}, bf16[1024,128]{1,0:T(8,128)(2,1)}, bf16[2048,128]{1,0:T(8,128)(2,1)}, bf16[2...) custom-call(f32[4,2]{1,0:T(4,128)} %pad_maximum_fusion.10.scal_ref, bf16[1024,1024]{1,0:T(8,128)(2,1)} %fusion.9.a_ref, ...), custom_call_target="tpu_custom_call" | custom-call | flops 1644167168 | bytes 8000000 | tf_op jit(solution)/shard_map/project/pallas_call | solution.py:172
  137.9 8.0 %project.7 = (bf16[1024,640]{1,0:T(8,128)(2,1)}, bf16[1024,128]{1,0:T(8,128)(2,1)}, bf16[1024,128]{1,0:T(8,128)(2,1)}, bf16[2048,128]{1,0:T(8,128)(2,1)}, bf16[2...) custom-call(f32[4,2]{1,0:T(4,128)} %pad_maximum_fusion.10.scal_ref, bf16[1024,1024]{1,0:T(8,128)(2,1)} %fusion.9.a_ref, ...), custom_call_target="tpu_custom_call" | custom-call | flops 1644167168 | bytes 8000000 | tf_op jit(solution)/shard_map/project/pallas_call | solution.py:172
  161.6 14.4 %recur.2 = (bf16[1024,512]{1,0:T(8,128)(2,1)}, f32[4,128,128]{2,1,0:T(8,128)}, bf16[512,128]{1,0:T(8,128)(2,1)}, bf16[512,128]{1,0:T(8,128)(2,1)}, bf16[512,128]...) custom-call(f32[1,128]{1,0:T(1,128)} %bitcast.110, ...), custom_call_target="tpu_custom_call" | custom-call | flops 2688000000 | bytes 1000000 | tf_op jit(solution)/shard_map/recur/pallas_call | solution.py:346
  176.1 5.8 collective-permute-done.28.refs_2_
  196.6 14.4 %recur.3 = (bf16[1024,512]{1,0:T(8,128)(2,1)}, f32[4,128,128]{2,1,0:T(8,128)}, bf16[512,128]{1,0:T(8,128)(2,1)}, bf16[512,128]{1,0:T(8,128)(2,1)}, bf16[512,128]...) custom-call(f32[1,128]{1,0:T(1,128)} %bitcast.111, ...), custom_call_target="tpu_custom_call", output_to_operand_aliasing={{0}: (22, {})} | custom-call | flops 2688000000 | bytes 1000000 | tf_op jit(solution)/shard_map/recur/pallas_call | solution.py:346
  211.0 11.1 %collective-permute-done.32.refs_4_ = bf16[1056,256]{1,0:T(8,128)(2,1)S(1)} collective-permute-done((bf16[1056,256]{1,0:T(8,128)(2,1)}, bf16[1056,256]{1,0:T(8,128)(2,1)S(1)}, u32[]{:S(2)}, u32[]{:S(2)}) %collective-permute-start.32) | collective-permute-done | bytes 540704 | tf_op jit(solution)/shard_map/ppermute | solution.py:969
  226.8 4.7 mix_out.1
  251.2 21.8 %ffn.2 = (f32[1024,1024]{1,0:T(8,128)}, f32[1024,1024]{1,0:T(8,128)}, bf16[2,1056,256]{2,1,0:T(8,128)(2,1)}, bf16[2,1056,256]{2,1,0:T(8,128)(2,1)}, bf16[2,1056,...) custom-call(bf16[1024,1024]{1,0:T(8,128)(2,1)} %multiply_convert_fusion.1.b_ref, ...), custom_call_target="tpu_custom_call" | custom-call | flops 13287555072 | bytes 1000000 | tf_op jit(solution)/shard_map/ffn/pallas_call | solution.py:928
  274.4 10.1 %collective-permute-done.40.refs_3_ = bf16[1056,256]{1,0:T(8,128)(2,1)S(1)} collective-permute-done((bf16[1056,256]{1,0:T(8,128)(2,1)}, bf16[1056,256]{1,0:T(8,128)(2,1)S(1)}, u32[]{:S(2)}, u32[]{:S(2)}) %collective-permute-start.40) | collective-permute-done | bytes 540704 | tf_op jit(solution)/shard_map/ppermute | solution.py:966
  287.4 23.4 %ffn.3 = (bf16[1024,1024]{1,0:T(8,128)(2,1)}, bf16[1024,1024]{1,0:T(8,128)(2,1)}, bf16[2,1056,256]{2,1,0:T(8,128)(2,1)}, bf16[2,1056,256]{2,1,0:T(8,128)(2,1)}, ...) custom-call(bf16[1024,1024]{1,0:T(8,128)(2,1)} %multiply_convert_fusion.1.b_ref, ...), custom_call_target="tpu_custom_call" | custom-call | flops 13287555072 | bytes 1000000 | tf_op jit(solution)/shard_map/ffn/pallas_call | solution.py:928
  320.1 10.3 %mix_back.1 = (bf16[1024,1024]{1,0:T(8,128)(2,1)}, bf16[1024,512]{1,0:T(8,128)(2,1)}, f32[1,1024]{1,0:T(1,128)}, bf16[128,256]{1,0:T(8,128)(2,1)}, bf16[128,256]...) custom-call(f32[1,1024]{1,0:T(1,128)} %bitcast.97, ...), custom_call_target="tpu_custom_call" | custom-call | flops 2147483648 | bytes 1000000 | tf_op jit(solution)/shard_map/mix_back/pallas_call | solution.py:797
  333.6 20.8 %recur_back.2 = (bf16[1024,768]{1,0:T(8,128)(2,1)}, bf16[1024,768]{1,0:T(8,128)(2,1)}, bf16[1024,768]{1,0:T(8,128)(2,1)}, bf16[1024,768]{1,0:T(8,128)(2,1)}, f32...) custom-call(f32[1,128]{1,0:T(1,128)} %bitcast.112, ...), custom_call_target="tpu_custom_call" | custom-call | flops 4032000000 | bytes 1000000 | tf_op jit(solution)/shard_map/recur_back/pallas_call | solution.py:505
  354.4 4.7 collective-permute-done.46.refs_3_
  373.8 20.7 %recur_back.3 = (bf16[1024,768]{1,0:T(8,128)(2,1)}, bf16[1024,768]{1,0:T(8,128)(2,1)}, bf16[1024,768]{1,0:T(8,128)(2,1)}, bf16[1024,768]{1,0:T(8,128)(2,1)}, f32...) custom-call(f32[1,128]{1,0:T(1,128)} %bitcast.113, ...), custom_call_target="tpu_custom_call", output_to_operand_aliasing={{0}: (33, {}), {1}: (34, {}), {2}: (35, {}), {3}: (36, {}),... | custom-call | flops 4032000000 | bytes 1000000 | tf_op jit(solution)/shard_map/recur_back/pallas_call | solution.py:505
  402.2 13.8 %project_back.4 = (bf16[1024,784]{1,0:T(8,128)(2,1)}, f32[8,640]{1,0:T(8,128)}, f32[8,128]{1,0:T(8,128)}, bf16[2,912,256]{2,1,0:T(8,128)(2,1)}, bf16[2,912,256]{2,1,0:T(8,128)(2,1)}) custom-call(f32[4,2]{1,0:T(4,128)} %pad_maximum_fusion.10.scal_ref, bf16[1024,1024]{1,0:T(8,128)(2,1)} %fusion.9.a_ref, f32[4,8,640]{2,1,0:T(8,128)} %select_reduce_fusion.cw_ref, ...), custom_call_target="tpu_custom_call" | custom-call | flops 1644167168 | bytes 1000000 | tf_op jit(solution)/shard_map/project_back/pallas_call | solution.py:639
  416.0 7.3 %collective-permute-done.52 = bf16[1056,256]{1,0:T(8,128)(2,1)S(1)} collective-permute-done((bf16[1056,256]{1,0:T(8,128)(2,1)S(1)}, bf16[1056,256]{1,0:T(8,128)(2,1)S(1)}, u32[]{:S(2)}, u32[]{:S(2)}) %collective-permute-start.52) | collective-permute-done | bytes 540704 | tf_op jit(solution)/shard_map/ppermute | solution.py:969
  425.7 13.7 %project_back.5 = (bf16[1024,784]{1,0:T(8,128)(2,1)}, f32[8,640]{1,0:T(8,128)}, f32[8,128]{1,0:T(8,128)}, bf16[2,912,256]{2,1,0:T(8,128)(2,1)}, bf16[2,912,256]{2,1,0:T(8,128)(2,1)}) custom-call(f32[4,2]{1,0:T(4,128)} %pad_maximum_fusion.10.scal_ref, bf16[1024,1024]{1,0:T(8,128)(2,1)} %fusion.9.a_ref, f32[4,8,640]{2,1,0:T(8,128)} %select_reduce_fusion.cw_ref, ...), custom_call_target="tpu_custom_call" | custom-call | flops 1644167168 | bytes 1000000 | tf_op jit(solution)/shard_map/project_back/pallas_call | solution.py:639
  439.5 7.4 %collective-permute-done.54.refs_1_ = bf16[2,912,256]{2,1,0:T(8,128)(2,1)S(1)} collective-permute-done((bf16[2,912,256]{2,1,0:T(8,128)(2,1)}, bf16[2,912,256]{2,1,0:T(8,128)(2,1)S(1)}, u32[]{:S(2)}, u32[]{:S(2)}) %collective-permute-start.54) | collective-permute-done | bytes 933920 | tf_op jit(solution)/shard_map/ppermute | solution.py:966
  460.4 13.7 %project_back.6 = (bf16[1024,784]{1,0:T(8,128)(2,1)}, f32[8,640]{1,0:T(8,128)}, f32[8,128]{1,0:T(8,128)}, bf16[2,912,256]{2,1,0:T(8,128)(2,1)}, bf16[2,912,256]{2,1,0:T(8,128)(2,1)}) custom-call(f32[4,2]{1,0:T(4,128)} %pad_maximum_fusion.10.scal_ref, bf16[1024,1024]{1,0:T(8,128)(2,1)} %fusion.9.a_ref, f32[4,8,640]{2,1,0:T(8,128)} %select_reduce_fusion.cw_ref, ...), custom_call_target="tpu_custom_call" | custom-call | flops 1644167168 | bytes 1000000 | tf_op jit(solution)/shard_map/project_back/pallas_call | solution.py:639
  487.2 13.7 %project_back.7 = (bf16[1024,784]{1,0:T(8,128)(2,1)}, f32[8,640]{1,0:T(8,128)}, f32[8,128]{1,0:T(8,128)}, bf16[2,912,256]{2,1,0:T(8,128)(2,1)}, bf16[2,912,256]{2,1,0:T(8,128)(2,1)}) custom-call(f32[4,2]{1,0:T(4,128)} %pad_maximum_fusion.10.scal_ref, bf16[1024,1024]{1,0:T(8,128)(2,1)} %fusion.9.a_ref, f32[4,8,640]{2,1,0:T(8,128)} %select_reduce_fusion.cw_ref, ...), custom_call_target="tpu_custom_call" | custom-call | flops 1644167168 | bytes 1000000 | tf_op jit(solution)/shard_map/project_back/pallas_call | solution.py:639
  504.1 13.4 %input_back.1 = (bf16[1024,1024]{1,0:T(8,128)(2,1)}, f32[1,1024]{1,0:T(1,128)}) custom-call(bf16[1024,784]{1,0:T(8,128)(2,1)} %get-tuple-element.900.refs_0_, bf16[1024,784]{1,0:T(8,128)(2,1)} %get-tuple-element.901.refs_1_, bf16[1024,784]{1,0:T(8,128)(2,1)} %get-tuple-element.902.refs_2_, bf16[1024,784]{1,0:T(8,128)(2,1)} %get-tuple-element.903.refs_3_, ...), custom_call_target="tpu_custom_call" | custom-call | flops 6576668672 | bytes 1000000 | tf_op jit(solution)/shard_map/input_back/pallas_call | solution.py:705
  541.7 5.2 collective-permute-done.65
  546.9 8.7 %collective-permute-done.64.refs_1_ = bf16[2,912,256]{2,1,0:T(8,128)(2,1)} collective-permute-done((bf16[2,912,256]{2,1,0:T(8,128)(2,1)}, bf16[2,912,256]{2,1,0:T(8,128)(2,1)}, u32[]{:S(2)}, u32[]{:S(2)}) %collective-permute-start.64) | collective-permute-done | bytes 933920 | tf_op jit(solution)/shard_map/ppermute | solution.py:966
  576.0 16.6 %collective-permute-done.68 = f32[185,128]{1,0:T(8,128)S(1)} collective-permute-done((f32[185,128]{1,0:T(8,128)S(1)}, f32[185,128]{1,0:T(8,128)S(1)}, u32[]{:S(2)}, u32[]{:S(2)}) %collective-permute-start.68) | collective-permute-done | bytes 94752 | tf_op jit(solution)/shard_map/ppermute | solution.py:969
  592.6 7.8 %collective-permute-done.69 = f32[185,128]{1,0:T(8,128)S(1)} collective-permute-done((f32[185,128]{1,0:T(8,128)S(1)}, f32[185,128]{1,0:T(8,128)S(1)}, u32[]{:S(2)}, u32[]{:S(2)}) %collective-permute-start.69) | collective-permute-done | bytes 94752 | tf_op jit(solution)/shard_map/ppermute | solution.py:969
  (480 shorter events, 239.1 us)
Async XLA Ops:
  43.1 39.7 %all-to-all-start = ((bf16[4,256,512]{2,1,0:T(8,128)(2,1)}), bf16[4,256,512]{2,1,0:T(8,128)(2,1)S(1)}, u32[]{:S(2)}, u32[]{:S(2)}) async-start(bf16[4,256,512]{2,1,0:T(8,128)(2,1)} %pad_maximum_fusion.1), calls=%async_computation | async-start | bytes 2097152 | tf_op jit(solution)/shard_map/all_to_all | solution.py:993
  48.2 30.1 %collective-permute-start.11 = (bf16[912,256]{1,0:T(8,128)(2,1)S(1)}, bf16[912,256]{1,0:T(8,128)(2,1)}, u32[]{:S(2)}, u32[]{:S(2)}) collective-permute-start(bf16[912,256]{1,0:T(8,128)(2,1)S(1)} %collective-permute-done.4.refs_0_.refs_4_.refs_8_), channel_id=1, source_target_pairs={{0,1},{1,2},{2,3},{3,0},{4,5},{5,6},{6,7},{7,4},{8,9},{9,10},{10,1... | collective-permute-start | bytes 1400840 | tf_op jit(solution)/shard_map/ppermute | solution.py:969
  50.1 28.2 %collective-permute-start.12 = (bf16[912,256]{1,0:T(8,128)(2,1)S(1)}, bf16[912,256]{1,0:T(8,128)(2,1)S(1)}, u32[]{:S(2)}, u32[]{:S(2)}) collective-permute-start(bf16[912,256]{1,0:T(8,128)(2,1)S(1)} %collective-permute-done.5.refs_0_.refs_12_.refs_16_), channel_id=1, source_target_pairs={{0,8},{4,12},{8,0},{12,4},{16,24},{20,28},{24,16},{28,20},{1,9},{5... | collective-permute-start | bytes 1400840 | tf_op jit(solution)/shard_map/ppermute | solution.py:966
  51.6 26.7 %collective-permute-start.13 = (bf16[912,256]{1,0:T(8,128)(2,1)S(1)}, bf16[912,256]{1,0:T(8,128)(2,1)S(1)}, u32[]{:S(2)}, u32[]{:S(2)}) collective-permute-start(bf16[912,256]{1,0:T(8,128)(2,1)S(1)} %collective-permute-done.5.refs_0_.refs_12_.refs_16_), channel_id=1, source_target_pairs={{0,16},{4,20},{8,24},{12,28},{16,0},{20,4},{24,8},{28,12},{1,17},{... | collective-permute-start | bytes 1400840 | tf_op jit(solution)/shard_map/ppermute | solution.py:966
  52.1 27.8 %collective-permute-start.9 = (bf16[912,256]{1,0:T(8,128)(2,1)S(1)}, bf16[912,256]{1,0:T(8,128)(2,1)}, u32[]{:S(2)}, u32[]{:S(2)}) collective-permute-start(bf16[912,256]{1,0:T(8,128)(2,1)S(1)} %collective-permute-done.4.refs_0_.refs_4_.refs_8_), channel_id=1, source_target_pairs={{0,8},{4,12},{8,0},{12,4},{16,24},{20,28},{24,16},{28,20},{1,9},{5... | collective-permute-start | bytes 1400840 | tf_op jit(solution)/shard_map/ppermute | solution.py:966
  82.8 46.8 %collective-permute-start.17 = (bf16[912,256]{1,0:T(8,128)(2,1)}, bf16[912,256]{1,0:T(8,128)(2,1)S(1)}, u32[]{:S(2)}, u32[]{:S(2)}) collective-permute-start(bf16[912,256]{1,0:T(8,128)(2,1)} %collective-permute-done.11.refs_0_.refs_8_.refs_12_), channel_id=1, source_target_pairs={{0,8},{4,12},{8,0},{12,4},{16,24},{20,28},{24,16},{28,20},{1,9},{5... | collective-permute-start | bytes 1400840 | tf_op jit(solution)/shard_map/ppermute | solution.py:966
  84.3 45.3 %collective-permute-start.18 = (bf16[912,256]{1,0:T(8,128)(2,1)}, bf16[912,256]{1,0:T(8,128)(2,1)S(1)}, u32[]{:S(2)}, u32[]{:S(2)}) collective-permute-start(bf16[912,256]{1,0:T(8,128)(2,1)} %collective-permute-done.11.refs_0_.refs_8_.refs_12_), channel_id=1, source_target_pairs={{0,16},{4,20},{8,24},{12,28},{16,0},{20,4},{24,8},{28,12},{1,17},{... | collective-permute-start | bytes 1400840 | tf_op jit(solution)/shard_map/ppermute | solution.py:966
  107.6 26.2 %collective-permute-start.21 = (bf16[1056,256]{1,0:T(8,128)(2,1)S(1)}, bf16[1056,256]{1,0:T(8,128)(2,1)S(1)}, u32[]{:S(2)}, u32[]{:S(2)}) collective-permute-start(bf16[1056,256]{1,0:T(8,128)(2,1)S(1)} %bitcast.90), channel_id=1, source_target_pairs={{0,3},{1,0},{2,1},{3,2},{4,7},{5,4},{6,5},{7,6},{8,11},{9,8},{10,9... | collective-permute-start | bytes 1622024 | tf_op jit(solution)/shard_map/ppermute | solution.py:969
  137.3 38.7 %collective-permute-start.25 = (bf16[1056,256]{1,0:T(8,128)(2,1)S(1)}, bf16[1056,256]{1,0:T(8,128)(2,1)}, u32[]{:S(2)}, u32[]{:S(2)}) collective-permute-start(bf16[1056,256]{1,0:T(8,128)(2,1)S(1)} %bitcast.92), channel_id=1, source_target_pairs={{0,16},{4,20},{8,24},{12,28},{16,0},{20,4},{24,8},{28,12},{1,17},{... | collective-permute-start | bytes 1622024 | tf_op jit(solution)/shard_map/ppermute | solution.py:966
  149.3 32.5 %collective-permute-start.26 = (bf16[1056,256]{1,0:T(8,128)(2,1)}, bf16[1056,256]{1,0:T(8,128)(2,1)S(1)}, u32[]{:S(2)}, u32[]{:S(2)}) collective-permute-start(bf16[1056,256]{1,0:T(8,128)(2,1)} %collective-permute-done.20.refs_4_), channel_id=1, source_target_pairs={{0,8},{4,12},{8,0},{12,4},{16,24},{20,28},{24,16},{28,20},{1,9},{5... | collective-permute-start | bytes 1622024 | tf_op jit(solution)/shard_map/ppermute | solution.py:966
  150.7 31.2 %collective-permute-start.27 = (bf16[1056,256]{1,0:T(8,128)(2,1)}, bf16[1056,256]{1,0:T(8,128)(2,1)}, u32[]{:S(2)}, u32[]{:S(2)}) collective-permute-start(bf16[1056,256]{1,0:T(8,128)(2,1)} %collective-permute-done.20.refs_4_), channel_id=1, source_target_pairs={{0,16},{4,20},{8,24},{12,28},{16,0},{20,4},{24,8},{28,12},{1,17},{... | collective-permute-start | bytes 1622024 | tf_op jit(solution)/shard_map/ppermute | solution.py:966
  187.4 39.4 %all-to-all-start.1 = ((bf16[4,256,512]{2,1,0:T(8,128)(2,1)}), bf16[4,256,512]{2,1,0:T(8,128)(2,1)S(1)}, u32[]{:S(2)}, u32[]{:S(2)}) async-start(bf16[4,256,512]{2,1,0:T(8,128)(2,1)} %select_blocks.3), calls=%async_computation.1 | async-start | bytes 2097152 | tf_op jit(solution)/shard_map/all_to_all | solution.py:993
  193.8 28.3 %collective-permute-start.32 = (bf16[1056,256]{1,0:T(8,128)(2,1)}, bf16[1056,256]{1,0:T(8,128)(2,1)S(1)}, u32[]{:S(2)}, u32[]{:S(2)}) collective-permute-start(bf16[1056,256]{1,0:T(8,128)(2,1)} %collective-permute-done.20.refs_4_), channel_id=1, source_target_pairs={{0,1},{1,2},{2,3},{3,0},{4,5},{5,6},{6,7},{7,4},{8,9},{9,10},{10,1... | collective-permute-start | bytes 1622024 | tf_op jit(solution)/shard_map/ppermute | solution.py:969
  195.9 27.1 %collective-permute-start.33 = (bf16[1056,256]{1,0:T(8,128)(2,1)}, bf16[1056,256]{1,0:T(8,128)(2,1)}, u32[]{:S(2)}, u32[]{:S(2)}) collective-permute-start(bf16[1056,256]{1,0:T(8,128)(2,1)} %copy-done.85), channel_id=1, source_target_pairs={{0,8},{4,12},{8,0},{12,4},{16,24},{20,28},{24,16},{28,20},{1,9},{5... | collective-permute-start | bytes 1622024 | tf_op jit(solution)/shard_map/ppermute | solution.py:966
  247.6 25.4 %collective-permute-start.38 = (bf16[1056,256]{1,0:T(8,128)(2,1)S(1)}, bf16[1056,256]{1,0:T(8,128)(2,1)S(1)}, u32[]{:S(2)}, u32[]{:S(2)}) collective-permute-start(bf16[1056,256]{1,0:T(8,128)(2,1)S(1)} %copy-done.89), channel_id=1, source_target_pairs={{0,16},{4,20},{8,24},{12,28},{16,0},{20,4},{24,8},{28,12},{1,17},{... | collective-permute-start | bytes 1622024 | tf_op jit(solution)/shard_map/ppermute | solution.py:966
  249.2 25.3 %collective-permute-start.39 = (bf16[1056,256]{1,0:T(8,128)(2,1)S(1)}, bf16[1056,256]{1,0:T(8,128)(2,1)S(1)}, u32[]{:S(2)}, u32[]{:S(2)}) collective-permute-start(bf16[1056,256]{1,0:T(8,128)(2,1)S(1)} %collective-permute-done.36.refs_5_), channel_id=1, source_target_pairs={{0,16},{4,20},{8,24},{12,28},{16,0},{20,4},{24,8},{28,12},{1,17},{... | collective-permute-start | bytes 1622024 | tf_op jit(solution)/shard_map/ppermute | solution.py:966
  249.7 34.9 %collective-permute-start.40 = (bf16[1056,256]{1,0:T(8,128)(2,1)}, bf16[1056,256]{1,0:T(8,128)(2,1)S(1)}, u32[]{:S(2)}, u32[]{:S(2)}) collective-permute-start(bf16[1056,256]{1,0:T(8,128)(2,1)} %collective-permute-done.33.refs_1_), channel_id=1, source_target_pairs={{0,16},{4,20},{8,24},{12,28},{16,0},{20,4},{24,8},{28,12},{1,17},{... | collective-permute-start | bytes 1622024 | tf_op jit(solution)/shard_map/ppermute | solution.py:966
  284.6 26.2 %collective-permute-start.41 = (bf16[2,1056,256]{2,1,0:T(8,128)(2,1)}, bf16[2,1056,256]{2,1,0:T(8,128)(2,1)S(1)}, u32[]{:S(2)}, u32[]{:S(2)}) collective-permute-start(bf16[2,1056,256]{2,1,0:T(8,128)(2,1)} %get-tuple-element.723), channel_id=1, source_target_pairs={{0,16},{4,20},{8,24},{12,28},{16,0},{20,4},{24,8},{28,12},{1,17},{... | collective-permute-start | bytes 3244040 | tf_op jit(solution)/shard_map/ppermute | solution.py:966
  332.6 26.8 %collective-permute-start.48 = (bf16[1024,1024]{1,0:T(8,128)(2,1)S(1)}, bf16[1024,1024]{1,0:T(8,128)(2,1)}, u32[]{:S(2)}, u32[]{:S(2)}) collective-permute-start(bf16[1024,1024]{1,0:T(8,128)(2,1)S(1)} %copy-done.12), channel_id=1, source_target_pairs={{0,4},{4,0},{8,12},{12,8},{16,20},{20,16},{24,28},{28,24},{1,5},{5... | collective-permute-start | bytes 6291464 | tf_op jit(solution)/shard_map/ppermute | solution.py:963
  332.6 26.5 %collective-permute-start.46 = (bf16[2,1056,256]{2,1,0:T(8,128)(2,1)}, bf16[2,1056,256]{2,1,0:T(8,128)(2,1)S(1)}, u32[]{:S(2)}, u32[]{:S(2)}) collective-permute-start(bf16[2,1056,256]{2,1,0:T(8,128)(2,1)} %get-tuple-element.776), channel_id=1, source_target_pairs={{0,8},{4,12},{8,0},{12,4},{16,24},{20,28},{24,16},{28,20},{1,9},{5... | collective-permute-start | bytes 3244040 | tf_op jit(solution)/shard_map/ppermute | solution.py:966
  333.1 26.3 %collective-permute-start.47 = (bf16[2,1056,256]{2,1,0:T(8,128)(2,1)}, bf16[2,1056,256]{2,1,0:T(8,128)(2,1)}, u32[]{:S(2)}, u32[]{:S(2)}) collective-permute-start(bf16[2,1056,256]{2,1,0:T(8,128)(2,1)} %get-tuple-element.777), channel_id=1, source_target_pairs={{0,16},{4,20},{8,24},{12,28},{16,0},{20,4},{24,8},{28,12},{1,17},{... | collective-permute-start | bytes 3244040 | tf_op jit(solution)/shard_map/ppermute | solution.py:966
  363.8 31.7 %all-to-all-start.2 = ((bf16[4,256,512]{2,1,0:T(8,128)(2,1)}), bf16[4,256,512]{2,1,0:T(8,128)(2,1)S(1)}, u32[]{:S(2)}, u32[]{:S(2)}) async-start(bf16[4,256,512]{2,1,0:T(8,128)(2,1)} %bitcast.23), calls=%async_computation.2 | async-start | bytes 2097152 | tf_op jit(solution)/shard_map/all_to_all | solution.py:1380
  447.9 28.8 %collective-permute-start.55 = (bf16[2,912,256]{2,1,0:T(8,128)(2,1)}, bf16[2,912,256]{2,1,0:T(8,128)(2,1)S(1)}, u32[]{:S(2)}, u32[]{:S(2)}) collective-permute-start(bf16[2,912,256]{2,1,0:T(8,128)(2,1)} %get-tuple-element.873), channel_id=1, source_target_pairs={{0,8},{4,12},{8,0},{12,4},{16,24},{20,28},{24,16},{28,20},{1,9},{5... | collective-permute-start | bytes 2801672 | tf_op jit(solution)/shard_map/ppermute | solution.py:966
  449.8 26.9 %collective-permute-start.57 = (bf16[1056,256]{1,0:T(8,128)(2,1)}, bf16[1056,256]{1,0:T(8,128)(2,1)S(1)}, u32[]{:S(2)}, u32[]{:S(2)}) collective-permute-start(bf16[1056,256]{1,0:T(8,128)(2,1)} %add_convert_fusion.1), channel_id=1, source_target_pairs={{0,3},{1,0},{2,1},{3,2},{4,7},{5,4},{6,5},{7,6},{8,11},{9,8},{10,9... | collective-permute-start | bytes 1622024 | tf_op jit(solution)/shard_map/ppermute | solution.py:969
  457.9 101.2 %collective-permute-start.51 = (bf16[2,256,512]{2,1,0:T(8,128)(2,1)}, bf16[2,256,512]{2,1,0:T(8,128)(2,1)}, u32[]{:S(2)}, u32[]{:S(2)}) collective-permute-start(bf16[2,256,512]{2,1,0:T(8,128)(2,1)} %constant_dynamic-slice_fusion.14), channel_id=1, source_target_pairs={{0,4},{4,0},{8,12},{12,8},{16,20},{20,16},{24,28},{28,24},{1,5},{5... | collective-permute-start | bytes 1572872 | tf_op jit(solution)/shard_map/ppermute | solution.py:963
  483.5 58.2 %collective-permute-start.67 = (bf16[912,256]{1,0:T(8,128)(2,1)}, bf16[912,256]{1,0:T(8,128)(2,1)}, u32[]{:S(2)}, u32[]{:S(2)}) collective-permute-start(bf16[912,256]{1,0:T(8,128)(2,1)} %add_convert_fusion.9), channel_id=1, source_target_pairs={{0,2},{1,3},{2,0},{3,1},{4,6},{5,7},{6,4},{7,5},{8,10},{9,11},{10,... | collective-permute-start | bytes 1400840 | tf_op jit(solution)/shard_map/ppermute | solution.py:969
  485.6 31.9 %collective-permute-start.59 = (bf16[2,912,256]{2,1,0:T(8,128)(2,1)}, bf16[2,912,256]{2,1,0:T(8,128)(2,1)S(1)}, u32[]{:S(2)}, u32[]{:S(2)}) collective-permute-start(bf16[2,912,256]{2,1,0:T(8,128)(2,1)} %get-tuple-element.906), channel_id=1, source_target_pairs={{0,16},{4,20},{8,24},{12,28},{16,0},{20,4},{24,8},{28,12},{1,17},{... | collective-permute-start | bytes 2801672 | tf_op jit(solution)/shard_map/ppermute | solution.py:966
  555.6 44.9 %all-to-all-start.3 = ((bf16[4,256,512]{2,1,0:T(8,128)(2,1)}), bf16[4,256,512]{2,1,0:T(8,128)(2,1)S(1)}, u32[]{:S(2)}, u32[]{:S(2)}) async-start(bf16[4,256,512]{2,1,0:T(8,128)(2,1)} %bitcast.24), calls=%async_computation.3 | async-start | bytes 2097152 | tf_op jit(solution)/shard_map/all_to_all | solution.py:1455
  562.8 37.7 %collective-permute-start.72 = (bf16[912,256]{1,0:T(8,128)(2,1)S(1)}, bf16[912,256]{1,0:T(8,128)(2,1)S(1)}, u32[]{:S(2)}, u32[]{:S(2)}) collective-permute-start(bf16[912,256]{1,0:T(8,128)(2,1)S(1)} %add_convert_fusion.8), channel_id=1, source_target_pairs={{0,1},{1,2},{2,3},{3,0},{4,5},{5,6},{6,7},{7,4},{8,9},{9,10},{10,1... | collective-permute-start | bytes 1400840 | tf_op jit(solution)/shard_map/ppermute | solution.py:969
  568.0 32.5 %collective-permute-start.71 = (bf16[912,256]{1,0:T(8,128)(2,1)}, bf16[912,256]{1,0:T(8,128)(2,1)S(1)}, u32[]{:S(2)}, u32[]{:S(2)}) collective-permute-start(bf16[912,256]{1,0:T(8,128)(2,1)} %get-tuple-element.937), channel_id=1, source_target_pairs={{0,8},{4,12},{8,0},{12,4},{16,24},{20,28},{24,16},{28,20},{1,9},{5... | collective-permute-start | bytes 1400840 | tf_op jit(solution)/shard_map/ppermute | solution.py:966
  571.4 29.0 %collective-permute-start.69 = (f32[185,128]{1,0:T(8,128)S(1)}, f32[185,128]{1,0:T(8,128)S(1)}, u32[]{:S(2)}, u32[]{:S(2)}) collective-permute-start(f32[185,128]{1,0:T(8,128)S(1)} %add.323), channel_id=1, source_target_pairs={{0,2},{1,3},{2,0},{3,1},{4,6},{5,7},{6,4},{7,5},{8,10},{9,11},{10,... | collective-permute-start | bytes 284168 | tf_op jit(solution)/shard_map/ppermute | solution.py:969
  572.4 28.1 %collective-permute-start.70 = (f32[185,128]{1,0:T(8,128)S(1)}, f32[185,128]{1,0:T(8,128)S(1)}, u32[]{:S(2)}, u32[]{:S(2)}) collective-permute-start(f32[185,128]{1,0:T(8,128)S(1)} %add.323), channel_id=1, source_target_pairs={{0,3},{1,0},{2,1},{3,2},{4,7},{5,4},{6,5},{7,6},{8,11},{9,8},{10,9... | collective-permute-start | bytes 284168 | tf_op jit(solution)/shard_map/ppermute | solution.py:969
  (150 other events, 2372.2 us)

commit v2 on v1

--- a/solution.py
+++ b/solution.py
@@ -992,6 +992,9 @@
             value = jnp.pad(value, ((0, self.n_t - value.shape[0]),) + ((0, 0),) * (value.ndim - 1))
         return lax.all_to_all(value, "tp", split_axis=0, concat_axis=0, tiled=True)
 
+    def all_sum(self, value):
+        return self.chip_sum(self.line_sum(value))
+
     def chip_sum(self, value):
         for bit in [1] + [2 * b for b in bits_of(self.chips)]:
             value = value + lax.ppermute(value, "fsdp", [(i, i ^ bit) for i in range(self.n_f)])
@@ -1002,7 +1005,6 @@
         for r in range(1, self.n_t):
             total = total + self.turn(value, r)
         return total
-
 
 def rms_terms(value):
     return lax.rsqrt(jnp.mean(value * value, axis=-1, keepdims=True) + EPS_NORM)
@@ -1039,13 +1041,14 @@
         return [self.full(r) for r in range(self.at.n_t)]
 
 
-def first_bit(at, r):
-    return at.chips // 2 if r % 3 == 0 else 1
+def first_bit(at, r, late=False):
+    return at.chips // 2 if r == 3 or (r == 0 and not late) else 1
 
 
 class Scatter:
-    def __init__(self, at):
+    def __init__(self, at, late=False):
         self.at = at
+        self.bit = lambda r: first_bit(at, r, late)
         self.near, self.far, self.two, self.one, self.end = {}, {}, {}, {}, {}
 
     def put(self, r, stacked):
@@ -1053,12 +1056,18 @@
 
     def cross(self, *turns):
         for r in turns:
-            self.far[r] = self.at.move(self.far[r], first_bit(self.at, r))
+            self.far[r] = self.at.move(self.far[r], self.bit(r))
+
+    def add(self, *turns):
+        sums = add_stacks([(self.near.pop(r), self.far.pop(r)) for r in turns])
+        return dict(zip(turns, sums))
+
+    def pass_on(self, sums):
+        for r, (keep, give) in sums.items():
+            self.two[r] = keep, self.at.move(give, 3 - self.bit(r))
 
     def fold(self, *turns):
-        sums = add_stacks([(self.near.pop(r), self.far.pop(r)) for r in turns])
-        for r, (keep, give) in zip(turns, sums):
-            self.two[r] = keep, self.at.move(give, 3 - first_bit(self.at, r))
+        self.pass_on(self.add(*turns))
 
     def close(self, *turns):
         for r in turns:
@@ -1086,7 +1095,7 @@
     def rest(self):
         for r in range(self.at.n_t):
             have = {}
-            for stack, group in zip((self.near.pop(r), self.far.pop(r)), sides(self.at.chips, first_bit(self.at, r))):
+            for stack, group in zip((self.near.pop(r), self.far.pop(r)), sides(self.at.chips, self.bit(r))):
                 have.update({p: stack[i] for i, p in enumerate(group)})
             for bit in bits_of(self.at.chips):
                 for p in [p for p in have if p & bit]:
@@ -1162,11 +1171,9 @@
     else:
         m_own = None
         head_ids = at.core * heads + jnp.arange(heads, dtype=jnp.int32)
-    m_own, tokens, gate_up_weight, down_weight, cotangent = sync(
-        m_own, tokens, gate_up_weight, down_weight, cotangent
-    )
     mine, give = at.halves(tokens, 2)
     both = at.in_order(mine, at.swap(give), 0)
+    both, m_own, gate_up_weight, down_weight, cotangent = sync(both, m_own, gate_up_weight, down_weight, cotangent)
     packed = jnp.concatenate([jnp.transpose(gate_up_weight, (1, 2, 0)), down_weight[None]], axis=0)
     mine, give = at.halves(packed, 1)
     f_own = at.in_order(mine, at.swap(give), 2)
@@ -1233,50 +1240,59 @@
         def without(parts, *keys):
             return {k: v for k, v in parts.items() if k not in keys}
 
+        came = at.spread_out(both)
         for p in range(1, chips):
             m.move(0, p, p)
-        m.turn(1)
-        m.turn(3)
-        m.parts, f.parts, both, cot_both, conv_t, scal, gain1, gain2, live, extra = sync(
-            m.parts, f.parts, both, cot_both, conv_t, scal, gain1, gain2, live, [(r.ask, r.keep) for r in routes]
+        m.parts, f.parts, came, cot_both, conv_t, scal, gain1, gain2, live, extra = sync(
+            m.parts, f.parts, came, cot_both, conv_t, scal, gain1, gain2, live, [(r.ask, r.keep) for r in routes]
         )
         for r, (ask, keep), part in zip(routes, extra, (cot_both[:, :, :quarter], cot_both[:, :, quarter:])):
             r.ask, r.keep, r.have = ask, keep, [part]
+        m.turn(1)
+        m.turn(3)
+        for r in routes:
+            r.step()
+        x = sequence(came)
+        normed_one = norm_first(x.astype(F32))
+        run(0)
+        state = route_state()
+        m.parts, f.parts, state, proj[0], normed_one, x = sync(m.parts, f.parts, state, proj[0], normed_one, x)
+        set_routes(state)
         for r in (1, 3):
             m.move(r, 1, 1)
             m.move(r, 2, 2)
-        came = at.spread_out(both)
         m.turn(2, 1)
-        m.parts, f.parts, came = sync(m.parts, f.parts, came)
+        give = asked()
+        m.parts, f.parts, give = sync(m.parts, f.parts, give)
         m.move(1, 3, 1)
         m.move(3, 3, 2)
+        f.turn(1)
+        m.parts, f.parts, give = sync(m.parts, f.parts, give)
         m.move(2, 1, 1)
         m.move(2, 2, 2)
-        x = sequence(came)
-        normed_one = norm_first(x.astype(F32))
-        run(0)
-        early = without(m.parts, (2, 1), (2, 2))
-        early, f.parts, proj[0], normed_one, x = sync(early, f.parts, proj[0], normed_one, x)
-        m.parts.update(early)
-        m.move(2, 3, 3)
-        f.turn(1)
+        for r, part in zip(routes, give):
+            r.last(part)
         f.turn(3)
         run(1)
         run(3)
         state = route_state()
         m.parts, proj, normed_one, f.parts, state = sync(m.parts, proj, normed_one, f.parts, state)
         set_routes(state)
-        for r in routes:
-            r.step()
+        m.move(2, 3, 1)
+        f.turn(2, 1)
         f.move(0, 1, 1)
         f.move(0, 2, 2)
+        cot_home = routed()
+        early = without(f.parts, (0, 1), (0, 2))
+        m.parts, early, cot_home, normed_one = sync(m.parts, early, cot_home, normed_one)
+        f.parts.update(early)
+        cot_came = at.spread_out(cot_home)
+        f.move(1, 1, 1)
+        f.move(1, 2, 2)
         run(2)
-        early = without(f.parts, (0, 1), (0, 2))
-        state = route_state()
-        proj, early, state = sync(proj, early, state)
+        early = without(f.parts, (1, 1), (1, 2))
+        proj, early = sync(proj, early)
         f.parts.update(early)
-        set_routes(state)
-        give = asked()
         m_parts = [m.full(r) for r in laps]
     else:
         x = sequence(at.spread_out(both))
@@ -1296,31 +1312,26 @@
         for r in routes:
             for _ in bits[1:]:
                 r.step()
-        give = asked()
+        for r, part in zip(routes, asked()):
+            r.last(part)
+        cot_came = at.spread_out(routed())
         f_parts = f.rest()
 
     raw, gate, q, k, v, rows = (list(group) for group in zip(*[proj[h] for h in range(heads)]))
-    for r, part in zip(routes, give):
-        r.last(part)
     if fast:
-        f.move(1, 1, 1)
-        f.move(1, 2, 2)
+        f.move(0, 3, 2)
     first = recur(gain_o, start_state, q, k, v, gate, rows, 0, steps)
     if fast:
-        state = route_state()
-        first, f.parts, state = sync(first, f.parts, state)
-        set_routes(state)
-    cot_came = at.spread_out(routed())
-    if fast:
-        f.move(0, 3, 2)
+        first, f.parts, cot_came = sync(first, f.parts, cot_came)
         f.move(1, 3, 1)
-        f.move(3, 1, 1)
-        f.turn(2, 1)
+        for r in (3, 2):
+            f.move(r, 1, 1)
+            f.move(r, 2, 2)
     second = recur(gain_o, first[1], q, k, v, gate, rows, steps, steps, first[0])
     if fast:
-        second, f.parts, cot_came = sync(second, f.parts, cot_came)
-        f.move(3, 2, 2)
-        f.move(2, 1, 1)
+        early = without(f.parts, (2, 1), (2, 2))
+        second, early = sync(second, early)
+        f.parts.update(early)
     z = second[0]
     mix = mix_out(z, m_parts)
     mid = x.astype(F32) + (mix.astype(F32) + at.swap(mix).astype(F32))
@@ -1333,9 +1344,8 @@
     bits_a, bits_b = [first_bit(at, r) for r in group_a], [first_bit(at, r) for r in group_b]
     if fast:
         normed_two, dy, f.parts = sync(normed_two, dy, f.parts)
+        f.move(2, 3, 1)
         f.move(3, 3, 2)
-        f.move(2, 2, 2)
-        f.move(2, 3, 2)
         f_parts = {r: f.full(r) for r in group_a}
     net, db, grads = ffn(normed_two, dy, [f_parts[r] for r in group_a], bits_a, last=False)
     if fast:
@@ -1391,39 +1401,43 @@
         f_rs.home(3)
 
     dps, g_conv, g_small = {}, {}, {}
-    m_rs = Scatter(at)
+    m_rs = Scatter(at, late=True)
 
     def run_back(h):
         dps[h], g_conv[h], g_small[h], grads = project_back(
-            h, normed_one, conv_t, scal, raw[h], rows[h], ds[h], drows[h], g_out[h], first_bit(at, h)
+            h, normed_one, conv_t, scal, raw[h], rows[h], ds[h], drows[h], g_out[h], m_rs.bit(h)
         )
         m_rs.put(h, grads)
 
+    def moved(group, key):
+        return {r: v for r, v in group.items() if r == key}
+
     if fast:
         run_back(2)
-        dps, state, f_state, ds = sync(dps, m_rs.state(), f_rs.state(), ds)
-        m_rs.take(state)
+        dps, m_rs.near, m_rs.far, ds = sync(dps, m_rs.near, m_rs.far, ds)
+        m_rs.cross(2)
+        run_back(1)
+        dps, m_rs.near, far, ds, f_state = sync(dps, m_rs.near, moved(m_rs.far, 1), ds, f_rs.state())
+        m_rs.far.update(far)
         f_rs.take(f_state)
         f_rs.join(2)
         f_rs.home(1)
-        m_rs.cross(2)
-        run_back(1)
-        dps, state, ds = sync(dps, m_rs.state(), ds)
-        m_rs.take(state)
-        m_rs.fold(2)
         m_rs.cross(1)
         run_back(3)
-        dps, state, ds, f_rs.end = sync(dps, m_rs.state(), ds, f_rs.end)
-        m_rs.take(state)
-        m_rs.close(2)
-        m_rs.home(2)
-        m_rs.fold(1)
+        far = {r: m_rs.far[r] for r in (2, 3)}
+        dps, m_rs.near, far, ds = sync(dps, m_rs.near, far, ds)
+        m_rs.far.update(far)
+        m_rs.fold(2)
         m_rs.cross(3)
         run_back(0)
-        dps, m_rs.two, m_rs.near, far = sync(dps, m_rs.two, m_rs.near, {0: m_rs.far[0]})
+        far = {r: m_rs.far[r] for r in (0, 1)}
+        dps, m_rs.near, far, m_rs.two, f_rs.end = sync(dps, m_rs.near, far, m_rs.two, f_rs.end)
         m_rs.far.update(far)
-        m_rs.close(1)
-        m_rs.home(1)
+        m_rs.close(2)
+        sums = m_rs.add(1, 3)
+        dps, m_rs.one, sums = sync(dps, m_rs.one, sums)
+        m_rs.merge(2)
+        m_rs.pass_on(sums)
         m_rs.cross(0)
     else:
         for h in range(heads):
@@ -1431,9 +1445,11 @@
     output = settle(out_came)
     da, g_gain1 = input_back([dps[h] for h in range(heads)], m_parts, x)
     if fast:
-        da, g_gain1, far, m_rs.near = sync(da, g_gain1, {3: m_rs.far[3]}, m_rs.near)
-        m_rs.far.update(far)
-        m_rs.fold(3)
+        da, g_gain1, m_rs.two, m_rs.end = sync(da, g_gain1, m_rs.two, m_rs.end)
+        m_rs.close(1, 3)
+        m_rs.join(2)
+        m_rs.home(1)
+        m_rs.home(3)
     da_other = at.swap(da)
     d_x_norm = rms_back(x.astype(F32), gain1, da.astype(F32) + da_other.astype(F32))
     dx_home = give_back(d_mix.astype(F32) + d_x_norm)
@@ -1444,17 +1460,14 @@
     gains = jnp.concatenate([at.relative(g_gain1[0]), 0.5 * at.relative(g_gain2[0])]).reshape(-1, HD)
     sums = jnp.concatenate([conv_all, decay_all, gains, g_gain_o], axis=0)
     if fast:
-        dx_home, sums, state = sync(dx_home, at.chip_sum(sums), m_rs.state())
-        m_rs.take(state)
+        dx_home, sums, m_rs.near, m_rs.end = sync(dx_home, at.line_sum(sums), m_rs.near, m_rs.end)
         m_rs.fold(0)
-        m_rs.close(3)
-        m_rs.home(3)
+        sums = at.chip_sum(sums)
     else:
-        sums = at.chip_sum(sums)
-    sums = at.line_sum(sums)
+        sums = at.all_sum(sums)
     dx_came = lax.all_to_all(dx_home, "tp", split_axis=0, concat_axis=0, tiled=True)
     if fast:
-        dx_came, sums, m_rs.two, m_rs.end = sync(dx_came, sums, m_rs.two, m_rs.end)
+        dx_came, m_rs.two, m_rs.end = sync(dx_came, m_rs.two, m_rs.end)
         m_rs.close(0)
     input_grad = settle(dx_came)
     n_conv = conv_all.shape[0]
@@ -1480,7 +1493,7 @@
         joined = []
         for h in range(heads):
             have = {}
-            for stack, group in zip((m_rs.near[h], m_rs.far[h]), sides(chips, first_bit(at, h))):
+            for stack, group in zip((m_rs.near[h], m_rs.far[h]), sides(chips, m_rs.bit(h))):
                 have.update({p: stack[i] for i, p in enumerate(group)})
             joined.append(jnp.concatenate([have[p] for p in range(chips)], axis=1))
         joined = jnp.stack(joined)

time: 616 us -> 548 us (0.89)
  waiting for transfers between devices: 165 us -> 112 us
  local copies, waits for them, and re-layouts: 30.7 us -> 23.2 us
    ppermute x15, waiting for transfers between devices: 73.1 us -> 31.1 us  [turn(): lax.ppermute(value, 'tp', [(i, (i + r) % self.n_t) for i in range(self.n_...]
    ppermute x44, waiting for transfers between devices: 77.7 us -> 65.2 us  [move(): lax.ppermute(value, 'fsdp', [(i, i ^ 2 * bit) for i in range(self.n_f)])]
    ppermute x3, waiting for transfers between devices: 5.59 us -> 13.1 us  [chip_sum(): lax.ppermute(value, 'fsdp', [(i, i ^ bit) for i in range(self.n_f)])]
    all_to_all x2, waiting for transfers between devices: 6.75 us -> 0.01 us  [spread_out(): return lax.all_to_all(value, 'tp', split_axis=0, concat_axis=0, tiled=True)]
    unnamed x210 -> x158, local copies, waits for them, and re-layouts: 14.7 us -> 11.6 us
    pallas_call x6 -> x5, Pallas kernels: 22 us -> 19.4 us  [add_stacks(): pl.pallas_call(functools.partial(add_kernel, len(pairs)), out_shape=[jax....]
  transfers between devices with their start and end apart: 80 -> 80, of which waited for: 30 -> 32; matrix products, arithmetic and copies ran while one was open for 10% -> 9% of each run, Pallas kernels for 41% -> 47%
where the time goes in v2:
time: 548 us; the launch traced here: 539 us
  Pallas kernels  259 us (47%)
  waiting for transfers between devices  112 us (20%)
  starting transfers between devices  94.4 us (17%)
  other arithmetic  47 us (9%)
  local copies, waits for them, and re-layouts  23.2 us (4%)
    ppermute x44, waiting for transfers between devices, move(): lax.ppermute(value, 'fsdp', [(i, i ^ 2 * bit) for i in range(self.n_f)])  65.2 us
    pallas_call x4, Pallas kernels, project_back(): pl.pallas_call(functools.partial(project_back_kernel, pieces, bit, h), ou...  55.1 us
    ppermute x44, starting transfers between devices, move(): lax.ppermute(value, 'fsdp', [(i, i ^ 2 * bit) for i in range(self.n_f)])  46.5 us
    pallas_call x2, Pallas kernels, ffn(): pl.pallas_call(functools.partial(ffn_kernel, pieces, chunks, bits, bool(m...  45.3 us
    pallas_call x2, Pallas kernels, recur_back(): pl.pallas_call(functools.partial(recur_back_kernel, heads, len(done)), ou...  41.6 us
    pallas_call x4, Pallas kernels, project(): pl.pallas_call(functools.partial(project_kernel, pieces, h), out_shape=[j...  31.8 us
    ppermute x15, waiting for transfers between devices, turn(): lax.ppermute(value, 'tp', [(i, (i + r) % self.n_t) for i in range(self.n_...  31.1 us
    pallas_call x2, Pallas kernels, recur(): pl.pallas_call(functools.partial(recur_kernel, heads, len(more)), out_sha...  28.8 us
  transfers between devices with their start and end apart: 80, of which 32 were waited for; matrix products, arithmetic and copies ran while one was open for 9% of the time, Pallas kernels for 47%

profile of v2, /device:TPU:0, one launch (start us, length us, event | category | flops | bytes accessed | tf_op | source)
XLA Modules:
  0.0 538.9 jit_solution(6825823777027576854)
XLA Ops:
  9.2 6.4 %all-to-all-start = ((bf16[4,256,512]{2,1,0:T(8,128)(2,1)}), bf16[4,256,512]{2,1,0:T(8,128)(2,1)S(1)}, u32[]{:S(2)}, u32[]{:S(2)}) async-start(bf16[4,256,512]{2,1,0:T(8,128)(2,1)} %pad_maximum_fusion.1), calls=%async_computation | async-start | bytes 2097152 | tf_op jit(solution)/shard_map/all_to_all | solution.py:993
  25.9 6.5 %collective-permute-done.2.refs_1_.refs_5_ = bf16[912,256]{1,0:T(8,128)(2,1)S(1)} collective-permute-done((bf16[912,256]{1,0:T(8,128)(2,1)S(1)}, bf16[912,256]{1,0:T(8,128)(2,1)S(1)}, u32[]{:S(2)}, u32[]{:S(2)}) %collective-permute-start.2) | collective-permute-done | bytes 466976 | tf_op jit(solution)/shard_map/ppermute | solution.py:966
  32.5 10.3 %collective-permute-done.3.refs_2_.refs_6_ = bf16[912,256]{1,0:T(8,128)(2,1)S(1)} collective-permute-done((bf16[912,256]{1,0:T(8,128)(2,1)S(1)}, bf16[912,256]{1,0:T(8,128)(2,1)S(1)}, u32[]{:S(2)}, u32[]{:S(2)}) %collective-permute-start.3) | collective-permute-done | bytes 466976 | tf_op jit(solution)/shard_map/ppermute | solution.py:966
  52.7 8.0 %project.4 = (bf16[1024,640]{1,0:T(8,128)(2,1)}, bf16[1024,128]{1,0:T(8,128)(2,1)}, bf16[1024,128]{1,0:T(8,128)(2,1)}, bf16[2048,128]{1,0:T(8,128)(2,1)}, bf16[2...) custom-call(f32[4,2]{1,0:T(4,128)} %pad_maximum_fusion.10.scal_ref, bf16[1024,1024]{1,0:T(8,128)(2,1)} %fusion.9.a_ref, ...), custom_call_target="tpu_custom_call" | custom-call | flops 1644167168 | bytes 8000000 | tf_op jit(solution)/shard_map/project/pallas_call | solution.py:172
  60.7 7.1 %collective-permute-done.8.refs_0_.refs_12_.refs_16_ = bf16[912,256]{1,0:T(8,128)(2,1)} collective-permute-done((bf16[912,256]{1,0:T(8,128)(2,1)S(1)}, bf16[912,256]{1,0:T(8,128)(2,1)}, u32[]{:S(2)}, u32[]{:S(2)}) %collective-permute-start.8) | collective-permute-done | bytes 466976 | tf_op jit(solution)/shard_map/ppermute | solution.py:969
  73.4 4.3 select_blocks.2
  83.7 6.7 %collective-permute-done.15.refs_1_.refs_13_.refs_17_ = bf16[912,256]{1,0:T(8,128)(2,1)S(1)} collective-permute-done((bf16[912,256]{1,0:T(8,128)(2,1)}, bf16[912,256]{1,0:T(8,128)(2,1)S(1)}, u32[]{:S(2)}, u32[]{:S(2)}) %collective-permute-start.15) | collective-permute-done | bytes 466976 | tf_op jit(solution)/shard_map/ppermute | solution.py:966
  94.9 8.9 %collective-permute-done.17.refs_3_.refs_7_.refs_11_ = bf16[912,256]{1,0:T(8,128)(2,1)S(1)} collective-permute-done((bf16[912,256]{1,0:T(8,128)(2,1)S(1)}, bf16[912,256]{1,0:T(8,128)(2,1)S(1)}, u32[]{:S(2)}, u32[]{:S(2)}) %collective-permute-start.17) | collective-permute-done | bytes 466976 | tf_op jit(solution)/shard_map/ppermute | solution.py:966
  110.6 8.0 %project.6 = (bf16[1024,640]{1,0:T(8,128)(2,1)}, bf16[1024,128]{1,0:T(8,128)(2,1)}, bf16[1024,128]{1,0:T(8,128)(2,1)}, bf16[2048,128]{1,0:T(8,128)(2,1)}, bf16[2...) custom-call(f32[4,2]{1,0:T(4,128)} %pad_maximum_fusion.10.scal_ref, bf16[1024,1024]{1,0:T(8,128)(2,1)} %fusion.9.a_ref, ...), custom_call_target="tpu_custom_call" | custom-call | flops 1644167168 | bytes 8000000 | tf_op jit(solution)/shard_map/project/pallas_call | solution.py:172
  118.6 8.0 %project.5 = (bf16[1024,640]{1,0:T(8,128)(2,1)}, bf16[1024,128]{1,0:T(8,128)(2,1)}, bf16[1024,128]{1,0:T(8,128)(2,1)}, bf16[2048,128]{1,0:T(8,128)(2,1)}, bf16[2...) custom-call(f32[4,2]{1,0:T(4,128)} %pad_maximum_fusion.10.scal_ref, bf16[1024,1024]{1,0:T(8,128)(2,1)} %fusion.9.a_ref, ...), custom_call_target="tpu_custom_call" | custom-call | flops 1644167168 | bytes 8000000 | tf_op jit(solution)/shard_map/project/pallas_call | solution.py:172
  133.0 4.5 select_blocks.3
  146.4 7.9 %project.7 = (bf16[1024,640]{1,0:T(8,128)(2,1)}, bf16[1024,128]{1,0:T(8,128)(2,1)}, bf16[1024,128]{1,0:T(8,128)(2,1)}, bf16[2048,128]{1,0:T(8,128)(2,1)}, bf16[2...) custom-call(f32[4,2]{1,0:T(4,128)} %pad_maximum_fusion.10.scal_ref, bf16[1024,1024]{1,0:T(8,128)(2,1)} %fusion.9.a_ref, ...), custom_call_target="tpu_custom_call" | custom-call | flops 1644167168 | bytes 8000000 | tf_op jit(solution)/shard_map/project/pallas_call | solution.py:172
  162.5 14.4 %recur.2 = (bf16[1024,512]{1,0:T(8,128)(2,1)}, f32[4,128,128]{2,1,0:T(8,128)}, bf16[512,128]{1,0:T(8,128)(2,1)}, bf16[512,128]{1,0:T(8,128)(2,1)}, bf16[512,128]...) custom-call(f32[1,128]{1,0:T(1,128)} %bitcast.110, ...), custom_call_target="tpu_custom_call" | custom-call | flops 2688000000 | bytes 1000000 | tf_op jit(solution)/shard_map/recur/pallas_call | solution.py:346
  183.7 14.4 %recur.3 = (bf16[1024,512]{1,0:T(8,128)(2,1)}, f32[4,128,128]{2,1,0:T(8,128)}, bf16[512,128]{1,0:T(8,128)(2,1)}, bf16[512,128]{1,0:T(8,128)(2,1)}, bf16[512,128]...) custom-call(f32[1,128]{1,0:T(1,128)} %bitcast.111, ...), custom_call_target="tpu_custom_call", output_to_operand_aliasing={{0}: (22, {})} | custom-call | flops 2688000000 | bytes 1000000 | tf_op jit(solution)/shard_map/recur/pallas_call | solution.py:346
  198.2 5.3 mix_out.1
  222.2 22.0 %ffn.2 = (f32[1024,1024]{1,0:T(8,128)}, f32[1024,1024]{1,0:T(8,128)}, bf16[2,1056,256]{2,1,0:T(8,128)(2,1)}, bf16[2,1056,256]{2,1,0:T(8,128)(2,1)}, bf16[2,1056,...) custom-call(bf16[1024,1024]{1,0:T(8,128)(2,1)} %multiply_convert_fusion.1.b_ref, ...), custom_call_target="tpu_custom_call" | custom-call | flops 13287555072 | bytes 1000000 | tf_op jit(solution)/shard_map/ffn/pallas_call | solution.py:928
  246.0 23.3 %ffn.3 = (bf16[1024,1024]{1,0:T(8,128)(2,1)}, bf16[1024,1024]{1,0:T(8,128)(2,1)}, bf16[2,1056,256]{2,1,0:T(8,128)(2,1)}, bf16[2,1056,256]{2,1,0:T(8,128)(2,1)}, ...) custom-call(bf16[1024,1024]{1,0:T(8,128)(2,1)} %multiply_convert_fusion.1.b_ref, ...), custom_call_target="tpu_custom_call" | custom-call | flops 13287555072 | bytes 1000000 | tf_op jit(solution)/shard_map/ffn/pallas_call | solution.py:928
  270.9 4.4 add_stacks.5
  279.1 10.3 %mix_back.1 = (bf16[1024,1024]{1,0:T(8,128)(2,1)}, bf16[1024,512]{1,0:T(8,128)(2,1)}, f32[1,1024]{1,0:T(1,128)}, bf16[128,256]{1,0:T(8,128)(2,1)}, bf16[128,256]...) custom-call(f32[1,1024]{1,0:T(1,128)} %bitcast.97, ...), custom_call_target="tpu_custom_call" | custom-call | flops 2147483648 | bytes 1000000 | tf_op jit(solution)/shard_map/mix_back/pallas_call | solution.py:797
  293.0 20.8 %recur_back.2 = (bf16[1024,768]{1,0:T(8,128)(2,1)}, bf16[1024,768]{1,0:T(8,128)(2,1)}, bf16[1024,768]{1,0:T(8,128)(2,1)}, bf16[1024,768]{1,0:T(8,128)(2,1)}, f32...) custom-call(f32[1,128]{1,0:T(1,128)} %bitcast.112, ...), custom_call_target="tpu_custom_call" | custom-call | flops 4032000000 | bytes 1000000 | tf_op jit(solution)/shard_map/recur_back/pallas_call | solution.py:505
  321.8 5.6 %all-to-all-start.2 = ((bf16[4,256,512]{2,1,0:T(8,128)(2,1)}), bf16[4,256,512]{2,1,0:T(8,128)(2,1)S(1)}, u32[]{:S(2)}, u32[]{:S(2)}) async-start(bf16[4,256,512]{2,1,0:T(8,128)(2,1)} %bitcast.23), calls=%async_computation.2 | async-start | bytes 2097152 | tf_op jit(solution)/shard_map/all_to_all | solution.py:1390
  327.4 4.4 add_stacks.6
  334.3 20.8 %recur_back.3 = (bf16[1024,768]{1,0:T(8,128)(2,1)}, bf16[1024,768]{1,0:T(8,128)(2,1)}, bf16[1024,768]{1,0:T(8,128)(2,1)}, bf16[1024,768]{1,0:T(8,128)(2,1)}, f32...) custom-call(f32[1,128]{1,0:T(1,128)} %bitcast.113, ...), custom_call_target="tpu_custom_call", output_to_operand_aliasing={{0}: (33, {}), {1}: (34, {}), {2}: (35, {}), {3}: (36, {}),... | custom-call | flops 4032000000 | bytes 1000000 | tf_op jit(solution)/shard_map/recur_back/pallas_call | solution.py:505
  360.3 13.7 %project_back.4 = (bf16[1024,784]{1,0:T(8,128)(2,1)}, f32[8,640]{1,0:T(8,128)}, f32[8,128]{1,0:T(8,128)}, bf16[2,912,256]{2,1,0:T(8,128)(2,1)}, bf16[2,912,256]{2,1,0:T(8,128)(2,1)}) custom-call(f32[4,2]{1,0:T(4,128)} %pad_maximum_fusion.10.scal_ref, bf16[1024,1024]{1,0:T(8,128)(2,1)} %fusion.9.a_ref, f32[4,8,640]{2,1,0:T(8,128)} %select_reduce_fusion.cw_ref, ...), custom_call_target="tpu_custom_call" | custom-call | flops 1644167168 | bytes 1000000 | tf_op jit(solution)/shard_map/project_back/pallas_call | solution.py:639
  378.0 14.1 %project_back.5 = (bf16[1024,784]{1,0:T(8,128)(2,1)}, f32[8,640]{1,0:T(8,128)}, f32[8,128]{1,0:T(8,128)}, bf16[2,912,256]{2,1,0:T(8,128)(2,1)}, bf16[2,912,256]{2,1,0:T(8,128)(2,1)}) custom-call(f32[4,2]{1,0:T(4,128)} %pad_maximum_fusion.10.scal_ref, bf16[1024,1024]{1,0:T(8,128)(2,1)} %fusion.9.a_ref, f32[4,8,640]{2,1,0:T(8,128)} %select_reduce_fusion.cw_ref, ...), custom_call_target="tpu_custom_call" | custom-call | flops 1644167168 | bytes 1000000 | tf_op jit(solution)/shard_map/project_back/pallas_call | solution.py:639
  396.2 13.7 %project_back.6 = (bf16[1024,784]{1,0:T(8,128)(2,1)}, f32[8,640]{1,0:T(8,128)}, f32[8,128]{1,0:T(8,128)}, bf16[2,912,256]{2,1,0:T(8,128)(2,1)}, bf16[2,912,256]{2,1,0:T(8,128)(2,1)}) custom-call(f32[4,2]{1,0:T(4,128)} %pad_maximum_fusion.10.scal_ref, bf16[1024,1024]{1,0:T(8,128)(2,1)} %fusion.9.a_ref, f32[4,8,640]{2,1,0:T(8,128)} %select_reduce_fusion.cw_ref, ...), custom_call_target="tpu_custom_call" | custom-call | flops 1644167168 | bytes 1000000 | tf_op jit(solution)/shard_map/project_back/pallas_call | solution.py:639
  419.7 13.7 %project_back.7 = (bf16[1024,784]{1,0:T(8,128)(2,1)}, f32[8,640]{1,0:T(8,128)}, f32[8,128]{1,0:T(8,128)}, bf16[2,912,256]{2,1,0:T(8,128)(2,1)}, bf16[2,912,256]{2,1,0:T(8,128)(2,1)}) custom-call(f32[4,2]{1,0:T(4,128)} %pad_maximum_fusion.10.scal_ref, bf16[1024,1024]{1,0:T(8,128)(2,1)} %fusion.9.a_ref, f32[4,8,640]{2,1,0:T(8,128)} %select_reduce_fusion.cw_ref, ...), custom_call_target="tpu_custom_call" | custom-call | flops 1644167168 | bytes 1000000 | tf_op jit(solution)/shard_map/project_back/pallas_call | solution.py:639
  435.0 8.1 %collective-permute-done.56 = bf16[912,256]{1,0:T(8,128)(2,1)} collective-permute-done((bf16[912,256]{1,0:T(8,128)(2,1)}, bf16[912,256]{1,0:T(8,128)(2,1)}, u32[]{:S(2)}, u32[]{:S(2)}) %collective-permute-start.56) | collective-permute-done | bytes 466976 | tf_op jit(solution)/shard_map/ppermute | solution.py:966
  452.4 13.0 %input_back.1 = (bf16[1024,1024]{1,0:T(8,128)(2,1)}, f32[1,1024]{1,0:T(1,128)}) custom-call(bf16[1024,784]{1,0:T(8,128)(2,1)} %get-tuple-element.988.refs_0_, bf16[1024,784]{1,0:T(8,128)(2,1)} %get-tuple-element.989.refs_1_, bf16[1024,784]{1,0:T(8,128)(2,1)} %get-tuple-element.990.refs_2_, bf16[1024,784]{1,0:T(8,128)(2,1)} %get-tuple-element.991.refs_3_, ...), custom_call_target="tpu_custom_call" | custom-call | flops 6576668672 | bytes 1000000 | tf_op jit(solution)/shard_map/input_back/pallas_call | solution.py:705
  488.9 6.4 %collective-permute-done.67 = bf16[912,256]{1,0:T(8,128)(2,1)S(1)} collective-permute-done((bf16[912,256]{1,0:T(8,128)(2,1)S(1)}, bf16[912,256]{1,0:T(8,128)(2,1)S(1)}, u32[]{:S(2)}, u32[]{:S(2)}) %collective-permute-start.67) | collective-permute-done | bytes 466976 | tf_op jit(solution)/shard_map/ppermute | solution.py:969
  495.3 7.7 %collective-permute-done.66 = bf16[912,256]{1,0:T(8,128)(2,1)S(1)} collective-permute-done((bf16[912,256]{1,0:T(8,128)(2,1)S(1)}, bf16[912,256]{1,0:T(8,128)(2,1)S(1)}, u32[]{:S(2)}, u32[]{:S(2)}) %collective-permute-start.66) | collective-permute-done | bytes 466976 | tf_op jit(solution)/shard_map/ppermute | solution.py:969
  519.5 11.9 %collective-permute-done.73 = f32[185,128]{1,0:T(8,128)S(1)} collective-permute-done((f32[185,128]{1,0:T(8,128)S(1)}, f32[185,128]{1,0:T(8,128)S(1)}, u32[]{:S(2)}, u32[]{:S(2)}) %collective-permute-start.73) | collective-permute-done | bytes 94752 | tf_op jit(solution)/shard_map/ppermute | solution.py:1000
  (425 shorter events, 201.6 us)
Async XLA Ops:
  9.2 33.6 %all-to-all-start = ((bf16[4,256,512]{2,1,0:T(8,128)(2,1)}), bf16[4,256,512]{2,1,0:T(8,128)(2,1)S(1)}, u32[]{:S(2)}, u32[]{:S(2)}) async-start(bf16[4,256,512]{2,1,0:T(8,128)(2,1)} %pad_maximum_fusion.1), calls=%async_computation | async-start | bytes 2097152 | tf_op jit(solution)/shard_map/all_to_all | solution.py:993
  20.4 22.4 %collective-permute-start.3 = (bf16[912,256]{1,0:T(8,128)(2,1)S(1)}, bf16[912,256]{1,0:T(8,128)(2,1)S(1)}, u32[]{:S(2)}, u32[]{:S(2)}) collective-permute-start(bf16[912,256]{1,0:T(8,128)(2,1)S(1)} %pad_maximum_fusion.6.refs_0_.refs_4_), channel_id=1, source_target_pairs={{0,16},{4,20},{8,24},{12,28},{16,0},{20,4},{24,8},{28,12},{1,17},{... | collective-permute-start | bytes 1400840 | tf_op jit(solution)/shard_map/ppermute | solution.py:966
  21.9 20.8 %collective-permute-start.4 = (bf16[912,256]{1,0:T(8,128)(2,1)S(1)}, bf16[912,256]{1,0:T(8,128)(2,1)}, u32[]{:S(2)}, u32[]{:S(2)}) collective-permute-start(bf16[912,256]{1,0:T(8,128)(2,1)S(1)} %pad_maximum_fusion.6.refs_0_.refs_4_), channel_id=1, source_target_pairs={{0,24},{4,28},{8,16},{12,20},{16,8},{20,12},{24,0},{28,4},{1,25},{... | collective-permute-start | bytes 1400840 | tf_op jit(solution)/shard_map/ppermute | solution.py:966
  44.9 22.9 %collective-permute-start.8 = (bf16[912,256]{1,0:T(8,128)(2,1)S(1)}, bf16[912,256]{1,0:T(8,128)(2,1)}, u32[]{:S(2)}, u32[]{:S(2)}) collective-permute-start(bf16[912,256]{1,0:T(8,128)(2,1)S(1)} %pad_maximum_fusion.6.refs_0_.refs_4_), channel_id=1, source_target_pairs={{0,3},{1,0},{2,1},{3,2},{4,7},{5,4},{6,5},{7,6},{8,11},{9,8},{10,9... | collective-permute-start | bytes 1400840 | tf_op jit(solution)/shard_map/ppermute | solution.py:969
  46.9 20.9 %collective-permute-start.10 = (bf16[4,256,256]{2,1,0:T(8,128)(2,1)S(1)}, bf16[4,256,256]{2,1,0:T(8,128)(2,1)S(1)}, u32[]{:S(2)}, u32[]{:S(2)}) collective-permute-start(bf16[4,256,256]{2,1,0:T(8,128)(2,1)S(1)} %get-tuple-element.646.refs_2_.refs_3_), channel_id=1, source_target_pairs={{0,16},{4,20},{8,24},{12,28},{16,0},{20,4},{24,8},{28,12},{1,17},{... | collective-permute-start | bytes 1572872 | tf_op jit(solution)/shard_map/ppermute | solution.py:966
  106.4 22.5 %collective-permute-start.22 = (bf16[1056,256]{1,0:T(8,128)(2,1)S(1)}, bf16[1056,256]{1,0:T(8,128)(2,1)}, u32[]{:S(2)}, u32[]{:S(2)}) collective-permute-start(bf16[1056,256]{1,0:T(8,128)(2,1)S(1)} %bitcast.92), channel_id=1, source_target_pairs={{0,3},{1,0},{2,1},{3,2},{4,7},{5,4},{6,5},{7,6},{8,11},{9,8},{10,9... | collective-permute-start | bytes 1622024 | tf_op jit(solution)/shard_map/ppermute | solution.py:969
  106.6 22.4 %collective-permute-start.23 = (bf16[4,256,256]{2,1,0:T(8,128)(2,1)}, bf16[4,256,256]{2,1,0:T(8,128)(2,1)}, u32[]{:S(2)}, u32[]{:S(2)}) collective-permute-start(bf16[4,256,256]{2,1,0:T(8,128)(2,1)} %get-tuple-element.609), channel_id=1, source_target_pairs={{0,16},{4,20},{8,24},{12,28},{16,0},{20,4},{24,8},{28,12},{1,17},{... | collective-permute-start | bytes 1572872 | tf_op jit(solution)/shard_map/ppermute | solution.py:966
  108.1 20.9 %collective-permute-start.24 = (bf16[4,256,256]{2,1,0:T(8,128)(2,1)}, bf16[4,256,256]{2,1,0:T(8,128)(2,1)}, u32[]{:S(2)}, u32[]{:S(2)}) collective-permute-start(bf16[4,256,256]{2,1,0:T(8,128)(2,1)} %get-tuple-element.610), channel_id=1, source_target_pairs={{0,8},{4,12},{8,0},{12,4},{16,24},{20,28},{24,16},{28,20},{1,9},{5... | collective-permute-start | bytes 1572872 | tf_op jit(solution)/shard_map/ppermute | solution.py:966
  108.8 20.1 %collective-permute-start.20 = (bf16[912,256]{1,0:T(8,128)(2,1)S(1)}, bf16[912,256]{1,0:T(8,128)(2,1)S(1)}, u32[]{:S(2)}, u32[]{:S(2)}) collective-permute-start(bf16[912,256]{1,0:T(8,128)(2,1)S(1)} %collective-permute-done.14.refs_0_.refs_8_.refs_12_), channel_id=1, source_target_pairs={{0,8},{4,12},{8,0},{12,4},{16,24},{20,28},{24,16},{28,20},{1,9},{5... | collective-permute-start | bytes 1400840 | tf_op jit(solution)/shard_map/ppermute | solution.py:966
  140.7 40.7 %all-to-all-start.1 = ((bf16[4,256,512]{2,1,0:T(8,128)(2,1)}), bf16[4,256,512]{2,1,0:T(8,128)(2,1)S(1)}, u32[]{:S(2)}, u32[]{:S(2)}) async-start(bf16[4,256,512]{2,1,0:T(8,128)(2,1)} %select_blocks.3), calls=%async_computation.1 | async-start | bytes 2097152 | tf_op jit(solution)/shard_map/all_to_all | solution.py:993
  160.7 20.8 %collective-permute-start.31 = (bf16[1056,256]{1,0:T(8,128)(2,1)}, bf16[1056,256]{1,0:T(8,128)(2,1)}, u32[]{:S(2)}, u32[]{:S(2)}) collective-permute-start(bf16[1056,256]{1,0:T(8,128)(2,1)} %collective-permute-done.19.refs_4_), channel_id=1, source_target_pairs={{0,16},{4,20},{8,24},{12,28},{16,0},{20,4},{24,8},{28,12},{1,17},{... | collective-permute-start | bytes 1622024 | tf_op jit(solution)/shard_map/ppermute | solution.py:966
  219.8 24.4 %collective-permute-start.39 = (bf16[1056,256]{1,0:T(8,128)(2,1)S(1)}, bf16[1056,256]{1,0:T(8,128)(2,1)S(1)}, u32[]{:S(2)}, u32[]{:S(2)}) collective-permute-start(bf16[1056,256]{1,0:T(8,128)(2,1)S(1)} %collective-permute-done.38.refs_6_), channel_id=1, source_target_pairs={{0,8},{4,12},{8,0},{12,4},{16,24},{20,28},{24,16},{28,20},{1,9},{5... | collective-permute-start | bytes 1622024 | tf_op jit(solution)/shard_map/ppermute | solution.py:966
  220.4 23.8 %collective-permute-start.40 = (bf16[1056,256]{1,0:T(8,128)(2,1)S(1)}, bf16[1056,256]{1,0:T(8,128)(2,1)S(1)}, u32[]{:S(2)}, u32[]{:S(2)}) collective-permute-start(bf16[1056,256]{1,0:T(8,128)(2,1)S(1)} %copy-done.64), channel_id=1, source_target_pairs={{0,16},{4,20},{8,24},{12,28},{16,0},{20,4},{24,8},{28,12},{1,17},{... | collective-permute-start | bytes 1622024 | tf_op jit(solution)/shard_map/ppermute | solution.py:966
  244.2 25.1 %collective-permute-start.41 = (bf16[2,1056,256]{2,1,0:T(8,128)(2,1)}, bf16[2,1056,256]{2,1,0:T(8,128)(2,1)S(1)}, u32[]{:S(2)}, u32[]{:S(2)}) collective-permute-start(bf16[2,1056,256]{2,1,0:T(8,128)(2,1)} %get-tuple-element.799), channel_id=1, source_target_pairs={{0,16},{4,20},{8,24},{12,28},{16,0},{20,4},{24,8},{28,12},{1,17},{... | collective-permute-start | bytes 3244040 | tf_op jit(solution)/shard_map/ppermute | solution.py:966
  244.6 25.4 %collective-permute-start.42 = (bf16[2,1056,256]{2,1,0:T(8,128)(2,1)}, bf16[2,1056,256]{2,1,0:T(8,128)(2,1)S(1)}, u32[]{:S(2)}, u32[]{:S(2)}) collective-permute-start(bf16[2,1056,256]{2,1,0:T(8,128)(2,1)} %get-tuple-element.800), channel_id=1, source_target_pairs={{0,8},{4,12},{8,0},{12,4},{16,24},{20,28},{24,16},{28,20},{1,9},{5... | collective-permute-start | bytes 3244040 | tf_op jit(solution)/shard_map/ppermute | solution.py:966
  290.3 27.2 %collective-permute-start.48 = (bf16[1024,1024]{1,0:T(8,128)(2,1)S(1)}, bf16[1024,1024]{1,0:T(8,128)(2,1)}, u32[]{:S(2)}, u32[]{:S(2)}) collective-permute-start(bf16[1024,1024]{1,0:T(8,128)(2,1)S(1)} %copy-done.9), channel_id=1, source_target_pairs={{0,4},{4,0},{8,12},{12,8},{16,20},{20,16},{24,28},{28,24},{1,5},{5... | collective-permute-start | bytes 6291464 | tf_op jit(solution)/shard_map/ppermute | solution.py:963
  290.6 26.2 %collective-permute-start.46 = (bf16[2,1056,256]{2,1,0:T(8,128)(2,1)}, bf16[2,1056,256]{2,1,0:T(8,128)(2,1)S(1)}, u32[]{:S(2)}, u32[]{:S(2)}) collective-permute-start(bf16[2,1056,256]{2,1,0:T(8,128)(2,1)} %get-tuple-element.852), channel_id=1, source_target_pairs={{0,8},{4,12},{8,0},{12,4},{16,24},{20,28},{24,16},{28,20},{1,9},{5... | collective-permute-start | bytes 3244040 | tf_op jit(solution)/shard_map/ppermute | solution.py:966
  291.9 25.5 %collective-permute-start.47 = (bf16[2,1056,256]{2,1,0:T(8,128)(2,1)}, bf16[2,1056,256]{2,1,0:T(8,128)(2,1)}, u32[]{:S(2)}, u32[]{:S(2)}) collective-permute-start(bf16[2,1056,256]{2,1,0:T(8,128)(2,1)} %get-tuple-element.853), channel_id=1, source_target_pairs={{0,16},{4,20},{8,24},{12,28},{16,0},{20,4},{24,8},{28,12},{1,17},{... | collective-permute-start | bytes 3244040 | tf_op jit(solution)/shard_map/ppermute | solution.py:966
  321.8 34.2 %all-to-all-start.2 = ((bf16[4,256,512]{2,1,0:T(8,128)(2,1)}), bf16[4,256,512]{2,1,0:T(8,128)(2,1)S(1)}, u32[]{:S(2)}, u32[]{:S(2)}) async-start(bf16[4,256,512]{2,1,0:T(8,128)(2,1)} %bitcast.23), calls=%async_computation.2 | async-start | bytes 2097152 | tf_op jit(solution)/shard_map/all_to_all | solution.py:1390
  331.8 23.5 %collective-permute-start.49 = (bf16[1056,256]{1,0:T(8,128)(2,1)}, bf16[1056,256]{1,0:T(8,128)(2,1)S(1)}, u32[]{:S(2)}, u32[]{:S(2)}) collective-permute-start(bf16[1056,256]{1,0:T(8,128)(2,1)} %get-tuple-element.893), channel_id=1, source_target_pairs={{0,16},{4,20},{8,24},{12,28},{16,0},{20,4},{24,8},{28,12},{1,17},{... | collective-permute-start | bytes 1622024 | tf_op jit(solution)/shard_map/ppermute | solution.py:966
  333.2 22.9 %collective-permute-start.50 = (bf16[1056,256]{1,0:T(8,128)(2,1)}, bf16[1056,256]{1,0:T(8,128)(2,1)}, u32[]{:S(2)}, u32[]{:S(2)}) collective-permute-start(bf16[1056,256]{1,0:T(8,128)(2,1)} %get-tuple-element.895), channel_id=1, source_target_pairs={{0,8},{4,12},{8,0},{12,4},{16,24},{20,28},{24,16},{28,20},{1,9},{5... | collective-permute-start | bytes 1622024 | tf_op jit(solution)/shard_map/ppermute | solution.py:966
  358.2 36.2 %collective-permute-start.53 = (bf16[1056,256]{1,0:T(8,128)(2,1)}, bf16[1056,256]{1,0:T(8,128)(2,1)}, u32[]{:S(2)}, u32[]{:S(2)}) collective-permute-start(bf16[1056,256]{1,0:T(8,128)(2,1)} %add_convert_fusion.2), channel_id=1, source_target_pairs={{0,1},{1,2},{2,3},{3,0},{4,5},{5,6},{6,7},{7,4},{8,9},{9,10},{10,1... | collective-permute-start | bytes 1622024 | tf_op jit(solution)/shard_map/ppermute | solution.py:969
  374.0 35.9 %collective-permute-start.54 = (bf16[2,912,256]{2,1,0:T(8,128)(2,1)}, bf16[2,912,256]{2,1,0:T(8,128)(2,1)}, u32[]{:S(2)}, u32[]{:S(2)}) collective-permute-start(bf16[2,912,256]{2,1,0:T(8,128)(2,1)} %get-tuple-element.949), channel_id=1, source_target_pairs={{0,8},{4,12},{8,0},{12,4},{16,24},{20,28},{24,16},{28,20},{1,9},{5... | collective-permute-start | bytes 2801672 | tf_op jit(solution)/shard_map/ppermute | solution.py:966
  394.4 113.1 %collective-permute-start.51 = (bf16[2,256,512]{2,1,0:T(8,128)(2,1)}, bf16[2,256,512]{2,1,0:T(8,128)(2,1)}, u32[]{:S(2)}, u32[]{:S(2)}) collective-permute-start(bf16[2,256,512]{2,1,0:T(8,128)(2,1)} %constant_dynamic-slice_fusion.14), channel_id=1, source_target_pairs={{0,4},{4,0},{8,12},{12,8},{16,20},{20,16},{24,28},{28,24},{1,5},{5... | collective-permute-start | bytes 1572872 | tf_op jit(solution)/shard_map/ppermute | solution.py:963
  395.3 47.8 %collective-permute-start.55 = (bf16[2,912,256]{2,1,0:T(8,128)(2,1)}, bf16[2,912,256]{2,1,0:T(8,128)(2,1)S(1)}, u32[]{:S(2)}, u32[]{:S(2)}) collective-permute-start(bf16[2,912,256]{2,1,0:T(8,128)(2,1)} %get-tuple-element.966), channel_id=1, source_target_pairs={{0,8},{4,12},{8,0},{12,4},{16,24},{20,28},{24,16},{28,20},{1,9},{5... | collective-permute-start | bytes 2801672 | tf_op jit(solution)/shard_map/ppermute | solution.py:966
  409.9 34.8 %collective-permute-start.58 = (bf16[2,912,256]{2,1,0:T(8,128)(2,1)}, bf16[2,912,256]{2,1,0:T(8,128)(2,1)}, u32[]{:S(2)}, u32[]{:S(2)}) collective-permute-start(bf16[2,912,256]{2,1,0:T(8,128)(2,1)} %get-tuple-element.983), channel_id=1, source_target_pairs={{0,16},{4,20},{8,24},{12,28},{16,0},{20,4},{24,8},{28,12},{1,17},{... | collective-permute-start | bytes 2801672 | tf_op jit(solution)/shard_map/ppermute | solution.py:966
  411.7 23.3 %collective-permute-start.57 = (bf16[1056,256]{1,0:T(8,128)(2,1)}, bf16[1056,256]{1,0:T(8,128)(2,1)}, u32[]{:S(2)}, u32[]{:S(2)}) collective-permute-start(bf16[1056,256]{1,0:T(8,128)(2,1)} %add_convert_fusion.1), channel_id=1, source_target_pairs={{0,3},{1,0},{2,1},{3,2},{4,7},{5,4},{6,5},{7,6},{8,11},{9,8},{10,9... | collective-permute-start | bytes 1622024 | tf_op jit(solution)/shard_map/ppermute | solution.py:969
  418.4 24.7 %collective-permute-start.56 = (bf16[912,256]{1,0:T(8,128)(2,1)}, bf16[912,256]{1,0:T(8,128)(2,1)}, u32[]{:S(2)}, u32[]{:S(2)}) collective-permute-start(bf16[912,256]{1,0:T(8,128)(2,1)} %get-tuple-element.970), channel_id=1, source_target_pairs={{0,16},{4,20},{8,24},{12,28},{16,0},{20,4},{24,8},{28,12},{1,17},{... | collective-permute-start | bytes 1400840 | tf_op jit(solution)/shard_map/ppermute | solution.py:966
  475.4 34.3 %collective-permute-start.75 = (bf16[3,352,128]{2,1,0:T(8,128)(2,1)}, bf16[3,352,128]{2,1,0:T(8,128)(2,1)S(1)}, u32[]{:S(2)}, u32[]{:S(2)}) collective-permute-start(bf16[3,352,128]{2,1,0:T(8,128)(2,1)} %constant_dynamic-slice_fusion), channel_id=1, source_target_pairs={{0,4},{4,0},{8,12},{12,8},{16,20},{20,16},{24,28},{28,24},{1,5},{5... | collective-permute-start | bytes 811016 | tf_op jit(solution)/shard_map/ppermute | solution.py:963
  478.7 34.6 %collective-permute-start.68 = (bf16[2,912,256]{2,1,0:T(8,128)(2,1)}, bf16[2,912,256]{2,1,0:T(8,128)(2,1)}, u32[]{:S(2)}, u32[]{:S(2)}) collective-permute-start(bf16[2,912,256]{2,1,0:T(8,128)(2,1)} %get-tuple-element.1020), channel_id=1, source_target_pairs={{0,8},{4,12},{8,0},{12,4},{16,24},{20,28},{24,16},{28,20},{1,9},{5... | collective-permute-start | bytes 2801672 | tf_op jit(solution)/shard_map/ppermute | solution.py:966
  481.0 22.0 %collective-permute-start.66 = (bf16[912,256]{1,0:T(8,128)(2,1)S(1)}, bf16[912,256]{1,0:T(8,128)(2,1)S(1)}, u32[]{:S(2)}, u32[]{:S(2)}) collective-permute-start(bf16[912,256]{1,0:T(8,128)(2,1)S(1)} %add_convert_fusion.9), channel_id=1, source_target_pairs={{0,3},{1,0},{2,1},{3,2},{4,7},{5,4},{6,5},{7,6},{8,11},{9,8},{10,9... | collective-permute-start | bytes 1400840 | tf_op jit(solution)/shard_map/ppermute | solution.py:969
  503.8 29.7 %all-to-all-start.3 = ((bf16[4,256,512]{2,1,0:T(8,128)(2,1)}), bf16[4,256,512]{2,1,0:T(8,128)(2,1)S(1)}, u32[]{:S(2)}, u32[]{:S(2)}) async-start(bf16[4,256,512]{2,1,0:T(8,128)(2,1)} %bitcast.24), calls=%async_computation.3 | async-start | bytes 2097152 | tf_op jit(solution)/shard_map/all_to_all | solution.py:1468
  (124 other events, 1756.6 us)

commit v3 on v2

--- a/solution.py
+++ b/solution.py
@@ -1042,7 +1042,7 @@
 
 
 def first_bit(at, r, late=False):
-    return at.chips // 2 if r == 3 or (r == 0 and not late) else 1
+    return at.chips // 2 if r == 3 or r == (2 if late else 0) else 1
 
 
 class Scatter:
@@ -1424,20 +1424,16 @@
         f_rs.home(1)
         m_rs.cross(1)
         run_back(3)
-        far = {r: m_rs.far[r] for r in (2, 3)}
-        dps, m_rs.near, far, ds = sync(dps, m_rs.near, far, ds)
-        m_rs.far.update(far)
-        m_rs.fold(2)
+        dps, m_rs.near, m_rs.far, ds = sync(dps, m_rs.near, m_rs.far, ds)
+        m_rs.fold(1, 2)
         m_rs.cross(3)
         run_back(0)
-        far = {r: m_rs.far[r] for r in (0, 1)}
+        far = {0: m_rs.far[0]}
         dps, m_rs.near, far, m_rs.two, f_rs.end = sync(dps, m_rs.near, far, m_rs.two, f_rs.end)
         m_rs.far.update(far)
-        m_rs.close(2)
-        sums = m_rs.add(1, 3)
-        dps, m_rs.one, sums = sync(dps, m_rs.one, sums)
+        m_rs.close(1, 2)
+        dps, m_rs.one = sync(dps, m_rs.one)
         m_rs.merge(2)
-        m_rs.pass_on(sums)
         m_rs.cross(0)
     else:
         for h in range(heads):
@@ -1445,11 +1441,12 @@
     output = settle(out_came)
     da, g_gain1 = input_back([dps[h] for h in range(heads)], m_parts, x)
     if fast:
-        da, g_gain1, m_rs.two, m_rs.end = sync(da, g_gain1, m_rs.two, m_rs.end)
-        m_rs.close(1, 3)
+        far = {3: m_rs.far[3]}
+        da, g_gain1, far, m_rs.end = sync(da, g_gain1, far, m_rs.end)
+        m_rs.far.update(far)
         m_rs.join(2)
         m_rs.home(1)
-        m_rs.home(3)
+        m_rs.fold(3)
     da_other = at.swap(da)
     d_x_norm = rms_back(x.astype(F32), gain1, da.astype(F32) + da_other.astype(F32))
     dx_home = give_back(d_mix.astype(F32) + d_x_norm)
@@ -1461,6 +1458,8 @@
     sums = jnp.concatenate([conv_all, decay_all, gains, g_gain_o], axis=0)
     if fast:
         dx_home, sums, m_rs.near, m_rs.end = sync(dx_home, at.line_sum(sums), m_rs.near, m_rs.end)
+        m_rs.close(3)
+        m_rs.home(3)
         m_rs.fold(0)
         sums = at.chip_sum(sums)
     else:

time: 548 us -> 537 us (0.980)
  waiting for transfers between devices: 112 us -> 97.9 us
    ppermute x15, waiting for transfers between devices: 31.1 us -> 20.5 us  [turn(): lax.ppermute(value, 'tp', [(i, (i + r) % self.n_t) for i in range(self.n_...]
    unnamed x158 -> x160, local copies, waits for them, and re-layouts: 11.6 us -> 11.3 us
  transfers between devices with their start and end apart: 80 -> 80, of which waited for: 32 -> 31; matrix products, arithmetic and copies ran while one was open for 9% -> 9% of each run, Pallas kernels for 47% -> 48%
where the time goes in v3:
time: 537 us; the launch traced here: 528 us
  Pallas kernels  259 us (48%)
  waiting for transfers between devices  97.9 us (18%)
  starting transfers between devices  95 us (18%)
  other arithmetic  50.3 us (9%)
  local copies, waits for them, and re-layouts  22 us (4%)
    ppermute x44, waiting for transfers between devices, move(): lax.ppermute(value, 'fsdp', [(i, i ^ 2 * bit) for i in range(self.n_f)])  66.3 us
    pallas_call x4, Pallas kernels, project_back(): pl.pallas_call(functools.partial(project_back_kernel, pieces, bit, h), ou...  55.4 us
    ppermute x44, starting transfers between devices, move(): lax.ppermute(value, 'fsdp', [(i, i ^ 2 * bit) for i in range(self.n_f)])  47 us
    pallas_call x2, Pallas kernels, ffn(): pl.pallas_call(functools.partial(ffn_kernel, pieces, chunks, bits, bool(m...  45.3 us
    pallas_call x2, Pallas kernels, recur_back(): pl.pallas_call(functools.partial(recur_back_kernel, heads, len(done)), ou...  41.5 us
    pallas_call x4, Pallas kernels, project(): pl.pallas_call(functools.partial(project_kernel, pieces, h), out_shape=[j...  31.8 us
    pallas_call x2, Pallas kernels, recur(): pl.pallas_call(functools.partial(recur_kernel, heads, len(more)), out_sha...  28.8 us
    ppermute x15, starting transfers between devices, turn(): lax.ppermute(value, 'tp', [(i, (i + r) % self.n_t) for i in range(self.n_...  23 us
  transfers between devices with their start and end apart: 80, of which 31 were waited for; matrix products, arithmetic and copies ran while one was open for 9% of the time, Pallas kernels for 48%

profile of v3, /device:TPU:0, one launch (start us, length us, event | category | flops | bytes accessed | tf_op | source)
XLA Modules:
  0.0 527.6 jit_solution(4445009749217671307)
XLA Ops:
  9.2 6.4 %all-to-all-start = ((bf16[4,256,512]{2,1,0:T(8,128)(2,1)}), bf16[4,256,512]{2,1,0:T(8,128)(2,1)S(1)}, u32[]{:S(2)}, u32[]{:S(2)}) async-start(bf16[4,256,512]{2,1,0:T(8,128)(2,1)} %pad_maximum_fusion.1), calls=%async_computation | async-start | bytes 2097152 | tf_op jit(solution)/shard_map/all_to_all | solution.py:993
  25.9 6.5 %collective-permute-done.2.refs_1_.refs_5_ = bf16[912,256]{1,0:T(8,128)(2,1)S(1)} collective-permute-done((bf16[912,256]{1,0:T(8,128)(2,1)S(1)}, bf16[912,256]{1,0:T(8,128)(2,1)S(1)}, u32[]{:S(2)}, u32[]{:S(2)}) %collective-permute-start.2) | collective-permute-done | bytes 466976 | tf_op jit(solution)/shard_map/ppermute | solution.py:966
  32.5 10.3 %collective-permute-done.3.refs_2_.refs_6_ = bf16[912,256]{1,0:T(8,128)(2,1)S(1)} collective-permute-done((bf16[912,256]{1,0:T(8,128)(2,1)S(1)}, bf16[912,256]{1,0:T(8,128)(2,1)S(1)}, u32[]{:S(2)}, u32[]{:S(2)}) %collective-permute-start.3) | collective-permute-done | bytes 466976 | tf_op jit(solution)/shard_map/ppermute | solution.py:966
  52.7 7.9 %project.4 = (bf16[1024,640]{1,0:T(8,128)(2,1)}, bf16[1024,128]{1,0:T(8,128)(2,1)}, bf16[1024,128]{1,0:T(8,128)(2,1)}, bf16[2048,128]{1,0:T(8,128)(2,1)}, bf16[2...) custom-call(f32[4,2]{1,0:T(4,128)} %pad_maximum_fusion.10.scal_ref, bf16[1024,1024]{1,0:T(8,128)(2,1)} %fusion.9.a_ref, ...), custom_call_target="tpu_custom_call" | custom-call | flops 1644167168 | bytes 8000000 | tf_op jit(solution)/shard_map/project/pallas_call | solution.py:172
  60.6 7.2 %collective-permute-done.8.refs_0_.refs_12_.refs_16_ = bf16[912,256]{1,0:T(8,128)(2,1)} collective-permute-done((bf16[912,256]{1,0:T(8,128)(2,1)S(1)}, bf16[912,256]{1,0:T(8,128)(2,1)}, u32[]{:S(2)}, u32[]{:S(2)}) %collective-permute-start.8) | collective-permute-done | bytes 466976 | tf_op jit(solution)/shard_map/ppermute | solution.py:969
  73.4 4.3 select_blocks.2
  83.7 6.7 %collective-permute-done.15.refs_1_.refs_13_.refs_17_ = bf16[912,256]{1,0:T(8,128)(2,1)S(1)} collective-permute-done((bf16[912,256]{1,0:T(8,128)(2,1)}, bf16[912,256]{1,0:T(8,128)(2,1)S(1)}, u32[]{:S(2)}, u32[]{:S(2)}) %collective-permute-start.15) | collective-permute-done | bytes 466976 | tf_op jit(solution)/shard_map/ppermute | solution.py:966
  94.9 8.9 %collective-permute-done.17.refs_3_.refs_7_.refs_11_ = bf16[912,256]{1,0:T(8,128)(2,1)S(1)} collective-permute-done((bf16[912,256]{1,0:T(8,128)(2,1)S(1)}, bf16[912,256]{1,0:T(8,128)(2,1)S(1)}, u32[]{:S(2)}, u32[]{:S(2)}) %collective-permute-start.17) | collective-permute-done | bytes 466976 | tf_op jit(solution)/shard_map/ppermute | solution.py:966
  110.6 8.0 %project.6 = (bf16[1024,640]{1,0:T(8,128)(2,1)}, bf16[1024,128]{1,0:T(8,128)(2,1)}, bf16[1024,128]{1,0:T(8,128)(2,1)}, bf16[2048,128]{1,0:T(8,128)(2,1)}, bf16[2...) custom-call(f32[4,2]{1,0:T(4,128)} %pad_maximum_fusion.10.scal_ref, bf16[1024,1024]{1,0:T(8,128)(2,1)} %fusion.9.a_ref, ...), custom_call_target="tpu_custom_call" | custom-call | flops 1644167168 | bytes 8000000 | tf_op jit(solution)/shard_map/project/pallas_call | solution.py:172
  118.6 8.0 %project.5 = (bf16[1024,640]{1,0:T(8,128)(2,1)}, bf16[1024,128]{1,0:T(8,128)(2,1)}, bf16[1024,128]{1,0:T(8,128)(2,1)}, bf16[2048,128]{1,0:T(8,128)(2,1)}, bf16[2...) custom-call(f32[4,2]{1,0:T(4,128)} %pad_maximum_fusion.10.scal_ref, bf16[1024,1024]{1,0:T(8,128)(2,1)} %fusion.9.a_ref, ...), custom_call_target="tpu_custom_call" | custom-call | flops 1644167168 | bytes 8000000 | tf_op jit(solution)/shard_map/project/pallas_call | solution.py:172
  133.0 4.5 select_blocks.3
  146.3 8.0 %project.7 = (bf16[1024,640]{1,0:T(8,128)(2,1)}, bf16[1024,128]{1,0:T(8,128)(2,1)}, bf16[1024,128]{1,0:T(8,128)(2,1)}, bf16[2048,128]{1,0:T(8,128)(2,1)}, bf16[2...) custom-call(f32[4,2]{1,0:T(4,128)} %pad_maximum_fusion.10.scal_ref, bf16[1024,1024]{1,0:T(8,128)(2,1)} %fusion.9.a_ref, ...), custom_call_target="tpu_custom_call" | custom-call | flops 1644167168 | bytes 8000000 | tf_op jit(solution)/shard_map/project/pallas_call | solution.py:172
  162.4 14.4 %recur.2 = (bf16[1024,512]{1,0:T(8,128)(2,1)}, f32[4,128,128]{2,1,0:T(8,128)}, bf16[512,128]{1,0:T(8,128)(2,1)}, bf16[512,128]{1,0:T(8,128)(2,1)}, bf16[512,128]...) custom-call(f32[1,128]{1,0:T(1,128)} %bitcast.110, ...), custom_call_target="tpu_custom_call" | custom-call | flops 2688000000 | bytes 1000000 | tf_op jit(solution)/shard_map/recur/pallas_call | solution.py:346
  183.6 14.4 %recur.3 = (bf16[1024,512]{1,0:T(8,128)(2,1)}, f32[4,128,128]{2,1,0:T(8,128)}, bf16[512,128]{1,0:T(8,128)(2,1)}, bf16[512,128]{1,0:T(8,128)(2,1)}, bf16[512,128]...) custom-call(f32[1,128]{1,0:T(1,128)} %bitcast.111, ...), custom_call_target="tpu_custom_call", output_to_operand_aliasing={{0}: (22, {})} | custom-call | flops 2688000000 | bytes 1000000 | tf_op jit(solution)/shard_map/recur/pallas_call | solution.py:346
  198.1 5.3 mix_out.1
  222.1 22.0 %ffn.2 = (f32[1024,1024]{1,0:T(8,128)}, f32[1024,1024]{1,0:T(8,128)}, bf16[2,1056,256]{2,1,0:T(8,128)(2,1)}, bf16[2,1056,256]{2,1,0:T(8,128)(2,1)}, bf16[2,1056,...) custom-call(bf16[1024,1024]{1,0:T(8,128)(2,1)} %multiply_convert_fusion.1.b_ref, ...), custom_call_target="tpu_custom_call" | custom-call | flops 13287555072 | bytes 1000000 | tf_op jit(solution)/shard_map/ffn/pallas_call | solution.py:928
  246.0 23.3 %ffn.3 = (bf16[1024,1024]{1,0:T(8,128)(2,1)}, bf16[1024,1024]{1,0:T(8,128)(2,1)}, bf16[2,1056,256]{2,1,0:T(8,128)(2,1)}, bf16[2,1056,256]{2,1,0:T(8,128)(2,1)}, ...) custom-call(bf16[1024,1024]{1,0:T(8,128)(2,1)} %multiply_convert_fusion.1.b_ref, ...), custom_call_target="tpu_custom_call" | custom-call | flops 13287555072 | bytes 1000000 | tf_op jit(solution)/shard_map/ffn/pallas_call | solution.py:928
  270.9 4.4 add_stacks.5
  279.1 10.2 %mix_back.1 = (bf16[1024,1024]{1,0:T(8,128)(2,1)}, bf16[1024,512]{1,0:T(8,128)(2,1)}, f32[1,1024]{1,0:T(1,128)}, bf16[128,256]{1,0:T(8,128)(2,1)}, bf16[128,256]...) custom-call(f32[1,1024]{1,0:T(1,128)} %bitcast.97, ...), custom_call_target="tpu_custom_call" | custom-call | flops 2147483648 | bytes 1000000 | tf_op jit(solution)/shard_map/mix_back/pallas_call | solution.py:797
  292.9 20.8 %recur_back.2 = (bf16[1024,768]{1,0:T(8,128)(2,1)}, bf16[1024,768]{1,0:T(8,128)(2,1)}, bf16[1024,768]{1,0:T(8,128)(2,1)}, bf16[1024,768]{1,0:T(8,128)(2,1)}, f32...) custom-call(f32[1,128]{1,0:T(1,128)} %bitcast.112, ...), custom_call_target="tpu_custom_call" | custom-call | flops 4032000000 | bytes 1000000 | tf_op jit(solution)/shard_map/recur_back/pallas_call | solution.py:505
  322.5 5.3 %all-to-all-start.2 = ((bf16[4,256,512]{2,1,0:T(8,128)(2,1)}), bf16[4,256,512]{2,1,0:T(8,128)(2,1)S(1)}, u32[]{:S(2)}, u32[]{:S(2)}) async-start(bf16[4,256,512]{2,1,0:T(8,128)(2,1)} %bitcast.23), calls=%async_computation.2 | async-start | bytes 2097152 | tf_op jit(solution)/shard_map/all_to_all | solution.py:1390
  327.9 4.4 add_stacks.6
  334.8 20.7 %recur_back.3 = (bf16[1024,768]{1,0:T(8,128)(2,1)}, bf16[1024,768]{1,0:T(8,128)(2,1)}, bf16[1024,768]{1,0:T(8,128)(2,1)}, bf16[1024,768]{1,0:T(8,128)(2,1)}, f32...) custom-call(f32[1,128]{1,0:T(1,128)} %bitcast.113, ...), custom_call_target="tpu_custom_call", output_to_operand_aliasing={{0}: (33, {}), {1}: (34, {}), {2}: (35, {}), {3}: (36, {}),... | custom-call | flops 4032000000 | bytes 1000000 | tf_op jit(solution)/shard_map/recur_back/pallas_call | solution.py:505
  364.6 13.9 %project_back.4 = (bf16[1024,784]{1,0:T(8,128)(2,1)}, f32[8,640]{1,0:T(8,128)}, f32[8,128]{1,0:T(8,128)}, bf16[2,912,256]{2,1,0:T(8,128)(2,1)}, bf16[2,912,256]{2,1,0:T(8,128)(2,1)}) custom-call(f32[4,2]{1,0:T(4,128)} %pad_maximum_fusion.10.scal_ref, bf16[1024,1024]{1,0:T(8,128)(2,1)} %fusion.9.a_ref, f32[4,8,640]{2,1,0:T(8,128)} %select_reduce_fusion.cw_ref, ...), custom_call_target="tpu_custom_call" | custom-call | flops 1644167168 | bytes 1000000 | tf_op jit(solution)/shard_map/project_back/pallas_call | solution.py:639
  379.0 13.7 %project_back.5 = (bf16[1024,784]{1,0:T(8,128)(2,1)}, f32[8,640]{1,0:T(8,128)}, f32[8,128]{1,0:T(8,128)}, bf16[2,912,256]{2,1,0:T(8,128)(2,1)}, bf16[2,912,256]{2,1,0:T(8,128)(2,1)}) custom-call(f32[4,2]{1,0:T(4,128)} %pad_maximum_fusion.10.scal_ref, bf16[1024,1024]{1,0:T(8,128)(2,1)} %fusion.9.a_ref, f32[4,8,640]{2,1,0:T(8,128)} %select_reduce_fusion.cw_ref, ...), custom_call_target="tpu_custom_call" | custom-call | flops 1644167168 | bytes 1000000 | tf_op jit(solution)/shard_map/project_back/pallas_call | solution.py:639
  400.8 14.1 %project_back.6 = (bf16[1024,784]{1,0:T(8,128)(2,1)}, f32[8,640]{1,0:T(8,128)}, f32[8,128]{1,0:T(8,128)}, bf16[2,912,256]{2,1,0:T(8,128)(2,1)}, bf16[2,912,256]{2,1,0:T(8,128)(2,1)}) custom-call(f32[4,2]{1,0:T(4,128)} %pad_maximum_fusion.10.scal_ref, bf16[1024,1024]{1,0:T(8,128)(2,1)} %fusion.9.a_ref, f32[4,8,640]{2,1,0:T(8,128)} %select_reduce_fusion.cw_ref, ...), custom_call_target="tpu_custom_call" | custom-call | flops 1644167168 | bytes 1000000 | tf_op jit(solution)/shard_map/project_back/pallas_call | solution.py:639
  422.7 13.7 %project_back.7 = (bf16[1024,784]{1,0:T(8,128)(2,1)}, f32[8,640]{1,0:T(8,128)}, f32[8,128]{1,0:T(8,128)}, bf16[2,912,256]{2,1,0:T(8,128)(2,1)}, bf16[2,912,256]{2,1,0:T(8,128)(2,1)}) custom-call(f32[4,2]{1,0:T(4,128)} %pad_maximum_fusion.10.scal_ref, bf16[1024,1024]{1,0:T(8,128)(2,1)} %fusion.9.a_ref, f32[4,8,640]{2,1,0:T(8,128)} %select_reduce_fusion.cw_ref, ...), custom_call_target="tpu_custom_call" | custom-call | flops 1644167168 | bytes 1000000 | tf_op jit(solution)/shard_map/project_back/pallas_call | solution.py:639
  441.5 13.2 %input_back.1 = (bf16[1024,1024]{1,0:T(8,128)(2,1)}, f32[1,1024]{1,0:T(1,128)}) custom-call(bf16[1024,784]{1,0:T(8,128)(2,1)} %get-tuple-element.979.refs_0_, bf16[1024,784]{1,0:T(8,128)(2,1)} %get-tuple-element.980.refs_1_, bf16[1024,784]{1,0:T(8,128)(2,1)} %get-tuple-element.981.refs_2_, bf16[1024,784]{1,0:T(8,128)(2,1)} %get-tuple-element.982.refs_3_, ...), custom_call_target="tpu_custom_call" | custom-call | flops 6576668672 | bytes 1000000 | tf_op jit(solution)/shard_map/input_back/pallas_call | solution.py:705
  476.8 4.6 collective-permute-done.65
  481.5 5.2 all-to-all-start.3
  494.6 8.5 %collective-permute-done.68 = bf16[912,256]{1,0:T(8,128)(2,1)S(1)} collective-permute-done((bf16[912,256]{1,0:T(8,128)(2,1)}, bf16[912,256]{1,0:T(8,128)(2,1)S(1)}, u32[]{:S(2)}, u32[]{:S(2)}) %collective-permute-start.68) | collective-permute-done | bytes 466976 | tf_op jit(solution)/shard_map/ppermute | solution.py:966
  511.1 7.8 %collective-permute-done.73 = f32[185,128]{1,0:T(8,128)S(1)} collective-permute-done((f32[185,128]{1,0:T(8,128)S(1)}, f32[185,128]{1,0:T(8,128)S(1)}, u32[]{:S(2)}, u32[]{:S(2)}) %collective-permute-start.73) | collective-permute-done | bytes 94752 | tf_op jit(solution)/shard_map/ppermute | solution.py:1000
  (428 shorter events, 198.0 us)
Async XLA Ops:
  9.2 33.6 %all-to-all-start = ((bf16[4,256,512]{2,1,0:T(8,128)(2,1)}), bf16[4,256,512]{2,1,0:T(8,128)(2,1)S(1)}, u32[]{:S(2)}, u32[]{:S(2)}) async-start(bf16[4,256,512]{2,1,0:T(8,128)(2,1)} %pad_maximum_fusion.1), calls=%async_computation | async-start | bytes 2097152 | tf_op jit(solution)/shard_map/all_to_all | solution.py:993
  20.4 22.4 %collective-permute-start.3 = (bf16[912,256]{1,0:T(8,128)(2,1)S(1)}, bf16[912,256]{1,0:T(8,128)(2,1)S(1)}, u32[]{:S(2)}, u32[]{:S(2)}) collective-permute-start(bf16[912,256]{1,0:T(8,128)(2,1)S(1)} %pad_maximum_fusion.6.refs_0_.refs_4_), channel_id=1, source_target_pairs={{0,16},{4,20},{8,24},{12,28},{16,0},{20,4},{24,8},{28,12},{1,17},{... | collective-permute-start | bytes 1400840 | tf_op jit(solution)/shard_map/ppermute | solution.py:966
  21.9 20.8 %collective-permute-start.4 = (bf16[912,256]{1,0:T(8,128)(2,1)S(1)}, bf16[912,256]{1,0:T(8,128)(2,1)}, u32[]{:S(2)}, u32[]{:S(2)}) collective-permute-start(bf16[912,256]{1,0:T(8,128)(2,1)S(1)} %pad_maximum_fusion.6.refs_0_.refs_4_), channel_id=1, source_target_pairs={{0,24},{4,28},{8,16},{12,20},{16,8},{20,12},{24,0},{28,4},{1,25},{... | collective-permute-start | bytes 1400840 | tf_op jit(solution)/shard_map/ppermute | solution.py:966
  44.9 22.9 %collective-permute-start.8 = (bf16[912,256]{1,0:T(8,128)(2,1)S(1)}, bf16[912,256]{1,0:T(8,128)(2,1)}, u32[]{:S(2)}, u32[]{:S(2)}) collective-permute-start(bf16[912,256]{1,0:T(8,128)(2,1)S(1)} %pad_maximum_fusion.6.refs_0_.refs_4_), channel_id=1, source_target_pairs={{0,3},{1,0},{2,1},{3,2},{4,7},{5,4},{6,5},{7,6},{8,11},{9,8},{10,9... | collective-permute-start | bytes 1400840 | tf_op jit(solution)/shard_map/ppermute | solution.py:969
  46.9 20.9 %collective-permute-start.10 = (bf16[4,256,256]{2,1,0:T(8,128)(2,1)S(1)}, bf16[4,256,256]{2,1,0:T(8,128)(2,1)S(1)}, u32[]{:S(2)}, u32[]{:S(2)}) collective-permute-start(bf16[4,256,256]{2,1,0:T(8,128)(2,1)S(1)} %get-tuple-element.640.refs_2_.refs_3_), channel_id=1, source_target_pairs={{0,16},{4,20},{8,24},{12,28},{16,0},{20,4},{24,8},{28,12},{1,17},{... | collective-permute-start | bytes 1572872 | tf_op jit(solution)/shard_map/ppermute | solution.py:966
  70.8 19.6 %collective-permute-start.15 = (bf16[912,256]{1,0:T(8,128)(2,1)}, bf16[912,256]{1,0:T(8,128)(2,1)S(1)}, u32[]{:S(2)}, u32[]{:S(2)}) collective-permute-start(bf16[912,256]{1,0:T(8,128)(2,1)} %collective-permute-done.8.refs_0_.refs_12_.refs_16_), channel_id=1, source_target_pairs={{0,8},{4,12},{8,0},{12,4},{16,24},{20,28},{24,16},{28,20},{1,9},{5... | collective-permute-start | bytes 1400840 | tf_op jit(solution)/shard_map/ppermute | solution.py:966
  106.4 22.5 %collective-permute-start.22 = (bf16[1056,256]{1,0:T(8,128)(2,1)S(1)}, bf16[1056,256]{1,0:T(8,128)(2,1)}, u32[]{:S(2)}, u32[]{:S(2)}) collective-permute-start(bf16[1056,256]{1,0:T(8,128)(2,1)S(1)} %bitcast.92), channel_id=1, source_target_pairs={{0,3},{1,0},{2,1},{3,2},{4,7},{5,4},{6,5},{7,6},{8,11},{9,8},{10,9... | collective-permute-start | bytes 1622024 | tf_op jit(solution)/shard_map/ppermute | solution.py:969
  106.5 22.4 %collective-permute-start.23 = (bf16[4,256,256]{2,1,0:T(8,128)(2,1)}, bf16[4,256,256]{2,1,0:T(8,128)(2,1)}, u32[]{:S(2)}, u32[]{:S(2)}) collective-permute-start(bf16[4,256,256]{2,1,0:T(8,128)(2,1)} %get-tuple-element.603), channel_id=1, source_target_pairs={{0,16},{4,20},{8,24},{12,28},{16,0},{20,4},{24,8},{28,12},{1,17},{... | collective-permute-start | bytes 1572872 | tf_op jit(solution)/shard_map/ppermute | solution.py:966
  108.1 20.9 %collective-permute-start.24 = (bf16[4,256,256]{2,1,0:T(8,128)(2,1)}, bf16[4,256,256]{2,1,0:T(8,128)(2,1)}, u32[]{:S(2)}, u32[]{:S(2)}) collective-permute-start(bf16[4,256,256]{2,1,0:T(8,128)(2,1)} %get-tuple-element.604), channel_id=1, source_target_pairs={{0,8},{4,12},{8,0},{12,4},{16,24},{20,28},{24,16},{28,20},{1,9},{5... | collective-permute-start | bytes 1572872 | tf_op jit(solution)/shard_map/ppermute | solution.py:966
  108.8 20.1 %collective-permute-start.20 = (bf16[912,256]{1,0:T(8,128)(2,1)S(1)}, bf16[912,256]{1,0:T(8,128)(2,1)S(1)}, u32[]{:S(2)}, u32[]{:S(2)}) collective-permute-start(bf16[912,256]{1,0:T(8,128)(2,1)S(1)} %collective-permute-done.14.refs_0_.refs_8_.refs_12_), channel_id=1, source_target_pairs={{0,8},{4,12},{8,0},{12,4},{16,24},{20,28},{24,16},{28,20},{1,9},{5... | collective-permute-start | bytes 1400840 | tf_op jit(solution)/shard_map/ppermute | solution.py:966
  140.7 40.7 %all-to-all-start.1 = ((bf16[4,256,512]{2,1,0:T(8,128)(2,1)}), bf16[4,256,512]{2,1,0:T(8,128)(2,1)S(1)}, u32[]{:S(2)}, u32[]{:S(2)}) async-start(bf16[4,256,512]{2,1,0:T(8,128)(2,1)} %select_blocks.3), calls=%async_computation.1 | async-start | bytes 2097152 | tf_op jit(solution)/shard_map/all_to_all | solution.py:993
  160.6 20.8 %collective-permute-start.31 = (bf16[1056,256]{1,0:T(8,128)(2,1)}, bf16[1056,256]{1,0:T(8,128)(2,1)}, u32[]{:S(2)}, u32[]{:S(2)}) collective-permute-start(bf16[1056,256]{1,0:T(8,128)(2,1)} %collective-permute-done.19.refs_4_), channel_id=1, source_target_pairs={{0,16},{4,20},{8,24},{12,28},{16,0},{20,4},{24,8},{28,12},{1,17},{... | collective-permute-start | bytes 1622024 | tf_op jit(solution)/shard_map/ppermute | solution.py:966
  219.7 24.4 %collective-permute-start.39 = (bf16[1056,256]{1,0:T(8,128)(2,1)S(1)}, bf16[1056,256]{1,0:T(8,128)(2,1)S(1)}, u32[]{:S(2)}, u32[]{:S(2)}) collective-permute-start(bf16[1056,256]{1,0:T(8,128)(2,1)S(1)} %collective-permute-done.38.refs_6_), channel_id=1, source_target_pairs={{0,8},{4,12},{8,0},{12,4},{16,24},{20,28},{24,16},{28,20},{1,9},{5... | collective-permute-start | bytes 1622024 | tf_op jit(solution)/shard_map/ppermute | solution.py:966
  220.4 23.8 %collective-permute-start.40 = (bf16[1056,256]{1,0:T(8,128)(2,1)S(1)}, bf16[1056,256]{1,0:T(8,128)(2,1)S(1)}, u32[]{:S(2)}, u32[]{:S(2)}) collective-permute-start(bf16[1056,256]{1,0:T(8,128)(2,1)S(1)} %copy-done.65), channel_id=1, source_target_pairs={{0,16},{4,20},{8,24},{12,28},{16,0},{20,4},{24,8},{28,12},{1,17},{... | collective-permute-start | bytes 1622024 | tf_op jit(solution)/shard_map/ppermute | solution.py:966
  244.2 25.0 %collective-permute-start.41 = (bf16[2,1056,256]{2,1,0:T(8,128)(2,1)}, bf16[2,1056,256]{2,1,0:T(8,128)(2,1)S(1)}, u32[]{:S(2)}, u32[]{:S(2)}) collective-permute-start(bf16[2,1056,256]{2,1,0:T(8,128)(2,1)} %get-tuple-element.793), channel_id=1, source_target_pairs={{0,16},{4,20},{8,24},{12,28},{16,0},{20,4},{24,8},{28,12},{1,17},{... | collective-permute-start | bytes 3244040 | tf_op jit(solution)/shard_map/ppermute | solution.py:966
  244.6 25.3 %collective-permute-start.42 = (bf16[2,1056,256]{2,1,0:T(8,128)(2,1)}, bf16[2,1056,256]{2,1,0:T(8,128)(2,1)S(1)}, u32[]{:S(2)}, u32[]{:S(2)}) collective-permute-start(bf16[2,1056,256]{2,1,0:T(8,128)(2,1)} %get-tuple-element.794), channel_id=1, source_target_pairs={{0,8},{4,12},{8,0},{12,4},{16,24},{20,28},{24,16},{28,20},{1,9},{5... | collective-permute-start | bytes 3244040 | tf_op jit(solution)/shard_map/ppermute | solution.py:966
  290.5 27.6 %collective-permute-start.48 = (bf16[1024,1024]{1,0:T(8,128)(2,1)S(1)}, bf16[1024,1024]{1,0:T(8,128)(2,1)}, u32[]{:S(2)}, u32[]{:S(2)}) collective-permute-start(bf16[1024,1024]{1,0:T(8,128)(2,1)S(1)} %copy-done.9), channel_id=1, source_target_pairs={{0,4},{4,0},{8,12},{12,8},{16,20},{20,16},{24,28},{28,24},{1,5},{5... | collective-permute-start | bytes 6291464 | tf_op jit(solution)/shard_map/ppermute | solution.py:963
  290.5 26.5 %collective-permute-start.46 = (bf16[2,1056,256]{2,1,0:T(8,128)(2,1)}, bf16[2,1056,256]{2,1,0:T(8,128)(2,1)S(1)}, u32[]{:S(2)}, u32[]{:S(2)}) collective-permute-start(bf16[2,1056,256]{2,1,0:T(8,128)(2,1)} %get-tuple-element.846), channel_id=1, source_target_pairs={{0,8},{4,12},{8,0},{12,4},{16,24},{20,28},{24,16},{28,20},{1,9},{5... | collective-permute-start | bytes 3244040 | tf_op jit(solution)/shard_map/ppermute | solution.py:966
  291.9 26.3 %collective-permute-start.47 = (bf16[2,1056,256]{2,1,0:T(8,128)(2,1)}, bf16[2,1056,256]{2,1,0:T(8,128)(2,1)}, u32[]{:S(2)}, u32[]{:S(2)}) collective-permute-start(bf16[2,1056,256]{2,1,0:T(8,128)(2,1)} %get-tuple-element.847), channel_id=1, source_target_pairs={{0,16},{4,20},{8,24},{12,28},{16,0},{20,4},{24,8},{28,12},{1,17},{... | collective-permute-start | bytes 3244040 | tf_op jit(solution)/shard_map/ppermute | solution.py:966
  322.5 33.9 %all-to-all-start.2 = ((bf16[4,256,512]{2,1,0:T(8,128)(2,1)}), bf16[4,256,512]{2,1,0:T(8,128)(2,1)S(1)}, u32[]{:S(2)}, u32[]{:S(2)}) async-start(bf16[4,256,512]{2,1,0:T(8,128)(2,1)} %bitcast.23), calls=%async_computation.2 | async-start | bytes 2097152 | tf_op jit(solution)/shard_map/all_to_all | solution.py:1390
  332.2 23.4 %collective-permute-start.49 = (bf16[1056,256]{1,0:T(8,128)(2,1)}, bf16[1056,256]{1,0:T(8,128)(2,1)S(1)}, u32[]{:S(2)}, u32[]{:S(2)}) collective-permute-start(bf16[1056,256]{1,0:T(8,128)(2,1)} %get-tuple-element.887), channel_id=1, source_target_pairs={{0,16},{4,20},{8,24},{12,28},{16,0},{20,4},{24,8},{28,12},{1,17},{... | collective-permute-start | bytes 1622024 | tf_op jit(solution)/shard_map/ppermute | solution.py:966
  333.3 23.2 %collective-permute-start.50 = (bf16[1056,256]{1,0:T(8,128)(2,1)}, bf16[1056,256]{1,0:T(8,128)(2,1)}, u32[]{:S(2)}, u32[]{:S(2)}) collective-permute-start(bf16[1056,256]{1,0:T(8,128)(2,1)} %get-tuple-element.889), channel_id=1, source_target_pairs={{0,8},{4,12},{8,0},{12,4},{16,24},{20,28},{24,16},{28,20},{1,9},{5... | collective-permute-start | bytes 1622024 | tf_op jit(solution)/shard_map/ppermute | solution.py:966
  358.6 34.1 %collective-permute-start.53 = (bf16[1056,256]{1,0:T(8,128)(2,1)}, bf16[1056,256]{1,0:T(8,128)(2,1)}, u32[]{:S(2)}, u32[]{:S(2)}) collective-permute-start(bf16[1056,256]{1,0:T(8,128)(2,1)} %add_convert_fusion.2), channel_id=1, source_target_pairs={{0,1},{1,2},{2,3},{3,0},{4,5},{5,6},{6,7},{7,4},{8,9},{9,10},{10,1... | collective-permute-start | bytes 1622024 | tf_op jit(solution)/shard_map/ppermute | solution.py:969
  362.8 29.9 %collective-permute-start.52 = (bf16[1056,256]{1,0:T(8,128)(2,1)}, bf16[1056,256]{1,0:T(8,128)(2,1)}, u32[]{:S(2)}, u32[]{:S(2)}) collective-permute-start(bf16[1056,256]{1,0:T(8,128)(2,1)} %add_convert_fusion.3), channel_id=1, source_target_pairs={{0,3},{1,0},{2,1},{3,2},{4,7},{5,4},{6,5},{7,6},{8,11},{9,8},{10,9... | collective-permute-start | bytes 1622024 | tf_op jit(solution)/shard_map/ppermute | solution.py:969
  378.6 36.3 %collective-permute-start.55 = (bf16[2,912,256]{2,1,0:T(8,128)(2,1)}, bf16[2,912,256]{2,1,0:T(8,128)(2,1)S(1)}, u32[]{:S(2)}, u32[]{:S(2)}) collective-permute-start(bf16[2,912,256]{2,1,0:T(8,128)(2,1)} %get-tuple-element.944), channel_id=1, source_target_pairs={{0,16},{4,20},{8,24},{12,28},{16,0},{20,4},{24,8},{28,12},{1,17},{... | collective-permute-start | bytes 2801672 | tf_op jit(solution)/shard_map/ppermute | solution.py:966
  392.7 22.2 %collective-permute-start.54 = (bf16[2,912,256]{2,1,0:T(8,128)(2,1)}, bf16[2,912,256]{2,1,0:T(8,128)(2,1)}, u32[]{:S(2)}, u32[]{:S(2)}) collective-permute-start(bf16[2,912,256]{2,1,0:T(8,128)(2,1)} %get-tuple-element.943), channel_id=1, source_target_pairs={{0,8},{4,12},{8,0},{12,4},{16,24},{20,28},{24,16},{28,20},{1,9},{5... | collective-permute-start | bytes 2801672 | tf_op jit(solution)/shard_map/ppermute | solution.py:966
  396.7 25.5 %collective-permute-start.51 = (bf16[2,256,512]{2,1,0:T(8,128)(2,1)S(1)}, bf16[2,256,512]{2,1,0:T(8,128)(2,1)S(1)}, u32[]{:S(2)}, u32[]{:S(2)}) collective-permute-start(bf16[2,256,512]{2,1,0:T(8,128)(2,1)S(1)} %constant_dynamic-slice_fusion.14), channel_id=1, source_target_pairs={{0,4},{4,0},{8,12},{12,8},{16,20},{20,16},{24,28},{28,24},{1,5},{5... | collective-permute-start | bytes 1572872 | tf_op jit(solution)/shard_map/ppermute | solution.py:963
  398.8 39.3 %collective-permute-start.58 = (bf16[1056,256]{1,0:T(8,128)(2,1)}, bf16[1056,256]{1,0:T(8,128)(2,1)S(1)}, u32[]{:S(2)}, u32[]{:S(2)}) collective-permute-start(bf16[1056,256]{1,0:T(8,128)(2,1)} %add_convert_fusion.1), channel_id=1, source_target_pairs={{0,3},{1,0},{2,1},{3,2},{4,7},{5,4},{6,5},{7,6},{8,11},{9,8},{10,9... | collective-permute-start | bytes 1622024 | tf_op jit(solution)/shard_map/ppermute | solution.py:969
  422.3 32.4 %collective-permute-start.59 = (bf16[2,912,256]{2,1,0:T(8,128)(2,1)}, bf16[2,912,256]{2,1,0:T(8,128)(2,1)S(1)}, u32[]{:S(2)}, u32[]{:S(2)}) collective-permute-start(bf16[2,912,256]{2,1,0:T(8,128)(2,1)} %get-tuple-element.985), channel_id=1, source_target_pairs={{0,16},{4,20},{8,24},{12,28},{16,0},{20,4},{24,8},{28,12},{1,17},{... | collective-permute-start | bytes 2801672 | tf_op jit(solution)/shard_map/ppermute | solution.py:966
  457.3 35.0 %collective-permute-start.75 = (bf16[3,352,128]{2,1,0:T(8,128)(2,1)}, bf16[3,352,128]{2,1,0:T(8,128)(2,1)S(1)}, u32[]{:S(2)}, u32[]{:S(2)}) collective-permute-start(bf16[3,352,128]{2,1,0:T(8,128)(2,1)} %constant_dynamic-slice_fusion), channel_id=1, source_target_pairs={{0,4},{4,0},{8,12},{12,8},{16,20},{20,16},{24,28},{28,24},{1,5},{5... | collective-permute-start | bytes 811016 | tf_op jit(solution)/shard_map/ppermute | solution.py:963
  465.5 39.6 %collective-permute-start.66 = (bf16[2,912,256]{2,1,0:T(8,128)(2,1)}, bf16[2,912,256]{2,1,0:T(8,128)(2,1)}, u32[]{:S(2)}, u32[]{:S(2)}) collective-permute-start(bf16[2,912,256]{2,1,0:T(8,128)(2,1)} %get-tuple-element.1005), channel_id=1, source_target_pairs={{0,8},{4,12},{8,0},{12,4},{16,24},{20,28},{24,16},{28,20},{1,9},{5... | collective-permute-start | bytes 2801672 | tf_op jit(solution)/shard_map/ppermute | solution.py:966
  481.5 39.7 %all-to-all-start.3 = ((bf16[4,256,512]{2,1,0:T(8,128)(2,1)}), bf16[4,256,512]{2,1,0:T(8,128)(2,1)S(1)}, u32[]{:S(2)}, u32[]{:S(2)}) async-start(bf16[4,256,512]{2,1,0:T(8,128)(2,1)} %bitcast.24), calls=%async_computation.3 | async-start | bytes 2097152 | tf_op jit(solution)/shard_map/all_to_all | solution.py:1467
  (125 other events, 1700.1 us)

commit v4 on v3

--- a/solution.py
+++ b/solution.py
@@ -1249,7 +1249,6 @@
         for r, (ask, keep), part in zip(routes, extra, (cot_both[:, :, :quarter], cot_both[:, :, quarter:])):
             r.ask, r.keep, r.have = ask, keep, [part]
         m.turn(1)
-        m.turn(3)
         for r in routes:
             r.step()
         x = sequence(came)
@@ -1258,11 +1257,14 @@
         state = route_state()
         m.parts, f.parts, state, proj[0], normed_one, x = sync(m.parts, f.parts, state, proj[0], normed_one, x)
         set_routes(state)
-        for r in (1, 3):
-            m.move(r, 1, 1)
-            m.move(r, 2, 2)
+        m.turn(3)
+        m.move(1, 1, 1)
+        m.move(1, 2, 2)
+        give = asked()
+        m.parts, f.parts, give = sync(m.parts, f.parts, give)
         m.turn(2, 1)
-        give = asked()
+        m.move(3, 1, 1)
+        m.move(3, 2, 2)
         m.parts, f.parts, give = sync(m.parts, f.parts, give)
         m.move(1, 3, 1)
         m.move(3, 3, 2)
@@ -1446,7 +1448,6 @@
         m_rs.far.update(far)
         m_rs.join(2)
         m_rs.home(1)
-        m_rs.fold(3)
     da_other = at.swap(da)
     d_x_norm = rms_back(x.astype(F32), gain1, da.astype(F32) + da_other.astype(F32))
     dx_home = give_back(d_mix.astype(F32) + d_x_norm)
@@ -1457,11 +1458,12 @@
     gains = jnp.concatenate([at.relative(g_gain1[0]), 0.5 * at.relative(g_gain2[0])]).reshape(-1, HD)
     sums = jnp.concatenate([conv_all, decay_all, gains, g_gain_o], axis=0)
     if fast:
-        dx_home, sums, m_rs.near, m_rs.end = sync(dx_home, at.line_sum(sums), m_rs.near, m_rs.end)
+        dx_home, sums, m_rs.near, m_rs.end = sync(dx_home, sums, m_rs.near, m_rs.end)
+        m_rs.fold(3)
         m_rs.close(3)
         m_rs.home(3)
         m_rs.fold(0)
-        sums = at.chip_sum(sums)
+        sums = at.chip_sum(at.line_sum(sums))
     else:
         sums = at.all_sum(sums)
     dx_came = lax.all_to_all(dx_home, "tp", split_axis=0, concat_axis=0, tiled=True)

time: 537 us -> 530 us (0.987)
  starting transfers between devices: 95 us -> 89 us
    ppermute x44, waiting for transfers between devices: 66.3 us -> 47.7 us  [move(): lax.ppermute(value, 'fsdp', [(i, i ^ 2 * bit) for i in range(self.n_f)])]
    all_to_all x1, waiting for transfers between devices: 0.38 us -> 6.95 us  [local(): lax.all_to_all(dx_home, 'tp', split_axis=0, concat_axis=0, tiled=True)]
    unnamed x160 -> x170, local copies, waits for them, and re-layouts: 11.3 us -> 12.1 us
  transfers between devices with their start and end apart: 80 -> 80, of which waited for: 31 -> 26; matrix products, arithmetic and copies ran while one was open for 9% -> 10% of each run, Pallas kernels for 48% -> 49%
where the time goes in v4:
time: 530 us; the launch traced here: 520 us
  Pallas kernels  259 us (49%)
  waiting for transfers between devices  93.3 us (18%)
  starting transfers between devices  89 us (17%)
  other arithmetic  53.2 us (10%)
  local copies, waits for them, and re-layouts  22.4 us (4%)
    pallas_call x4, Pallas kernels, project_back(): pl.pallas_call(functools.partial(project_back_kernel, pieces, bit, h), ou...  55.4 us
    ppermute x44, waiting for transfers between devices, move(): lax.ppermute(value, 'fsdp', [(i, i ^ 2 * bit) for i in range(self.n_f)])  47.7 us
    pallas_call x2, Pallas kernels, ffn(): pl.pallas_call(functools.partial(ffn_kernel, pieces, chunks, bits, bool(m...  45.2 us
    ppermute x44, starting transfers between devices, move(): lax.ppermute(value, 'fsdp', [(i, i ^ 2 * bit) for i in range(self.n_f)])  44.9 us
    pallas_call x2, Pallas kernels, recur_back(): pl.pallas_call(functools.partial(recur_back_kernel, heads, len(done)), ou...  41.6 us
    pallas_call x4, Pallas kernels, project(): pl.pallas_call(functools.partial(project_kernel, pieces, h), out_shape=[j...  31.8 us
    pallas_call x2, Pallas kernels, recur(): pl.pallas_call(functools.partial(recur_kernel, heads, len(more)), out_sha...  28.8 us
    ppermute x15, waiting for transfers between devices, turn(): lax.ppermute(value, 'tp', [(i, (i + r) % self.n_t) for i in range(self.n_...  22.7 us
  transfers between devices with their start and end apart: 80, of which 26 were waited for; matrix products, arithmetic and copies ran while one was open for 10% of the time, Pallas kernels for 49%

profile of v4, /device:TPU:0, one launch (start us, length us, event | category | flops | bytes accessed | tf_op | source)
XLA Modules:
  0.0 520.3 jit_solution(8901434134152392497)
XLA Ops:
  8.8 6.4 %all-to-all-start = ((bf16[4,256,512]{2,1,0:T(8,128)(2,1)}), bf16[4,256,512]{2,1,0:T(8,128)(2,1)S(1)}, u32[]{:S(2)}, u32[]{:S(2)}) async-start(bf16[4,256,512]{2,1,0:T(8,128)(2,1)} %pad_maximum_fusion.1), calls=%async_computation | async-start | bytes 2097152 | tf_op jit(solution)/shard_map/all_to_all | solution.py:993
  25.1 6.8 %collective-permute-done.2.refs_1_.refs_5_ = bf16[912,256]{1,0:T(8,128)(2,1)S(1)} collective-permute-done((bf16[912,256]{1,0:T(8,128)(2,1)}, bf16[912,256]{1,0:T(8,128)(2,1)S(1)}, u32[]{:S(2)}, u32[]{:S(2)}) %collective-permute-start.2) | collective-permute-done | bytes 466976 | tf_op jit(solution)/shard_map/ppermute | solution.py:966
  31.9 10.3 %collective-permute-done.3.refs_2_.refs_6_ = bf16[912,256]{1,0:T(8,128)(2,1)S(1)} collective-permute-done((bf16[912,256]{1,0:T(8,128)(2,1)}, bf16[912,256]{1,0:T(8,128)(2,1)S(1)}, u32[]{:S(2)}, u32[]{:S(2)}) %collective-permute-start.3) | collective-permute-done | bytes 466976 | tf_op jit(solution)/shard_map/ppermute | solution.py:966
  50.2 7.9 %project.4 = (bf16[1024,640]{1,0:T(8,128)(2,1)}, bf16[1024,128]{1,0:T(8,128)(2,1)}, bf16[1024,128]{1,0:T(8,128)(2,1)}, bf16[2048,128]{1,0:T(8,128)(2,1)}, bf16[2...) custom-call(f32[4,2]{1,0:T(4,128)} %pad_maximum_fusion.10.scal_ref, bf16[1024,1024]{1,0:T(8,128)(2,1)} %fusion.9.a_ref, ...), custom_call_target="tpu_custom_call" | custom-call | flops 1644167168 | bytes 8000000 | tf_op jit(solution)/shard_map/project/pallas_call | solution.py:172
  64.4 4.3 select_blocks.2
  75.7 10.7 %collective-permute-done.14.refs_0_.refs_8_.refs_12_ = bf16[912,256]{1,0:T(8,128)(2,1)S(1)} collective-permute-done((bf16[912,256]{1,0:T(8,128)(2,1)}, bf16[912,256]{1,0:T(8,128)(2,1)S(1)}, u32[]{:S(2)}, u32[]{:S(2)}) %collective-permute-start.14) | collective-permute-done | bytes 466976 | tf_op jit(solution)/shard_map/ppermute | solution.py:969
  88.8 7.0 %collective-permute-done.17.refs_3_.refs_7_.refs_11_ = bf16[912,256]{1,0:T(8,128)(2,1)S(1)} collective-permute-done((bf16[912,256]{1,0:T(8,128)(2,1)S(1)}, bf16[912,256]{1,0:T(8,128)(2,1)S(1)}, u32[]{:S(2)}, u32[]{:S(2)}) %collective-permute-start.17) | collective-permute-done | bytes 466976 | tf_op jit(solution)/shard_map/ppermute | solution.py:966
  106.1 8.0 %project.6 = (bf16[1024,640]{1,0:T(8,128)(2,1)}, bf16[1024,128]{1,0:T(8,128)(2,1)}, bf16[1024,128]{1,0:T(8,128)(2,1)}, bf16[2048,128]{1,0:T(8,128)(2,1)}, bf16[2...) custom-call(f32[4,2]{1,0:T(4,128)} %pad_maximum_fusion.10.scal_ref, bf16[1024,1024]{1,0:T(8,128)(2,1)} %fusion.9.a_ref, ...), custom_call_target="tpu_custom_call" | custom-call | flops 1644167168 | bytes 8000000 | tf_op jit(solution)/shard_map/project/pallas_call | solution.py:172
  114.1 8.0 %project.5 = (bf16[1024,640]{1,0:T(8,128)(2,1)}, bf16[1024,128]{1,0:T(8,128)(2,1)}, bf16[1024,128]{1,0:T(8,128)(2,1)}, bf16[2048,128]{1,0:T(8,128)(2,1)}, bf16[2...) custom-call(f32[4,2]{1,0:T(4,128)} %pad_maximum_fusion.10.scal_ref, bf16[1024,1024]{1,0:T(8,128)(2,1)} %fusion.9.a_ref, ...), custom_call_target="tpu_custom_call" | custom-call | flops 1644167168 | bytes 8000000 | tf_op jit(solution)/shard_map/project/pallas_call | solution.py:172
  126.4 4.5 select_blocks.3
  130.9 4.2 collective-permute-done.25.refs_3_.refs_11_.refs_15_
  142.9 7.9 %project.7 = (bf16[1024,640]{1,0:T(8,128)(2,1)}, bf16[1024,128]{1,0:T(8,128)(2,1)}, bf16[1024,128]{1,0:T(8,128)(2,1)}, bf16[2048,128]{1,0:T(8,128)(2,1)}, bf16[2...) custom-call(f32[4,2]{1,0:T(4,128)} %pad_maximum_fusion.10.scal_ref, bf16[1024,1024]{1,0:T(8,128)(2,1)} %fusion.9.a_ref, ...), custom_call_target="tpu_custom_call" | custom-call | flops 1644167168 | bytes 8000000 | tf_op jit(solution)/shard_map/project/pallas_call | solution.py:172
  159.9 14.4 %recur.2 = (bf16[1024,512]{1,0:T(8,128)(2,1)}, f32[4,128,128]{2,1,0:T(8,128)}, bf16[512,128]{1,0:T(8,128)(2,1)}, bf16[512,128]{1,0:T(8,128)(2,1)}, bf16[512,128]...) custom-call(f32[1,128]{1,0:T(1,128)} %bitcast.109, ...), custom_call_target="tpu_custom_call" | custom-call | flops 2688000000 | bytes 1000000 | tf_op jit(solution)/shard_map/recur/pallas_call | solution.py:346
  181.4 14.4 %recur.3 = (bf16[1024,512]{1,0:T(8,128)(2,1)}, f32[4,128,128]{2,1,0:T(8,128)}, bf16[512,128]{1,0:T(8,128)(2,1)}, bf16[512,128]{1,0:T(8,128)(2,1)}, bf16[512,128]...) custom-call(f32[1,128]{1,0:T(1,128)} %bitcast.110, ...), custom_call_target="tpu_custom_call", output_to_operand_aliasing={{0}: (22, {})} | custom-call | flops 2688000000 | bytes 1000000 | tf_op jit(solution)/shard_map/recur/pallas_call | solution.py:346
  195.9 5.3 %mix_out.1 = bf16[1024,1024]{1,0:T(8,128)(2,1)} custom-call(bf16[1024,512]{1,0:T(8,128)(2,1)} %get-tuple-element.747.z_ref, bf16[912,256]{1,0:T(8,128)(2,1)} %pad_maximum_fusion.6.refs_0_.refs_4_, bf16[912,256]{1,0:T(8,128)(2,1)} %copy-done.13, bf16[912,256]{1,0:T(8,128)(2,1)} %copy-done.14, bf16[912,256]{1,0:T(8,128)(2,1)} %copy-done.15, ...), custom_call_target="tpu_custom_call" | custom-call | flops 1073741824 | bytes 1000000 | tf_op jit(solution)/shard_map/mix_out/pallas_call | solution.py:737
  218.4 22.0 %ffn.2 = (f32[1024,1024]{1,0:T(8,128)}, f32[1024,1024]{1,0:T(8,128)}, bf16[2,1056,256]{2,1,0:T(8,128)(2,1)}, bf16[2,1056,256]{2,1,0:T(8,128)(2,1)}, bf16[2,1056,...) custom-call(bf16[1024,1024]{1,0:T(8,128)(2,1)} %multiply_convert_fusion.1.b_ref, ...), custom_call_target="tpu_custom_call" | custom-call | flops 13287555072 | bytes 1000000 | tf_op jit(solution)/shard_map/ffn/pallas_call | solution.py:928
  242.8 23.2 %ffn.3 = (bf16[1024,1024]{1,0:T(8,128)(2,1)}, bf16[1024,1024]{1,0:T(8,128)(2,1)}, bf16[2,1056,256]{2,1,0:T(8,128)(2,1)}, bf16[2,1056,256]{2,1,0:T(8,128)(2,1)}, ...) custom-call(bf16[1024,1024]{1,0:T(8,128)(2,1)} %multiply_convert_fusion.1.b_ref, ...), custom_call_target="tpu_custom_call" | custom-call | flops 13287555072 | bytes 1000000 | tf_op jit(solution)/shard_map/ffn/pallas_call | solution.py:928
  267.6 4.4 add_stacks.5
  275.7 10.3 %mix_back.1 = (bf16[1024,1024]{1,0:T(8,128)(2,1)}, bf16[1024,512]{1,0:T(8,128)(2,1)}, f32[1,1024]{1,0:T(1,128)}, bf16[128,256]{1,0:T(8,128)(2,1)}, bf16[128,256]...) custom-call(f32[1,1024]{1,0:T(1,128)} %bitcast.97, ...), custom_call_target="tpu_custom_call" | custom-call | flops 2147483648 | bytes 1000000 | tf_op jit(solution)/shard_map/mix_back/pallas_call | solution.py:797
  288.2 20.8 %recur_back.2 = (bf16[1024,768]{1,0:T(8,128)(2,1)}, bf16[1024,768]{1,0:T(8,128)(2,1)}, bf16[1024,768]{1,0:T(8,128)(2,1)}, bf16[1024,768]{1,0:T(8,128)(2,1)}, f32...) custom-call(f32[1,128]{1,0:T(1,128)} %bitcast.111, ...), custom_call_target="tpu_custom_call" | custom-call | flops 4032000000 | bytes 1000000 | tf_op jit(solution)/shard_map/recur_back/pallas_call | solution.py:505
  309.0 4.9 collective-permute-done.46.refs_3_
  318.6 5.1 all-to-all-start.2
  323.7 4.3 add_stacks.6
  330.0 20.8 %recur_back.3 = (bf16[1024,768]{1,0:T(8,128)(2,1)}, bf16[1024,768]{1,0:T(8,128)(2,1)}, bf16[1024,768]{1,0:T(8,128)(2,1)}, bf16[1024,768]{1,0:T(8,128)(2,1)}, f32...) custom-call(f32[1,128]{1,0:T(1,128)} %bitcast.112, ...), custom_call_target="tpu_custom_call", output_to_operand_aliasing={{0}: (33, {}), {1}: (34, {}), {2}: (35, {}), {3}: (36, {}),... | custom-call | flops 4032000000 | bytes 1000000 | tf_op jit(solution)/shard_map/recur_back/pallas_call | solution.py:505
  359.8 13.9 %project_back.4 = (bf16[1024,784]{1,0:T(8,128)(2,1)}, f32[8,640]{1,0:T(8,128)}, f32[8,128]{1,0:T(8,128)}, bf16[2,912,256]{2,1,0:T(8,128)(2,1)}, bf16[2,912,256]{2,1,0:T(8,128)(2,1)}) custom-call(f32[4,2]{1,0:T(4,128)} %pad_maximum_fusion.10.scal_ref, bf16[1024,1024]{1,0:T(8,128)(2,1)} %fusion.9.a_ref, f32[4,8,640]{2,1,0:T(8,128)} %select_reduce_fusion.cw_ref, ...), custom_call_target="tpu_custom_call" | custom-call | flops 1644167168 | bytes 1000000 | tf_op jit(solution)/shard_map/project_back/pallas_call | solution.py:639
  375.6 13.7 %project_back.5 = (bf16[1024,784]{1,0:T(8,128)(2,1)}, f32[8,640]{1,0:T(8,128)}, f32[8,128]{1,0:T(8,128)}, bf16[2,912,256]{2,1,0:T(8,128)(2,1)}, bf16[2,912,256]{2,1,0:T(8,128)(2,1)}) custom-call(f32[4,2]{1,0:T(4,128)} %pad_maximum_fusion.10.scal_ref, bf16[1024,1024]{1,0:T(8,128)(2,1)} %fusion.9.a_ref, f32[4,8,640]{2,1,0:T(8,128)} %select_reduce_fusion.cw_ref, ...), custom_call_target="tpu_custom_call" | custom-call | flops 1644167168 | bytes 1000000 | tf_op jit(solution)/shard_map/project_back/pallas_call | solution.py:639
  397.2 14.1 %project_back.6 = (bf16[1024,784]{1,0:T(8,128)(2,1)}, f32[8,640]{1,0:T(8,128)}, f32[8,128]{1,0:T(8,128)}, bf16[2,912,256]{2,1,0:T(8,128)(2,1)}, bf16[2,912,256]{2,1,0:T(8,128)(2,1)}) custom-call(f32[4,2]{1,0:T(4,128)} %pad_maximum_fusion.10.scal_ref, bf16[1024,1024]{1,0:T(8,128)(2,1)} %fusion.9.a_ref, f32[4,8,640]{2,1,0:T(8,128)} %select_reduce_fusion.cw_ref, ...), custom_call_target="tpu_custom_call" | custom-call | flops 1644167168 | bytes 1000000 | tf_op jit(solution)/shard_map/project_back/pallas_call | solution.py:639
  421.0 13.7 %project_back.7 = (bf16[1024,784]{1,0:T(8,128)(2,1)}, f32[8,640]{1,0:T(8,128)}, f32[8,128]{1,0:T(8,128)}, bf16[2,912,256]{2,1,0:T(8,128)(2,1)}, bf16[2,912,256]{2,1,0:T(8,128)(2,1)}) custom-call(f32[4,2]{1,0:T(4,128)} %pad_maximum_fusion.10.scal_ref, bf16[1024,1024]{1,0:T(8,128)(2,1)} %fusion.9.a_ref, f32[4,8,640]{2,1,0:T(8,128)} %select_reduce_fusion.cw_ref, ...), custom_call_target="tpu_custom_call" | custom-call | flops 1644167168 | bytes 1000000 | tf_op jit(solution)/shard_map/project_back/pallas_call | solution.py:639
  438.1 13.1 %input_back.1 = (bf16[1024,1024]{1,0:T(8,128)(2,1)}, f32[1,1024]{1,0:T(1,128)}) custom-call(bf16[1024,784]{1,0:T(8,128)(2,1)} %get-tuple-element.1000.refs_0_, bf16[1024,784]{1,0:T(8,128)(2,1)} %get-tuple-element.1001.refs_1_, bf16[1024,784]{1,0:T(8,128)(2,1)} %get-tuple-element.1002.refs_2_, bf16[1024,784]{1,0:T(8,128)(2,1)} %get-tuple-element.1003.refs_3_, ...), custom_call_target="tpu_custom_call" | custom-call | flops 6576668672 | bytes 1000000 | tf_op jit(solution)/shard_map/input_back/pallas_call | solution.py:705
  488.4 5.3 %collective-permute-done.72 = f32[185,128]{1,0:T(8,128)S(1)} collective-permute-done((f32[185,128]{1,0:T(8,128)S(1)}, f32[185,128]{1,0:T(8,128)S(1)}, u32[]{:S(2)}, u32[]{:S(2)}) %collective-permute-start.72) | collective-permute-done | bytes 94752 | tf_op jit(solution)/shard_map/ppermute | solution.py:1000
  497.7 5.1 collective-permute-done.73
  507.0 7.0 %all-to-all-done.3 = bf16[4,256,512]{2,1,0:T(8,128)(2,1)S(1)} async-done(((bf16[4,256,512]{2,1,0:T(8,128)(2,1)}), bf16[4,256,512]{2,1,0:T(8,128)(2,1)S(1)}, u32[]{:S(2)}, u32[]{:S(2)}) %all-to-all-start.3) | async-done | bytes 1048608 | tf_op jit(solution)/shard_map/all_to_all | solution.py:1469
  (438 shorter events, 195.7 us)
Async XLA Ops:
  8.8 33.4 %all-to-all-start = ((bf16[4,256,512]{2,1,0:T(8,128)(2,1)}), bf16[4,256,512]{2,1,0:T(8,128)(2,1)S(1)}, u32[]{:S(2)}, u32[]{:S(2)}) async-start(bf16[4,256,512]{2,1,0:T(8,128)(2,1)} %pad_maximum_fusion.1), calls=%async_computation | async-start | bytes 2097152 | tf_op jit(solution)/shard_map/all_to_all | solution.py:993
  19.6 22.6 %collective-permute-start.3 = (bf16[912,256]{1,0:T(8,128)(2,1)}, bf16[912,256]{1,0:T(8,128)(2,1)S(1)}, u32[]{:S(2)}, u32[]{:S(2)}) collective-permute-start(bf16[912,256]{1,0:T(8,128)(2,1)} %pad_maximum_fusion.6.refs_0_.refs_4_), channel_id=1, source_target_pairs={{0,16},{4,20},{8,24},{12,28},{16,0},{20,4},{24,8},{28,12},{1,17},{... | collective-permute-start | bytes 1400840 | tf_op jit(solution)/shard_map/ppermute | solution.py:966
  21.1 21.0 %collective-permute-start.4 = (bf16[912,256]{1,0:T(8,128)(2,1)}, bf16[912,256]{1,0:T(8,128)(2,1)S(1)}, u32[]{:S(2)}, u32[]{:S(2)}) collective-permute-start(bf16[912,256]{1,0:T(8,128)(2,1)} %pad_maximum_fusion.6.refs_0_.refs_4_), channel_id=1, source_target_pairs={{0,24},{4,28},{8,16},{12,20},{16,8},{20,12},{24,0},{28,4},{1,25},{... | collective-permute-start | bytes 1400840 | tf_op jit(solution)/shard_map/ppermute | solution.py:966
  100.9 21.3 %collective-permute-start.22 = (bf16[1056,256]{1,0:T(8,128)(2,1)S(1)}, bf16[1056,256]{1,0:T(8,128)(2,1)}, u32[]{:S(2)}, u32[]{:S(2)}) collective-permute-start(bf16[1056,256]{1,0:T(8,128)(2,1)S(1)} %bitcast.92), channel_id=1, source_target_pairs={{0,3},{1,0},{2,1},{3,2},{4,7},{5,4},{6,5},{7,6},{8,11},{9,8},{10,9... | collective-permute-start | bytes 1622024 | tf_op jit(solution)/shard_map/ppermute | solution.py:969
  102.0 20.2 %collective-permute-start.23 = (bf16[4,256,256]{2,1,0:T(8,128)(2,1)}, bf16[4,256,256]{2,1,0:T(8,128)(2,1)}, u32[]{:S(2)}, u32[]{:S(2)}) collective-permute-start(bf16[4,256,256]{2,1,0:T(8,128)(2,1)} %get-tuple-element.624), channel_id=1, source_target_pairs={{0,16},{4,20},{8,24},{12,28},{16,0},{20,4},{24,8},{28,12},{1,17},{... | collective-permute-start | bytes 1572872 | tf_op jit(solution)/shard_map/ppermute | solution.py:966
  103.3 18.9 %collective-permute-start.24 = (bf16[4,256,256]{2,1,0:T(8,128)(2,1)}, bf16[4,256,256]{2,1,0:T(8,128)(2,1)}, u32[]{:S(2)}, u32[]{:S(2)}) collective-permute-start(bf16[4,256,256]{2,1,0:T(8,128)(2,1)} %get-tuple-element.625), channel_id=1, source_target_pairs={{0,8},{4,12},{8,0},{12,4},{16,24},{20,28},{24,16},{28,20},{1,9},{5... | collective-permute-start | bytes 1572872 | tf_op jit(solution)/shard_map/ppermute | solution.py:966
  135.9 41.5 %all-to-all-start.1 = ((bf16[4,256,512]{2,1,0:T(8,128)(2,1)}), bf16[4,256,512]{2,1,0:T(8,128)(2,1)S(1)}, u32[]{:S(2)}, u32[]{:S(2)}) async-start(bf16[4,256,512]{2,1,0:T(8,128)(2,1)} %select_blocks.3), calls=%async_computation.1 | async-start | bytes 2097152 | tf_op jit(solution)/shard_map/all_to_all | solution.py:993
  156.4 17.9 %collective-permute-start.29 = (bf16[1056,256]{1,0:T(8,128)(2,1)S(1)}, bf16[1056,256]{1,0:T(8,128)(2,1)S(1)}, u32[]{:S(2)}, u32[]{:S(2)}) collective-permute-start(bf16[1056,256]{1,0:T(8,128)(2,1)S(1)} %collective-permute-done.27.refs_1_), channel_id=1, source_target_pairs={{0,16},{4,20},{8,24},{12,28},{16,0},{20,4},{24,8},{28,12},{1,17},{... | collective-permute-start | bytes 1622024 | tf_op jit(solution)/shard_map/ppermute | solution.py:966
  158.4 19.0 %collective-permute-start.31 = (bf16[1056,256]{1,0:T(8,128)(2,1)S(1)}, bf16[1056,256]{1,0:T(8,128)(2,1)}, u32[]{:S(2)}, u32[]{:S(2)}) collective-permute-start(bf16[1056,256]{1,0:T(8,128)(2,1)S(1)} %copy-done.64), channel_id=1, source_target_pairs={{0,16},{4,20},{8,24},{12,28},{16,0},{20,4},{24,8},{28,12},{1,17},{... | collective-permute-start | bytes 1622024 | tf_op jit(solution)/shard_map/ppermute | solution.py:966
  177.4 18.4 %collective-permute-start.32 = (bf16[1056,256]{1,0:T(8,128)(2,1)}, bf16[1056,256]{1,0:T(8,128)(2,1)S(1)}, u32[]{:S(2)}, u32[]{:S(2)}) collective-permute-start(bf16[1056,256]{1,0:T(8,128)(2,1)} %collective-permute-done.31.refs_6_), channel_id=1, source_target_pairs={{0,8},{4,12},{8,0},{12,4},{16,24},{20,28},{24,16},{28,20},{1,9},{5... | collective-permute-start | bytes 1622024 | tf_op jit(solution)/shard_map/ppermute | solution.py:966
  216.5 23.9 %collective-permute-start.39 = (bf16[1056,256]{1,0:T(8,128)(2,1)S(1)}, bf16[1056,256]{1,0:T(8,128)(2,1)S(1)}, u32[]{:S(2)}, u32[]{:S(2)}) collective-permute-start(bf16[1056,256]{1,0:T(8,128)(2,1)S(1)} %collective-permute-done.38.refs_6_), channel_id=1, source_target_pairs={{0,8},{4,12},{8,0},{12,4},{16,24},{20,28},{24,16},{28,20},{1,9},{5... | collective-permute-start | bytes 1622024 | tf_op jit(solution)/shard_map/ppermute | solution.py:966
  218.1 22.4 %collective-permute-start.40 = (bf16[1056,256]{1,0:T(8,128)(2,1)S(1)}, bf16[1056,256]{1,0:T(8,128)(2,1)S(1)}, u32[]{:S(2)}, u32[]{:S(2)}) collective-permute-start(bf16[1056,256]{1,0:T(8,128)(2,1)S(1)} %copy-done.70), channel_id=1, source_target_pairs={{0,16},{4,20},{8,24},{12,28},{16,0},{20,4},{24,8},{28,12},{1,17},{... | collective-permute-start | bytes 1622024 | tf_op jit(solution)/shard_map/ppermute | solution.py:966
  240.5 25.6 %collective-permute-start.41 = (bf16[2,1056,256]{2,1,0:T(8,128)(2,1)}, bf16[2,1056,256]{2,1,0:T(8,128)(2,1)S(1)}, u32[]{:S(2)}, u32[]{:S(2)}) collective-permute-start(bf16[2,1056,256]{2,1,0:T(8,128)(2,1)} %get-tuple-element.814), channel_id=1, source_target_pairs={{0,16},{4,20},{8,24},{12,28},{16,0},{20,4},{24,8},{28,12},{1,17},{... | collective-permute-start | bytes 3244040 | tf_op jit(solution)/shard_map/ppermute | solution.py:966
  242.2 24.4 %collective-permute-start.42 = (bf16[2,1056,256]{2,1,0:T(8,128)(2,1)}, bf16[2,1056,256]{2,1,0:T(8,128)(2,1)S(1)}, u32[]{:S(2)}, u32[]{:S(2)}) collective-permute-start(bf16[2,1056,256]{2,1,0:T(8,128)(2,1)} %get-tuple-element.815), channel_id=1, source_target_pairs={{0,8},{4,12},{8,0},{12,4},{16,24},{20,28},{24,16},{28,20},{1,9},{5... | collective-permute-start | bytes 3244040 | tf_op jit(solution)/shard_map/ppermute | solution.py:966
  287.4 26.7 %collective-permute-start.48 = (bf16[1024,1024]{1,0:T(8,128)(2,1)S(1)}, bf16[1024,1024]{1,0:T(8,128)(2,1)}, u32[]{:S(2)}, u32[]{:S(2)}) collective-permute-start(bf16[1024,1024]{1,0:T(8,128)(2,1)S(1)} %copy-done.8), channel_id=1, source_target_pairs={{0,4},{4,0},{8,12},{12,8},{16,20},{20,16},{24,28},{28,24},{1,5},{5... | collective-permute-start | bytes 6291464 | tf_op jit(solution)/shard_map/ppermute | solution.py:963
  287.4 26.5 %collective-permute-start.46 = (bf16[2,1056,256]{2,1,0:T(8,128)(2,1)}, bf16[2,1056,256]{2,1,0:T(8,128)(2,1)S(1)}, u32[]{:S(2)}, u32[]{:S(2)}) collective-permute-start(bf16[2,1056,256]{2,1,0:T(8,128)(2,1)} %get-tuple-element.867), channel_id=1, source_target_pairs={{0,8},{4,12},{8,0},{12,4},{16,24},{20,28},{24,16},{28,20},{1,9},{5... | collective-permute-start | bytes 3244040 | tf_op jit(solution)/shard_map/ppermute | solution.py:966
  287.8 26.2 %collective-permute-start.47 = (bf16[2,1056,256]{2,1,0:T(8,128)(2,1)}, bf16[2,1056,256]{2,1,0:T(8,128)(2,1)}, u32[]{:S(2)}, u32[]{:S(2)}) collective-permute-start(bf16[2,1056,256]{2,1,0:T(8,128)(2,1)} %get-tuple-element.868), channel_id=1, source_target_pairs={{0,16},{4,20},{8,24},{12,28},{16,0},{20,4},{24,8},{28,12},{1,17},{... | collective-permute-start | bytes 3244040 | tf_op jit(solution)/shard_map/ppermute | solution.py:966
  318.6 33.1 %all-to-all-start.2 = ((bf16[4,256,512]{2,1,0:T(8,128)(2,1)}), bf16[4,256,512]{2,1,0:T(8,128)(2,1)S(1)}, u32[]{:S(2)}, u32[]{:S(2)}) async-start(bf16[4,256,512]{2,1,0:T(8,128)(2,1)} %bitcast.23), calls=%async_computation.2 | async-start | bytes 2097152 | tf_op jit(solution)/shard_map/all_to_all | solution.py:1392
  328.0 22.9 %collective-permute-start.49 = (bf16[1056,256]{1,0:T(8,128)(2,1)}, bf16[1056,256]{1,0:T(8,128)(2,1)S(1)}, u32[]{:S(2)}, u32[]{:S(2)}) collective-permute-start(bf16[1056,256]{1,0:T(8,128)(2,1)} %get-tuple-element.908), channel_id=1, source_target_pairs={{0,16},{4,20},{8,24},{12,28},{16,0},{20,4},{24,8},{28,12},{1,17},{... | collective-permute-start | bytes 1622024 | tf_op jit(solution)/shard_map/ppermute | solution.py:966
  328.3 23.4 %collective-permute-start.50 = (bf16[1056,256]{1,0:T(8,128)(2,1)}, bf16[1056,256]{1,0:T(8,128)(2,1)}, u32[]{:S(2)}, u32[]{:S(2)}) collective-permute-start(bf16[1056,256]{1,0:T(8,128)(2,1)} %get-tuple-element.910), channel_id=1, source_target_pairs={{0,8},{4,12},{8,0},{12,4},{16,24},{20,28},{24,16},{28,20},{1,9},{5... | collective-permute-start | bytes 1622024 | tf_op jit(solution)/shard_map/ppermute | solution.py:966
  353.9 35.4 %collective-permute-start.53 = (bf16[1056,256]{1,0:T(8,128)(2,1)}, bf16[1056,256]{1,0:T(8,128)(2,1)}, u32[]{:S(2)}, u32[]{:S(2)}) collective-permute-start(bf16[1056,256]{1,0:T(8,128)(2,1)} %add_convert_fusion.2), channel_id=1, source_target_pairs={{0,1},{1,2},{2,3},{3,0},{4,5},{5,6},{6,7},{7,4},{8,9},{9,10},{10,1... | collective-permute-start | bytes 1622024 | tf_op jit(solution)/shard_map/ppermute | solution.py:969
  358.0 31.2 %collective-permute-start.52 = (bf16[1056,256]{1,0:T(8,128)(2,1)}, bf16[1056,256]{1,0:T(8,128)(2,1)}, u32[]{:S(2)}, u32[]{:S(2)}) collective-permute-start(bf16[1056,256]{1,0:T(8,128)(2,1)} %add_convert_fusion.3), channel_id=1, source_target_pairs={{0,3},{1,0},{2,1},{3,2},{4,7},{5,4},{6,5},{7,6},{8,11},{9,8},{10,9... | collective-permute-start | bytes 1622024 | tf_op jit(solution)/shard_map/ppermute | solution.py:969
  373.8 37.4 %collective-permute-start.55 = (bf16[2,912,256]{2,1,0:T(8,128)(2,1)}, bf16[2,912,256]{2,1,0:T(8,128)(2,1)S(1)}, u32[]{:S(2)}, u32[]{:S(2)}) collective-permute-start(bf16[2,912,256]{2,1,0:T(8,128)(2,1)} %get-tuple-element.965), channel_id=1, source_target_pairs={{0,16},{4,20},{8,24},{12,28},{16,0},{20,4},{24,8},{28,12},{1,17},{... | collective-permute-start | bytes 2801672 | tf_op jit(solution)/shard_map/ppermute | solution.py:966
  389.2 22.0 %collective-permute-start.54 = (bf16[2,912,256]{2,1,0:T(8,128)(2,1)}, bf16[2,912,256]{2,1,0:T(8,128)(2,1)}, u32[]{:S(2)}, u32[]{:S(2)}) collective-permute-start(bf16[2,912,256]{2,1,0:T(8,128)(2,1)} %get-tuple-element.964), channel_id=1, source_target_pairs={{0,8},{4,12},{8,0},{12,4},{16,24},{20,28},{24,16},{28,20},{1,9},{5... | collective-permute-start | bytes 2801672 | tf_op jit(solution)/shard_map/ppermute | solution.py:966
  393.1 24.9 %collective-permute-start.51 = (bf16[2,256,512]{2,1,0:T(8,128)(2,1)S(1)}, bf16[2,256,512]{2,1,0:T(8,128)(2,1)S(1)}, u32[]{:S(2)}, u32[]{:S(2)}) collective-permute-start(bf16[2,256,512]{2,1,0:T(8,128)(2,1)S(1)} %constant_dynamic-slice_fusion.14), channel_id=1, source_target_pairs={{0,4},{4,0},{8,12},{12,8},{16,20},{20,16},{24,28},{28,24},{1,5},{5... | collective-permute-start | bytes 1572872 | tf_op jit(solution)/shard_map/ppermute | solution.py:963
  395.2 40.3 %collective-permute-start.58 = (bf16[1056,256]{1,0:T(8,128)(2,1)}, bf16[1056,256]{1,0:T(8,128)(2,1)}, u32[]{:S(2)}, u32[]{:S(2)}) collective-permute-start(bf16[1056,256]{1,0:T(8,128)(2,1)} %add_convert_fusion.1), channel_id=1, source_target_pairs={{0,3},{1,0},{2,1},{3,2},{4,7},{5,4},{6,5},{7,6},{8,11},{9,8},{10,9... | collective-permute-start | bytes 1622024 | tf_op jit(solution)/shard_map/ppermute | solution.py:969
  416.2 19.3 %collective-permute-start.56 = (bf16[912,256]{1,0:T(8,128)(2,1)}, bf16[912,256]{1,0:T(8,128)(2,1)S(1)}, u32[]{:S(2)}, u32[]{:S(2)}) collective-permute-start(bf16[912,256]{1,0:T(8,128)(2,1)} %get-tuple-element.986), channel_id=1, source_target_pairs={{0,16},{4,20},{8,24},{12,28},{16,0},{20,4},{24,8},{28,12},{1,17},{... | collective-permute-start | bytes 1400840 | tf_op jit(solution)/shard_map/ppermute | solution.py:966
  416.5 18.9 %collective-permute-start.57 = (bf16[912,256]{1,0:T(8,128)(2,1)}, bf16[912,256]{1,0:T(8,128)(2,1)}, u32[]{:S(2)}, u32[]{:S(2)}) collective-permute-start(bf16[912,256]{1,0:T(8,128)(2,1)} %get-tuple-element.988), channel_id=1, source_target_pairs={{0,8},{4,12},{8,0},{12,4},{16,24},{20,28},{24,16},{28,20},{1,9},{5... | collective-permute-start | bytes 1400840 | tf_op jit(solution)/shard_map/ppermute | solution.py:966
  419.3 32.0 %collective-permute-start.59 = (bf16[2,912,256]{2,1,0:T(8,128)(2,1)}, bf16[2,912,256]{2,1,0:T(8,128)(2,1)S(1)}, u32[]{:S(2)}, u32[]{:S(2)}) collective-permute-start(bf16[2,912,256]{2,1,0:T(8,128)(2,1)} %get-tuple-element.1006), channel_id=1, source_target_pairs={{0,16},{4,20},{8,24},{12,28},{16,0},{20,4},{24,8},{28,12},{1,17},{... | collective-permute-start | bytes 2801672 | tf_op jit(solution)/shard_map/ppermute | solution.py:966
  455.0 22.1 %collective-permute-start.75 = (bf16[3,352,128]{2,1,0:T(8,128)(2,1)}, bf16[3,352,128]{2,1,0:T(8,128)(2,1)S(1)}, u32[]{:S(2)}, u32[]{:S(2)}) collective-permute-start(bf16[3,352,128]{2,1,0:T(8,128)(2,1)} %constant_dynamic-slice_fusion), channel_id=1, source_target_pairs={{0,4},{4,0},{8,12},{12,8},{16,20},{20,16},{24,28},{28,24},{1,5},{5... | collective-permute-start | bytes 811016 | tf_op jit(solution)/shard_map/ppermute | solution.py:963
  455.5 29.4 %collective-permute-start.63 = (bf16[2,912,256]{2,1,0:T(8,128)(2,1)}, bf16[2,912,256]{2,1,0:T(8,128)(2,1)}, u32[]{:S(2)}, u32[]{:S(2)}) collective-permute-start(bf16[2,912,256]{2,1,0:T(8,128)(2,1)} %get-tuple-element.1027), channel_id=1, source_target_pairs={{0,8},{4,12},{8,0},{12,4},{16,24},{20,28},{24,16},{28,20},{1,9},{5... | collective-permute-start | bytes 2801672 | tf_op jit(solution)/shard_map/ppermute | solution.py:966
  473.5 40.4 %all-to-all-start.3 = ((bf16[4,256,512]{2,1,0:T(8,128)(2,1)}), bf16[4,256,512]{2,1,0:T(8,128)(2,1)S(1)}, u32[]{:S(2)}, u32[]{:S(2)}) async-start(bf16[4,256,512]{2,1,0:T(8,128)(2,1)} %bitcast.24), calls=%async_computation.3 | async-start | bytes 2097152 | tf_op jit(solution)/shard_map/all_to_all | solution.py:1469
  (130 other events, 1776.8 us)

commit v5 on v4

--- a/solution.py
+++ b/solution.py
@@ -1265,7 +1265,9 @@
         m.turn(2, 1)
         m.move(3, 1, 1)
         m.move(3, 2, 2)
-        m.parts, f.parts, give = sync(m.parts, f.parts, give)
+        early = without(m.parts, (2, 0))
+        early, f.parts, give = sync(early, f.parts, give)
+        m.parts.update(early)
         m.move(1, 3, 1)
         m.move(3, 3, 2)
         f.turn(1)

time: 530 us -> 538 us (1.015)
  waiting for transfers between devices: 93.3 us -> 100 us
    ppermute x15, waiting for transfers between devices: 22.7 us -> 29.6 us  [turn(): lax.ppermute(value, 'tp', [(i, (i + r) % self.n_t) for i in range(self.n_...]
  transfers between devices with their start and end apart: 80 -> 80, of which waited for: 26 -> 29; matrix products, arithmetic and copies ran while one was open for 10% -> 10% of each run, Pallas kernels for 49% -> 48%
where the time goes in v5:
time: 538 us; the launch traced here: 529 us
  Pallas kernels  259 us (48%)
  waiting for transfers between devices  100 us (19%)
  starting transfers between devices  90.8 us (17%)
  other arithmetic  53 us (10%)
  local copies, waits for them, and re-layouts  22.6 us (4%)
    pallas_call x4, Pallas kernels, project_back(): pl.pallas_call(functools.partial(project_back_kernel, pieces, bit, h), ou...  55.4 us
    ppermute x44, waiting for transfers between devices, move(): lax.ppermute(value, 'fsdp', [(i, i ^ 2 * bit) for i in range(self.n_f)])  50.4 us
    ppermute x44, starting transfers between devices, move(): lax.ppermute(value, 'fsdp', [(i, i ^ 2 * bit) for i in range(self.n_f)])  45.9 us
    pallas_call x2, Pallas kernels, ffn(): pl.pallas_call(functools.partial(ffn_kernel, pieces, chunks, bits, bool(m...  45.2 us
    pallas_call x2, Pallas kernels, recur_back(): pl.pallas_call(functools.partial(recur_back_kernel, heads, len(done)), ou...  41.6 us
    pallas_call x4, Pallas kernels, project(): pl.pallas_call(functools.partial(project_kernel, pieces, h), out_shape=[j...  31.8 us
    ppermute x15, waiting for transfers between devices, turn(): lax.ppermute(value, 'tp', [(i, (i + r) % self.n_t) for i in range(self.n_...  29.6 us
    pallas_call x2, Pallas kernels, recur(): pl.pallas_call(functools.partial(recur_kernel, heads, len(more)), out_sha...  28.8 us
  transfers between devices with their start and end apart: 80, of which 29 were waited for; matrix products, arithmetic and copies ran while one was open for 10% of the time, Pallas kernels for 48%

profile of v5, /device:TPU:0, one launch (start us, length us, event | category | flops | bytes accessed | tf_op | source)
XLA Modules:
  0.0 528.7 jit_solution(3017784609827785810)
XLA Ops:
  8.8 6.4 %all-to-all-start = ((bf16[4,256,512]{2,1,0:T(8,128)(2,1)}), bf16[4,256,512]{2,1,0:T(8,128)(2,1)S(1)}, u32[]{:S(2)}, u32[]{:S(2)}) async-start(bf16[4,256,512]{2,1,0:T(8,128)(2,1)} %pad_maximum_fusion.1), calls=%async_computation | async-start | bytes 2097152 | tf_op jit(solution)/shard_map/all_to_all | solution.py:993
  25.1 6.8 %collective-permute-done.2.refs_1_.refs_5_ = bf16[912,256]{1,0:T(8,128)(2,1)S(1)} collective-permute-done((bf16[912,256]{1,0:T(8,128)(2,1)}, bf16[912,256]{1,0:T(8,128)(2,1)S(1)}, u32[]{:S(2)}, u32[]{:S(2)}) %collective-permute-start.2) | collective-permute-done | bytes 466976 | tf_op jit(solution)/shard_map/ppermute | solution.py:966
  31.9 10.3 %collective-permute-done.3.refs_2_.refs_6_ = bf16[912,256]{1,0:T(8,128)(2,1)S(1)} collective-permute-done((bf16[912,256]{1,0:T(8,128)(2,1)}, bf16[912,256]{1,0:T(8,128)(2,1)S(1)}, u32[]{:S(2)}, u32[]{:S(2)}) %collective-permute-start.3) | collective-permute-done | bytes 466976 | tf_op jit(solution)/shard_map/ppermute | solution.py:966
  50.2 7.9 %project.4 = (bf16[1024,640]{1,0:T(8,128)(2,1)}, bf16[1024,128]{1,0:T(8,128)(2,1)}, bf16[1024,128]{1,0:T(8,128)(2,1)}, bf16[2048,128]{1,0:T(8,128)(2,1)}, bf16[2...) custom-call(f32[4,2]{1,0:T(4,128)} %pad_maximum_fusion.10.scal_ref, bf16[1024,1024]{1,0:T(8,128)(2,1)} %fusion.9.a_ref, ...), custom_call_target="tpu_custom_call" | custom-call | flops 1644167168 | bytes 8000000 | tf_op jit(solution)/shard_map/project/pallas_call | solution.py:172
  64.4 4.3 select_blocks.2
  75.2 8.6 %collective-permute-done.14.refs_1_.refs_13_.refs_17_ = bf16[912,256]{1,0:T(8,128)(2,1)S(1)} collective-permute-done((bf16[912,256]{1,0:T(8,128)(2,1)S(1)}, bf16[912,256]{1,0:T(8,128)(2,1)S(1)}, u32[]{:S(2)}, u32[]{:S(2)}) %collective-permute-start.14) | collective-permute-done | bytes 466976 | tf_op jit(solution)/shard_map/ppermute | solution.py:966
  89.1 20.3 %collective-permute-done.17.refs_0_.refs_8_.refs_12_ = bf16[912,256]{1,0:T(8,128)(2,1)S(1)} collective-permute-done((bf16[912,256]{1,0:T(8,128)(2,1)}, bf16[912,256]{1,0:T(8,128)(2,1)S(1)}, u32[]{:S(2)}, u32[]{:S(2)}) %collective-permute-start.17) | collective-permute-done | bytes 466976 | tf_op jit(solution)/shard_map/ppermute | solution.py:969
  114.2 8.0 %project.6 = (bf16[1024,640]{1,0:T(8,128)(2,1)}, bf16[1024,128]{1,0:T(8,128)(2,1)}, bf16[1024,128]{1,0:T(8,128)(2,1)}, bf16[2048,128]{1,0:T(8,128)(2,1)}, bf16[2...) custom-call(f32[4,2]{1,0:T(4,128)} %pad_maximum_fusion.10.scal_ref, bf16[1024,1024]{1,0:T(8,128)(2,1)} %fusion.9.a_ref, ...), custom_call_target="tpu_custom_call" | custom-call | flops 1644167168 | bytes 8000000 | tf_op jit(solution)/shard_map/project/pallas_call | solution.py:172
  122.2 8.0 %project.5 = (bf16[1024,640]{1,0:T(8,128)(2,1)}, bf16[1024,128]{1,0:T(8,128)(2,1)}, bf16[1024,128]{1,0:T(8,128)(2,1)}, bf16[2048,128]{1,0:T(8,128)(2,1)}, bf16[2...) custom-call(f32[4,2]{1,0:T(4,128)} %pad_maximum_fusion.10.scal_ref, bf16[1024,1024]{1,0:T(8,128)(2,1)} %fusion.9.a_ref, ...), custom_call_target="tpu_custom_call" | custom-call | flops 1644167168 | bytes 8000000 | tf_op jit(solution)/shard_map/project/pallas_call | solution.py:172
  134.0 4.5 select_blocks.3
  149.9 7.9 %project.7 = (bf16[1024,640]{1,0:T(8,128)(2,1)}, bf16[1024,128]{1,0:T(8,128)(2,1)}, bf16[1024,128]{1,0:T(8,128)(2,1)}, bf16[2048,128]{1,0:T(8,128)(2,1)}, bf16[2...) custom-call(f32[4,2]{1,0:T(4,128)} %pad_maximum_fusion.10.scal_ref, bf16[1024,1024]{1,0:T(8,128)(2,1)} %fusion.9.a_ref, ...), custom_call_target="tpu_custom_call" | custom-call | flops 1644167168 | bytes 8000000 | tf_op jit(solution)/shard_map/project/pallas_call | solution.py:172
  167.6 14.4 %recur.2 = (bf16[1024,512]{1,0:T(8,128)(2,1)}, f32[4,128,128]{2,1,0:T(8,128)}, bf16[512,128]{1,0:T(8,128)(2,1)}, bf16[512,128]{1,0:T(8,128)(2,1)}, bf16[512,128]...) custom-call(f32[1,128]{1,0:T(1,128)} %bitcast.109, ...), custom_call_target="tpu_custom_call" | custom-call | flops 2688000000 | bytes 1000000 | tf_op jit(solution)/shard_map/recur/pallas_call | solution.py:346
  189.4 14.4 %recur.3 = (bf16[1024,512]{1,0:T(8,128)(2,1)}, f32[4,128,128]{2,1,0:T(8,128)}, bf16[512,128]{1,0:T(8,128)(2,1)}, bf16[512,128]{1,0:T(8,128)(2,1)}, bf16[512,128]...) custom-call(f32[1,128]{1,0:T(1,128)} %bitcast.110, ...), custom_call_target="tpu_custom_call", output_to_operand_aliasing={{0}: (22, {})} | custom-call | flops 2688000000 | bytes 1000000 | tf_op jit(solution)/shard_map/recur/pallas_call | solution.py:346
  203.9 5.3 mix_out.1
  226.5 22.0 %ffn.2 = (f32[1024,1024]{1,0:T(8,128)}, f32[1024,1024]{1,0:T(8,128)}, bf16[2,1056,256]{2,1,0:T(8,128)(2,1)}, bf16[2,1056,256]{2,1,0:T(8,128)(2,1)}, bf16[2,1056,...) custom-call(bf16[1024,1024]{1,0:T(8,128)(2,1)} %multiply_convert_fusion.1.b_ref, ...), custom_call_target="tpu_custom_call" | custom-call | flops 13287555072 | bytes 1000000 | tf_op jit(solution)/shard_map/ffn/pallas_call | solution.py:928
  251.2 23.2 %ffn.3 = (bf16[1024,1024]{1,0:T(8,128)(2,1)}, bf16[1024,1024]{1,0:T(8,128)(2,1)}, bf16[2,1056,256]{2,1,0:T(8,128)(2,1)}, bf16[2,1056,256]{2,1,0:T(8,128)(2,1)}, ...) custom-call(bf16[1024,1024]{1,0:T(8,128)(2,1)} %multiply_convert_fusion.1.b_ref, ...), custom_call_target="tpu_custom_call" | custom-call | flops 13287555072 | bytes 1000000 | tf_op jit(solution)/shard_map/ffn/pallas_call | solution.py:928
  276.2 4.4 add_stacks.5
  283.7 10.3 %mix_back.1 = (bf16[1024,1024]{1,0:T(8,128)(2,1)}, bf16[1024,512]{1,0:T(8,128)(2,1)}, f32[1,1024]{1,0:T(1,128)}, bf16[128,256]{1,0:T(8,128)(2,1)}, bf16[128,256]...) custom-call(f32[1,1024]{1,0:T(1,128)} %bitcast.97, ...), custom_call_target="tpu_custom_call" | custom-call | flops 2147483648 | bytes 1000000 | tf_op jit(solution)/shard_map/mix_back/pallas_call | solution.py:797
  297.3 20.8 %recur_back.2 = (bf16[1024,768]{1,0:T(8,128)(2,1)}, bf16[1024,768]{1,0:T(8,128)(2,1)}, bf16[1024,768]{1,0:T(8,128)(2,1)}, bf16[1024,768]{1,0:T(8,128)(2,1)}, f32...) custom-call(f32[1,128]{1,0:T(1,128)} %bitcast.111, ...), custom_call_target="tpu_custom_call" | custom-call | flops 4032000000 | bytes 1000000 | tf_op jit(solution)/shard_map/recur_back/pallas_call | solution.py:505
  318.0 3.8 collective-permute-done.46.refs_3_
  326.9 5.1 all-to-all-start.2
  332.0 4.3 add_stacks.6
  338.0 20.8 %recur_back.3 = (bf16[1024,768]{1,0:T(8,128)(2,1)}, bf16[1024,768]{1,0:T(8,128)(2,1)}, bf16[1024,768]{1,0:T(8,128)(2,1)}, bf16[1024,768]{1,0:T(8,128)(2,1)}, f32...) custom-call(f32[1,128]{1,0:T(1,128)} %bitcast.112, ...), custom_call_target="tpu_custom_call", output_to_operand_aliasing={{0}: (33, {}), {1}: (34, {}), {2}: (35, {}), {3}: (36, {}),... | custom-call | flops 4032000000 | bytes 1000000 | tf_op jit(solution)/shard_map/recur_back/pallas_call | solution.py:505
  367.9 13.9 %project_back.4 = (bf16[1024,784]{1,0:T(8,128)(2,1)}, f32[8,640]{1,0:T(8,128)}, f32[8,128]{1,0:T(8,128)}, bf16[2,912,256]{2,1,0:T(8,128)(2,1)}, bf16[2,912,256]{2,1,0:T(8,128)(2,1)}) custom-call(f32[4,2]{1,0:T(4,128)} %pad_maximum_fusion.10.scal_ref, bf16[1024,1024]{1,0:T(8,128)(2,1)} %fusion.9.a_ref, f32[4,8,640]{2,1,0:T(8,128)} %select_reduce_fusion.cw_ref, ...), custom_call_target="tpu_custom_call" | custom-call | flops 1644167168 | bytes 1000000 | tf_op jit(solution)/shard_map/project_back/pallas_call | solution.py:639
  383.0 13.7 %project_back.5 = (bf16[1024,784]{1,0:T(8,128)(2,1)}, f32[8,640]{1,0:T(8,128)}, f32[8,128]{1,0:T(8,128)}, bf16[2,912,256]{2,1,0:T(8,128)(2,1)}, bf16[2,912,256]{2,1,0:T(8,128)(2,1)}) custom-call(f32[4,2]{1,0:T(4,128)} %pad_maximum_fusion.10.scal_ref, bf16[1024,1024]{1,0:T(8,128)(2,1)} %fusion.9.a_ref, f32[4,8,640]{2,1,0:T(8,128)} %select_reduce_fusion.cw_ref, ...), custom_call_target="tpu_custom_call" | custom-call | flops 1644167168 | bytes 1000000 | tf_op jit(solution)/shard_map/project_back/pallas_call | solution.py:639
  405.6 14.1 %project_back.6 = (bf16[1024,784]{1,0:T(8,128)(2,1)}, f32[8,640]{1,0:T(8,128)}, f32[8,128]{1,0:T(8,128)}, bf16[2,912,256]{2,1,0:T(8,128)(2,1)}, bf16[2,912,256]{2,1,0:T(8,128)(2,1)}) custom-call(f32[4,2]{1,0:T(4,128)} %pad_maximum_fusion.10.scal_ref, bf16[1024,1024]{1,0:T(8,128)(2,1)} %fusion.9.a_ref, f32[4,8,640]{2,1,0:T(8,128)} %select_reduce_fusion.cw_ref, ...), custom_call_target="tpu_custom_call" | custom-call | flops 1644167168 | bytes 1000000 | tf_op jit(solution)/shard_map/project_back/pallas_call | solution.py:639
  420.6 4.0 add_stacks.7
  428.4 13.7 %project_back.7 = (bf16[1024,784]{1,0:T(8,128)(2,1)}, f32[8,640]{1,0:T(8,128)}, f32[8,128]{1,0:T(8,128)}, bf16[2,912,256]{2,1,0:T(8,128)(2,1)}, bf16[2,912,256]{2,1,0:T(8,128)(2,1)}) custom-call(f32[4,2]{1,0:T(4,128)} %pad_maximum_fusion.10.scal_ref, bf16[1024,1024]{1,0:T(8,128)(2,1)} %fusion.9.a_ref, f32[4,8,640]{2,1,0:T(8,128)} %select_reduce_fusion.cw_ref, ...), custom_call_target="tpu_custom_call" | custom-call | flops 1644167168 | bytes 1000000 | tf_op jit(solution)/shard_map/project_back/pallas_call | solution.py:639
  445.6 13.1 %input_back.1 = (bf16[1024,1024]{1,0:T(8,128)(2,1)}, f32[1,1024]{1,0:T(1,128)}) custom-call(bf16[1024,784]{1,0:T(8,128)(2,1)} %get-tuple-element.998.refs_0_, bf16[1024,784]{1,0:T(8,128)(2,1)} %get-tuple-element.999.refs_1_, bf16[1024,784]{1,0:T(8,128)(2,1)} %get-tuple-element.1000.refs_2_, bf16[1024,784]{1,0:T(8,128)(2,1)} %get-tuple-element.1001.refs_3_, ...), custom_call_target="tpu_custom_call" | custom-call | flops 6576668672 | bytes 1000000 | tf_op jit(solution)/shard_map/input_back/pallas_call | solution.py:705
  497.4 4.7 collective-permute-done.72
  506.5 4.7 collective-permute-done.73
  515.9 6.4 %all-to-all-done.3 = bf16[4,256,512]{2,1,0:T(8,128)(2,1)S(1)} async-done(((bf16[4,256,512]{2,1,0:T(8,128)(2,1)}), bf16[4,256,512]{2,1,0:T(8,128)(2,1)S(1)}, u32[]{:S(2)}, u32[]{:S(2)}) %all-to-all-start.3) | async-done | bytes 1048608 | tf_op jit(solution)/shard_map/all_to_all | solution.py:1471
  (438 shorter events, 195.8 us)
Async XLA Ops:
  8.8 33.4 %all-to-all-start = ((bf16[4,256,512]{2,1,0:T(8,128)(2,1)}), bf16[4,256,512]{2,1,0:T(8,128)(2,1)S(1)}, u32[]{:S(2)}, u32[]{:S(2)}) async-start(bf16[4,256,512]{2,1,0:T(8,128)(2,1)} %pad_maximum_fusion.1), calls=%async_computation | async-start | bytes 2097152 | tf_op jit(solution)/shard_map/all_to_all | solution.py:993
  19.6 22.6 %collective-permute-start.3 = (bf16[912,256]{1,0:T(8,128)(2,1)}, bf16[912,256]{1,0:T(8,128)(2,1)S(1)}, u32[]{:S(2)}, u32[]{:S(2)}) collective-permute-start(bf16[912,256]{1,0:T(8,128)(2,1)} %pad_maximum_fusion.6.refs_0_.refs_4_), channel_id=1, source_target_pairs={{0,16},{4,20},{8,24},{12,28},{16,0},{20,4},{24,8},{28,12},{1,17},{... | collective-permute-start | bytes 1400840 | tf_op jit(solution)/shard_map/ppermute | solution.py:966
  21.1 21.0 %collective-permute-start.4 = (bf16[912,256]{1,0:T(8,128)(2,1)}, bf16[912,256]{1,0:T(8,128)(2,1)S(1)}, u32[]{:S(2)}, u32[]{:S(2)}) collective-permute-start(bf16[912,256]{1,0:T(8,128)(2,1)} %pad_maximum_fusion.6.refs_0_.refs_4_), channel_id=1, source_target_pairs={{0,24},{4,28},{8,16},{12,20},{16,8},{20,12},{24,0},{28,4},{1,25},{... | collective-permute-start | bytes 1400840 | tf_op jit(solution)/shard_map/ppermute | solution.py:966
  84.6 24.9 %collective-permute-start.19 = (bf16[1056,256]{1,0:T(8,128)(2,1)S(1)}, bf16[1056,256]{1,0:T(8,128)(2,1)S(1)}, u32[]{:S(2)}, u32[]{:S(2)}) collective-permute-start(bf16[1056,256]{1,0:T(8,128)(2,1)S(1)} %bitcast.91), channel_id=1, source_target_pairs={{0,1},{1,2},{2,3},{3,0},{4,5},{5,6},{6,7},{7,4},{8,9},{9,10},{10,1... | collective-permute-start | bytes 1622024 | tf_op jit(solution)/shard_map/ppermute | solution.py:969
  85.3 24.2 %collective-permute-start.17 = (bf16[912,256]{1,0:T(8,128)(2,1)}, bf16[912,256]{1,0:T(8,128)(2,1)S(1)}, u32[]{:S(2)}, u32[]{:S(2)}) collective-permute-start(bf16[912,256]{1,0:T(8,128)(2,1)} %collective-permute-done.7.refs_0_.refs_4_.refs_8_), channel_id=1, source_target_pairs={{0,1},{1,2},{2,3},{3,0},{4,5},{5,6},{6,7},{7,4},{8,9},{9,10},{10,1... | collective-permute-start | bytes 1400840 | tf_op jit(solution)/shard_map/ppermute | solution.py:969
  86.7 22.7 %collective-permute-start.16 = (bf16[912,256]{1,0:T(8,128)(2,1)S(1)}, bf16[912,256]{1,0:T(8,128)(2,1)S(1)}, u32[]{:S(2)}, u32[]{:S(2)}) collective-permute-start(bf16[912,256]{1,0:T(8,128)(2,1)S(1)} %collective-permute-done.12.refs_2_.refs_6_.refs_10_), channel_id=1, source_target_pairs={{0,8},{4,12},{8,0},{12,4},{16,24},{20,28},{24,16},{28,20},{1,9},{5... | collective-permute-start | bytes 1400840 | tf_op jit(solution)/shard_map/ppermute | solution.py:966
  87.7 21.7 %collective-permute-start.18 = (bf16[912,256]{1,0:T(8,128)(2,1)S(1)}, bf16[912,256]{1,0:T(8,128)(2,1)S(1)}, u32[]{:S(2)}, u32[]{:S(2)}) collective-permute-start(bf16[912,256]{1,0:T(8,128)(2,1)S(1)} %collective-permute-done.14.refs_1_.refs_13_.refs_17_), channel_id=1, source_target_pairs={{0,16},{4,20},{8,24},{12,28},{16,0},{20,4},{24,8},{28,12},{1,17},{... | collective-permute-start | bytes 1400840 | tf_op jit(solution)/shard_map/ppermute | solution.py:966
  109.5 22.5 %collective-permute-start.22 = (bf16[1056,256]{1,0:T(8,128)(2,1)S(1)}, bf16[1056,256]{1,0:T(8,128)(2,1)}, u32[]{:S(2)}, u32[]{:S(2)}) collective-permute-start(bf16[1056,256]{1,0:T(8,128)(2,1)S(1)} %bitcast.92), channel_id=1, source_target_pairs={{0,3},{1,0},{2,1},{3,2},{4,7},{5,4},{6,5},{7,6},{8,11},{9,8},{10,9... | collective-permute-start | bytes 1622024 | tf_op jit(solution)/shard_map/ppermute | solution.py:969
  110.1 21.9 %collective-permute-start.23 = (bf16[4,256,256]{2,1,0:T(8,128)(2,1)}, bf16[4,256,256]{2,1,0:T(8,128)(2,1)}, u32[]{:S(2)}, u32[]{:S(2)}) collective-permute-start(bf16[4,256,256]{2,1,0:T(8,128)(2,1)} %get-tuple-element.622), channel_id=1, source_target_pairs={{0,16},{4,20},{8,24},{12,28},{16,0},{20,4},{24,8},{28,12},{1,17},{... | collective-permute-start | bytes 1572872 | tf_op jit(solution)/shard_map/ppermute | solution.py:966
  110.7 21.3 %collective-permute-start.24 = (bf16[4,256,256]{2,1,0:T(8,128)(2,1)}, bf16[4,256,256]{2,1,0:T(8,128)(2,1)}, u32[]{:S(2)}, u32[]{:S(2)}) collective-permute-start(bf16[4,256,256]{2,1,0:T(8,128)(2,1)} %get-tuple-element.623), channel_id=1, source_target_pairs={{0,8},{4,12},{8,0},{12,4},{16,24},{20,28},{24,16},{28,20},{1,9},{5... | collective-permute-start | bytes 1572872 | tf_op jit(solution)/shard_map/ppermute | solution.py:966
  111.6 20.4 %collective-permute-start.20 = (bf16[912,256]{1,0:T(8,128)(2,1)S(1)}, bf16[912,256]{1,0:T(8,128)(2,1)S(1)}, u32[]{:S(2)}, u32[]{:S(2)}) collective-permute-start(bf16[912,256]{1,0:T(8,128)(2,1)S(1)} %collective-permute-done.17.refs_0_.refs_8_.refs_12_), channel_id=1, source_target_pairs={{0,8},{4,12},{8,0},{12,4},{16,24},{20,28},{24,16},{28,20},{1,9},{5... | collective-permute-start | bytes 1400840 | tf_op jit(solution)/shard_map/ppermute | solution.py:966
  143.4 42.2 %all-to-all-start.1 = ((bf16[4,256,512]{2,1,0:T(8,128)(2,1)}), bf16[4,256,512]{2,1,0:T(8,128)(2,1)S(1)}, u32[]{:S(2)}, u32[]{:S(2)}) async-start(bf16[4,256,512]{2,1,0:T(8,128)(2,1)} %select_blocks.3), calls=%async_computation.1 | async-start | bytes 2097152 | tf_op jit(solution)/shard_map/all_to_all | solution.py:993
  225.0 23.5 %collective-permute-start.39 = (bf16[1056,256]{1,0:T(8,128)(2,1)S(1)}, bf16[1056,256]{1,0:T(8,128)(2,1)S(1)}, u32[]{:S(2)}, u32[]{:S(2)}) collective-permute-start(bf16[1056,256]{1,0:T(8,128)(2,1)S(1)} %collective-permute-done.38.refs_6_), channel_id=1, source_target_pairs={{0,8},{4,12},{8,0},{12,4},{16,24},{20,28},{24,16},{28,20},{1,9},{5... | collective-permute-start | bytes 1622024 | tf_op jit(solution)/shard_map/ppermute | solution.py:966
  226.1 22.4 %collective-permute-start.40 = (bf16[1056,256]{1,0:T(8,128)(2,1)S(1)}, bf16[1056,256]{1,0:T(8,128)(2,1)S(1)}, u32[]{:S(2)}, u32[]{:S(2)}) collective-permute-start(bf16[1056,256]{1,0:T(8,128)(2,1)S(1)} %copy-done.70), channel_id=1, source_target_pairs={{0,16},{4,20},{8,24},{12,28},{16,0},{20,4},{24,8},{28,12},{1,17},{... | collective-permute-start | bytes 1622024 | tf_op jit(solution)/shard_map/ppermute | solution.py:966
  248.5 25.8 %collective-permute-start.41 = (bf16[2,1056,256]{2,1,0:T(8,128)(2,1)}, bf16[2,1056,256]{2,1,0:T(8,128)(2,1)S(1)}, u32[]{:S(2)}, u32[]{:S(2)}) collective-permute-start(bf16[2,1056,256]{2,1,0:T(8,128)(2,1)} %get-tuple-element.812), channel_id=1, source_target_pairs={{0,16},{4,20},{8,24},{12,28},{16,0},{20,4},{24,8},{28,12},{1,17},{... | collective-permute-start | bytes 3244040 | tf_op jit(solution)/shard_map/ppermute | solution.py:966
  250.2 24.9 %collective-permute-start.42 = (bf16[2,1056,256]{2,1,0:T(8,128)(2,1)}, bf16[2,1056,256]{2,1,0:T(8,128)(2,1)S(1)}, u32[]{:S(2)}, u32[]{:S(2)}) collective-permute-start(bf16[2,1056,256]{2,1,0:T(8,128)(2,1)} %get-tuple-element.813), channel_id=1, source_target_pairs={{0,8},{4,12},{8,0},{12,4},{16,24},{20,28},{24,16},{28,20},{1,9},{5... | collective-permute-start | bytes 3244040 | tf_op jit(solution)/shard_map/ppermute | solution.py:966
  295.4 27.2 %collective-permute-start.48 = (bf16[1024,1024]{1,0:T(8,128)(2,1)S(1)}, bf16[1024,1024]{1,0:T(8,128)(2,1)}, u32[]{:S(2)}, u32[]{:S(2)}) collective-permute-start(bf16[1024,1024]{1,0:T(8,128)(2,1)S(1)} %copy-done.8), channel_id=1, source_target_pairs={{0,4},{4,0},{8,12},{12,8},{16,20},{20,16},{24,28},{28,24},{1,5},{5... | collective-permute-start | bytes 6291464 | tf_op jit(solution)/shard_map/ppermute | solution.py:963
  295.4 26.5 %collective-permute-start.46 = (bf16[2,1056,256]{2,1,0:T(8,128)(2,1)}, bf16[2,1056,256]{2,1,0:T(8,128)(2,1)S(1)}, u32[]{:S(2)}, u32[]{:S(2)}) collective-permute-start(bf16[2,1056,256]{2,1,0:T(8,128)(2,1)} %get-tuple-element.865), channel_id=1, source_target_pairs={{0,8},{4,12},{8,0},{12,4},{16,24},{20,28},{24,16},{28,20},{1,9},{5... | collective-permute-start | bytes 3244040 | tf_op jit(solution)/shard_map/ppermute | solution.py:966
  296.3 26.3 %collective-permute-start.47 = (bf16[2,1056,256]{2,1,0:T(8,128)(2,1)}, bf16[2,1056,256]{2,1,0:T(8,128)(2,1)}, u32[]{:S(2)}, u32[]{:S(2)}) collective-permute-start(bf16[2,1056,256]{2,1,0:T(8,128)(2,1)} %get-tuple-element.866), channel_id=1, source_target_pairs={{0,16},{4,20},{8,24},{12,28},{16,0},{20,4},{24,8},{28,12},{1,17},{... | collective-permute-start | bytes 3244040 | tf_op jit(solution)/shard_map/ppermute | solution.py:966
  326.9 32.9 %all-to-all-start.2 = ((bf16[4,256,512]{2,1,0:T(8,128)(2,1)}), bf16[4,256,512]{2,1,0:T(8,128)(2,1)S(1)}, u32[]{:S(2)}, u32[]{:S(2)}) async-start(bf16[4,256,512]{2,1,0:T(8,128)(2,1)} %bitcast.23), calls=%async_computation.2 | async-start | bytes 2097152 | tf_op jit(solution)/shard_map/all_to_all | solution.py:1394
  336.4 22.6 %collective-permute-start.49 = (bf16[1056,256]{1,0:T(8,128)(2,1)}, bf16[1056,256]{1,0:T(8,128)(2,1)S(1)}, u32[]{:S(2)}, u32[]{:S(2)}) collective-permute-start(bf16[1056,256]{1,0:T(8,128)(2,1)} %get-tuple-element.906), channel_id=1, source_target_pairs={{0,16},{4,20},{8,24},{12,28},{16,0},{20,4},{24,8},{28,12},{1,17},{... | collective-permute-start | bytes 1622024 | tf_op jit(solution)/shard_map/ppermute | solution.py:966
  337.3 22.5 %collective-permute-start.50 = (bf16[1056,256]{1,0:T(8,128)(2,1)}, bf16[1056,256]{1,0:T(8,128)(2,1)}, u32[]{:S(2)}, u32[]{:S(2)}) collective-permute-start(bf16[1056,256]{1,0:T(8,128)(2,1)} %get-tuple-element.908), channel_id=1, source_target_pairs={{0,8},{4,12},{8,0},{12,4},{16,24},{20,28},{24,16},{28,20},{1,9},{5... | collective-permute-start | bytes 1622024 | tf_op jit(solution)/shard_map/ppermute | solution.py:966
  361.9 34.7 %collective-permute-start.53 = (bf16[1056,256]{1,0:T(8,128)(2,1)}, bf16[1056,256]{1,0:T(8,128)(2,1)}, u32[]{:S(2)}, u32[]{:S(2)}) collective-permute-start(bf16[1056,256]{1,0:T(8,128)(2,1)} %add_convert_fusion.2), channel_id=1, source_target_pairs={{0,1},{1,2},{2,3},{3,0},{4,5},{5,6},{6,7},{7,4},{8,9},{9,10},{10,1... | collective-permute-start | bytes 1622024 | tf_op jit(solution)/shard_map/ppermute | solution.py:969
  366.1 30.6 %collective-permute-start.52 = (bf16[1056,256]{1,0:T(8,128)(2,1)}, bf16[1056,256]{1,0:T(8,128)(2,1)}, u32[]{:S(2)}, u32[]{:S(2)}) collective-permute-start(bf16[1056,256]{1,0:T(8,128)(2,1)} %add_convert_fusion.3), channel_id=1, source_target_pairs={{0,3},{1,0},{2,1},{3,2},{4,7},{5,4},{6,5},{7,6},{8,11},{9,8},{10,9... | collective-permute-start | bytes 1622024 | tf_op jit(solution)/shard_map/ppermute | solution.py:969
  381.9 37.7 %collective-permute-start.55 = (bf16[2,912,256]{2,1,0:T(8,128)(2,1)}, bf16[2,912,256]{2,1,0:T(8,128)(2,1)S(1)}, u32[]{:S(2)}, u32[]{:S(2)}) collective-permute-start(bf16[2,912,256]{2,1,0:T(8,128)(2,1)} %get-tuple-element.963), channel_id=1, source_target_pairs={{0,16},{4,20},{8,24},{12,28},{16,0},{20,4},{24,8},{28,12},{1,17},{... | collective-permute-start | bytes 2801672 | tf_op jit(solution)/shard_map/ppermute | solution.py:966
  396.7 22.9 %collective-permute-start.54 = (bf16[2,912,256]{2,1,0:T(8,128)(2,1)}, bf16[2,912,256]{2,1,0:T(8,128)(2,1)}, u32[]{:S(2)}, u32[]{:S(2)}) collective-permute-start(bf16[2,912,256]{2,1,0:T(8,128)(2,1)} %get-tuple-element.962), channel_id=1, source_target_pairs={{0,8},{4,12},{8,0},{12,4},{16,24},{20,28},{24,16},{28,20},{1,9},{5... | collective-permute-start | bytes 2801672 | tf_op jit(solution)/shard_map/ppermute | solution.py:966
  401.5 24.6 %collective-permute-start.51 = (bf16[2,256,512]{2,1,0:T(8,128)(2,1)S(1)}, bf16[2,256,512]{2,1,0:T(8,128)(2,1)S(1)}, u32[]{:S(2)}, u32[]{:S(2)}) collective-permute-start(bf16[2,256,512]{2,1,0:T(8,128)(2,1)S(1)} %constant_dynamic-slice_fusion.14), channel_id=1, source_target_pairs={{0,4},{4,0},{8,12},{12,8},{16,20},{20,16},{24,28},{28,24},{1,5},{5... | collective-permute-start | bytes 1572872 | tf_op jit(solution)/shard_map/ppermute | solution.py:963
  403.5 39.4 %collective-permute-start.58 = (bf16[1056,256]{1,0:T(8,128)(2,1)}, bf16[1056,256]{1,0:T(8,128)(2,1)}, u32[]{:S(2)}, u32[]{:S(2)}) collective-permute-start(bf16[1056,256]{1,0:T(8,128)(2,1)} %add_convert_fusion.1), channel_id=1, source_target_pairs={{0,3},{1,0},{2,1},{3,2},{4,7},{5,4},{6,5},{7,6},{8,11},{9,8},{10,9... | collective-permute-start | bytes 1622024 | tf_op jit(solution)/shard_map/ppermute | solution.py:969
  427.3 31.4 %collective-permute-start.59 = (bf16[2,912,256]{2,1,0:T(8,128)(2,1)}, bf16[2,912,256]{2,1,0:T(8,128)(2,1)S(1)}, u32[]{:S(2)}, u32[]{:S(2)}) collective-permute-start(bf16[2,912,256]{2,1,0:T(8,128)(2,1)} %get-tuple-element.1004), channel_id=1, source_target_pairs={{0,16},{4,20},{8,24},{12,28},{16,0},{20,4},{24,8},{28,12},{1,17},{... | collective-permute-start | bytes 2801672 | tf_op jit(solution)/shard_map/ppermute | solution.py:966
  462.4 23.0 %collective-permute-start.75 = (bf16[3,352,128]{2,1,0:T(8,128)(2,1)}, bf16[3,352,128]{2,1,0:T(8,128)(2,1)S(1)}, u32[]{:S(2)}, u32[]{:S(2)}) collective-permute-start(bf16[3,352,128]{2,1,0:T(8,128)(2,1)} %constant_dynamic-slice_fusion), channel_id=1, source_target_pairs={{0,4},{4,0},{8,12},{12,8},{16,20},{20,16},{24,28},{28,24},{1,5},{5... | collective-permute-start | bytes 811016 | tf_op jit(solution)/shard_map/ppermute | solution.py:963
  462.9 30.3 %collective-permute-start.63 = (bf16[2,912,256]{2,1,0:T(8,128)(2,1)}, bf16[2,912,256]{2,1,0:T(8,128)(2,1)}, u32[]{:S(2)}, u32[]{:S(2)}) collective-permute-start(bf16[2,912,256]{2,1,0:T(8,128)(2,1)} %get-tuple-element.1025), channel_id=1, source_target_pairs={{0,8},{4,12},{8,0},{12,4},{16,24},{20,28},{24,16},{28,20},{1,9},{5... | collective-permute-start | bytes 2801672 | tf_op jit(solution)/shard_map/ppermute | solution.py:966
  481.9 40.4 %all-to-all-start.3 = ((bf16[4,256,512]{2,1,0:T(8,128)(2,1)}), bf16[4,256,512]{2,1,0:T(8,128)(2,1)S(1)}, u32[]{:S(2)}, u32[]{:S(2)}) async-start(bf16[4,256,512]{2,1,0:T(8,128)(2,1)} %bitcast.24), calls=%async_computation.3 | async-start | bytes 2097152 | tf_op jit(solution)/shard_map/all_to_all | solution.py:1471
  (130 other events, 1831.4 us)
